TPU v7x, 32 devices: a whole 2x2x4 slice. The times are simulated.
32 devices in a mesh: shard: 4 (over z), ctx: 4 (over y, x), tp: 2 (over core).
Axes of the slice: x: 2, y: 2, z: 4, core: 2. Of those that a mesh axis runs over, the one named last changes fastest.
Arguments:
- tokens: bfloat16 [8192, 2048], P(('shard', 'ctx')), may hold values from -6 to 6
- cotangent: bfloat16 [8192, 2048], P(('shard', 'ctx')), may hold values from -6 to 6
- lengths: int32 [4, 3], P('shard'), may hold values from 1 to 320, 512 in all within a row
- norm_gain: float32 [2, 2, 2048], replicated, may hold values from 0.5 to 1.5
- norm_bias: float32 [2, 2, 2048], replicated, may hold values from -1.75 to 1.75
- input_bias: float32 [2, 3, 2048], P(None, None, 'tp'), may hold values from -1.75 to 1.75
- input_projection: bfloat16 [2, 2048, 3, 2048], P(None, ('shard', 'ctx'), None, 'tp'), may hold values from -0.125 to 0.125
- output_projection: bfloat16 [2, 2048, 2048], P(None, ('shard', 'ctx'), 'tp'), may hold values from -0.5 to 0.5
- gate_up_weight: bfloat16 [2, 2048, 2, 5632], P(None, ('shard', 'ctx'), None, 'tp'), may hold values from -0.125 to 0.125
- down_weight: bfloat16 [2, 2048, 5632], P(None, ('shard', 'ctx'), 'tp'), may hold values from -0.078125 to 0.078125
Outputs:
- result: bfloat16 [8192, 2048], P(('shard', 'ctx'))
- tokens_grad: float32 [8192, 2048], P(('shard', 'ctx'))
- norm_gain_grad: float32 [2, 2, 2048], replicated
- norm_bias_grad: float32 [2, 2, 2048], replicated
- input_bias_grad: float32 [2, 3, 2048], P(None, None, 'tp')
- input_projection_grad: float32 [2, 2048, 3, 2048], P(None, ('shard', 'ctx'), None, 'tp')
- output_projection_grad: float32 [2, 2048, 2048], P(None, ('shard', 'ctx'), 'tp')
- gate_up_grad: float32 [2, 2048, 2, 5632], P(None, ('shard', 'ctx'), None, 'tp')
- down_grad: float32 [2, 2048, 5632], P(None, ('shard', 'ctx'), 'tp')
Inputs may be any that keep to these rules, and one draw needn't show every extreme that they name: `lengths`: row s gives, for the 3 sequences of shard index s, the tokens of each on one device of ctx: a sequence has 4 times as many tokens, cut into equal consecutive pieces in ctx order, and every device stores its pieces in the order of the sequences. Each row sums to 512; the largest entry of each row is exactly 320.
All inputs are finite; a program needn't handle non-finite values.
Results may differ from a plain program's by a relative error of at most 0.019.
Values may be sent and summed in bfloat16 or wider, within the bound.
No kernel may reach another device: no remote copies, remote signals or barrier semaphores. Data moves between devices by JAX's collectives and lax.ppermute only.
A program may use at most 448 MiB of HBM per device.

v0:
```python
import math

import jax
import jax.numpy as jnp
from jax import lax
from jax.sharding import PartitionSpec as P

HEAD = 64
ROT = 16


norm_eps = 1e-05
rotary_base = 10000.0
masked_score = -1e30


def row_meta(seq_lengths, row_count):
    seq_ends = jnp.cumsum(seq_lengths, dtype=jnp.int32)
    row_index = jnp.arange(row_count, dtype=jnp.int32)
    seq_ids = jnp.sum(
        (row_index[:, None] >= seq_ends[None, :]).astype(jnp.int32), axis=1, dtype=jnp.int32
    )
    one_hot = (
        seq_ids[:, None] == jnp.arange(seq_lengths.shape[0], dtype=jnp.int32)[None, :]
    ).astype(jnp.int32)
    seq_start = jnp.sum(one_hot * (seq_ends - seq_lengths)[None, :], axis=1, dtype=jnp.int32)
    length = jnp.sum(one_hot * seq_lengths[None, :], axis=1, dtype=jnp.int32)
    return (seq_ids, length, row_index - seq_start)


def rotary_tables(positions):
    half_rot = ROT // 2
    frequency = rotary_base ** (-(2.0 * jnp.arange(half_rot, dtype=jnp.float32)) / ROT)
    angles = positions.astype(jnp.float32)[:, None] * frequency[None, :]
    return (jnp.cos(angles), jnp.sin(angles))


def rotate(vectors, cosine, sine):
    half_rot = cosine.shape[-1]
    lead_half = vectors[..., :half_rot]
    trail_half = vectors[..., half_rot : 2 * half_rot]
    cos_wide = cosine[:, None, :]
    sin_wide = sine[:, None, :]
    return jnp.concatenate(
        [
            lead_half * cos_wide - trail_half * sin_wide,
            trail_half * cos_wide + lead_half * sin_wide,
            vectors[..., 2 * half_rot :],
        ],
        axis=-1,
    )


def norm_parts(stream, gain_row, bias_row):
    row_mean = jnp.mean(stream, axis=-1, keepdims=True)
    centered = stream - row_mean
    variance = jnp.mean(centered * centered, axis=-1, keepdims=True)
    inverse = lax.rsqrt(variance + norm_eps)
    scaled = centered * inverse
    return (scaled, inverse, scaled * gain_row + bias_row)


def norm_back(grad_normed, scaled, inverse, gain_row):
    grad_scaled = grad_normed * gain_row
    inner = (
        grad_scaled
        - jnp.mean(grad_scaled, axis=-1, keepdims=True)
        - scaled * jnp.mean(grad_scaled * scaled, axis=-1, keepdims=True)
    )
    return (inverse * inner, jnp.sum(grad_normed * scaled, axis=0), jnp.sum(grad_normed, axis=0))


def split_blocks(keys_all, values_all, key_seq, key_pos):
    key_count, head_count, head_size = keys_all.shape
    block_rows = math.gcd(key_count, 512)
    block_count = key_count // block_rows
    return (
        keys_all.reshape(block_count, block_rows, head_count, head_size),
        values_all.reshape(block_count, block_rows, head_count, head_size),
        key_seq.reshape(block_count, block_rows),
        key_pos.reshape(block_count, block_rows),
    )


def masked_scores(queries, key_block, query_seq, query_pos, block_seq, block_pos, score_scale):
    scores = (
        jnp.einsum("rhe,khe->hrk", queries, key_block, preferred_element_type=jnp.float32)
        * score_scale
    )
    allowed = (query_seq[:, None] == block_seq[None, :]) & (
        block_pos[None, :] <= query_pos[:, None]
    )
    return jnp.where(allowed[None], scores, masked_score)


def attend(queries, keys_all, values_all, query_seq, query_pos, key_seq, key_pos, score_scale):
    row_count, head_count, head_size = queries.shape
    blocks = split_blocks(keys_all, values_all, key_seq, key_pos)

    def running(state_pair, block):
        running_max, running_sum = state_pair
        scores = masked_scores(
            queries, block[0], query_seq, query_pos, block[2], block[3], score_scale
        )
        new_max = jnp.maximum(running_max, jnp.max(scores, axis=-1))
        running_sum = running_sum * jnp.exp(running_max - new_max) + jnp.sum(
            jnp.exp(scores - new_max[..., None]), axis=-1
        )
        return ((new_max, running_sum), None)

    start_max = jnp.full((head_count, row_count), masked_score, jnp.float32)
    (final_max, final_sum), unused = lax.scan(
        running, (start_max, jnp.zeros_like(start_max)), blocks
    )
    log_total = final_max + jnp.log(final_sum)

    def weigh(state_pair, block):
        coarse, fine = state_pair
        scores = masked_scores(
            queries, block[0], query_seq, query_pos, block[2], block[3], score_scale
        )
        probs = jnp.exp(scores - log_total[..., None])
        probs_low = probs.astype(jnp.bfloat16)
        remainder = (probs - probs_low.astype(jnp.float32)).astype(jnp.bfloat16)
        coarse = coarse + jnp.einsum(
            "hrk,khe->rhe", probs_low, block[1], preferred_element_type=jnp.float32
        )
        fine = fine + jnp.einsum(
            "hrk,khe->rhe", remainder, block[1], preferred_element_type=jnp.float32
        )
        return ((coarse, fine), None)

    zeros_out = jnp.zeros((row_count, head_count, head_size), jnp.float32)
    (coarse, fine), unused = lax.scan(weigh, (zeros_out, zeros_out), blocks)
    return (coarse, coarse + fine, log_total)


def attend_back(
    queries,
    keys_all,
    values_all,
    grad_out,
    row_dots,
    log_total,
    query_seq,
    query_pos,
    key_seq,
    key_pos,
    score_scale,
):
    row_count, head_count, head_size = queries.shape
    key_count = keys_all.shape[0]
    blocks = split_blocks(keys_all, values_all, key_seq, key_pos)

    def step(grad_query, block):
        scores = masked_scores(
            queries, block[0], query_seq, query_pos, block[2], block[3], score_scale
        )
        probs = jnp.exp(scores - log_total[..., None])
        grad_probs = jnp.einsum(
            "rhe,khe->hrk", grad_out, block[1], preferred_element_type=jnp.float32
        )
        grad_scores = (probs * (grad_probs - row_dots[..., None])).astype(jnp.bfloat16)
        grad_query = grad_query + jnp.einsum(
            "hrk,khe->rhe", grad_scores, block[0], preferred_element_type=jnp.float32
        )
        grad_key = (
            jnp.einsum("hrk,rhe->khe", grad_scores, queries, preferred_element_type=jnp.float32)
            * score_scale
        )
        grad_value = jnp.einsum(
            "hrk,rhe->khe", probs.astype(jnp.bfloat16), grad_out, preferred_element_type=jnp.float32
        )
        return (grad_query, (grad_key, grad_value))

    zeros_out = jnp.zeros((row_count, head_count, head_size), jnp.float32)
    grad_query, (grad_keys, grad_values) = lax.scan(step, zeros_out, blocks)
    return (
        grad_query * score_scale,
        grad_keys.reshape(key_count, head_count, head_size),
        grad_values.reshape(key_count, head_count, head_size),
    )


def body(
    tokens,
    cotangent,
    lengths,
    norm_gain,
    norm_bias,
    input_bias,
    input_projection,
    output_projection,
    gate_up_weight,
    down_weight,
):
    row_count = tokens.shape[0]
    layer_total = input_projection.shape[0]
    local_width = input_bias.shape[2]
    head_size = HEAD
    head_count = local_width // head_size
    score_scale = float(head_size) ** (-0.5)
    ctx_spread = lax.axis_size("ctx")
    ctx_place = lax.axis_index("ctx")
    seq_ids, length, offset = row_meta(lengths[0], row_count)
    query_pos = ctx_place * length + offset
    key_seq = jnp.tile(seq_ids, ctx_spread)
    key_pos = (
        jnp.arange(ctx_spread, dtype=jnp.int32)[:, None] * length[None, :] + offset[None, :]
    ).reshape(-1)
    cosine, sine = rotary_tables(query_pos)
    stream = tokens.astype(jnp.float32)
    saved = []
    for layer_index in range(layer_total):
        weights = (
            lax.all_gather(input_projection[layer_index], ("shard", "ctx"), axis=0, tiled=True),
            lax.all_gather(output_projection[layer_index], ("shard", "ctx"), axis=0, tiled=True),
            lax.all_gather(gate_up_weight[layer_index], ("shard", "ctx"), axis=0, tiled=True),
            lax.all_gather(down_weight[layer_index], ("shard", "ctx"), axis=0, tiled=True),
        )
        qkv_full, out_full, gate_up_full, down_full = weights
        scaled_one, inverse_one, normed_one = norm_parts(
            stream, norm_gain[layer_index, 0], norm_bias[layer_index, 0]
        )
        normed_low = normed_one.astype(jnp.bfloat16)
        joined = (
            jnp.einsum("td,dch->tch", normed_low, qkv_full, preferred_element_type=jnp.float32)
            + input_bias[layer_index]
        )
        split_qkv = joined.reshape(row_count, 3, head_count, head_size)
        queries = rotate(split_qkv[:, 0], cosine, sine).astype(jnp.bfloat16)
        keys_local = rotate(split_qkv[:, 1], cosine, sine).astype(jnp.bfloat16)
        values_local = split_qkv[:, 2].astype(jnp.bfloat16)
        keys_all, values_all = (
            lax.all_gather(keys_local, "ctx", axis=0, tiled=True),
            lax.all_gather(values_local, "ctx", axis=0, tiled=True),
        )
        coarse, refined, log_total = attend(
            queries, keys_all, values_all, seq_ids, query_pos, key_seq, key_pos, score_scale
        )
        heads_low = coarse.reshape(row_count, local_width).astype(jnp.bfloat16)
        attention = lax.psum(
            jnp.einsum("th,dh->td", heads_low, out_full, preferred_element_type=jnp.float32), "tp"
        )
        middle = stream + attention
        scaled_two, inverse_two, normed_two = norm_parts(
            middle, norm_gain[layer_index, 1], norm_bias[layer_index, 1]
        )
        normed_mid = normed_two.astype(jnp.bfloat16)
        gate_up = jnp.einsum(
            "td,dcf->tcf", normed_mid, gate_up_full, preferred_element_type=jnp.float32
        )
        hidden = (jax.nn.silu(gate_up[:, 0]) * gate_up[:, 1]).astype(jnp.bfloat16)
        feed = lax.psum(
            jnp.einsum("tf,df->td", hidden, down_full, preferred_element_type=jnp.float32).astype(
                jnp.bfloat16
            ),
            "tp",
        ).astype(jnp.float32)
        stream = middle + feed
        kept_weights = None
        saved.append(
            (
                kept_weights,
                scaled_one,
                inverse_one,
                normed_low,
                queries,
                keys_all,
                values_all,
                log_total,
                heads_low,
                refined,
                scaled_two,
                inverse_two,
                normed_mid,
                gate_up,
                hidden,
            )
        )
    grad_stream = cotangent.astype(jnp.float32)
    gain_list = [None] * layer_total
    bias_list = [None] * layer_total
    input_bias_list = [None] * layer_total
    qkv_shards = [None] * layer_total
    out_shards = [None] * layer_total
    gate_up_shards = [None] * layer_total
    down_shards = [None] * layer_total
    for layer_index in reversed(range(layer_total)):
        (
            kept_weights,
            scaled_one,
            inverse_one,
            normed_low,
            queries,
            keys_all,
            values_all,
            log_total,
            heads_low,
            refined,
            scaled_two,
            inverse_two,
            normed_mid,
            gate_up,
            hidden,
        ) = saved[layer_index]
        weights = (
            lax.all_gather(input_projection[layer_index], ("shard", "ctx"), axis=0, tiled=True),
            lax.all_gather(output_projection[layer_index], ("shard", "ctx"), axis=0, tiled=True),
            lax.all_gather(gate_up_weight[layer_index], ("shard", "ctx"), axis=0, tiled=True),
            lax.all_gather(down_weight[layer_index], ("shard", "ctx"), axis=0, tiled=True),
        )
        qkv_full, out_full, gate_up_full, down_full = weights
        branch = grad_stream.astype(jnp.bfloat16)
        grad_down = jnp.einsum("td,tf->df", branch, hidden, preferred_element_type=jnp.float32)
        grad_hidden = jnp.einsum("td,df->tf", branch, down_full, preferred_element_type=jnp.float32)
        gate_half = gate_up[:, 0]
        up_half = gate_up[:, 1]
        sigmoid_gate = jax.nn.sigmoid(gate_half)
        grad_gate = (
            grad_hidden * up_half * (sigmoid_gate * (1.0 + gate_half * (1.0 - sigmoid_gate)))
        )
        grad_up = grad_hidden * (gate_half * sigmoid_gate)
        grad_gate_up = jnp.stack([grad_gate, grad_up], axis=1).astype(jnp.bfloat16)
        grad_gate_weight = jnp.einsum(
            "td,tcf->dcf", normed_mid, grad_gate_up, preferred_element_type=jnp.float32
        )
        gate_up_shards[layer_index], down_shards[layer_index] = (
            lax.psum_scatter(grad_gate_weight, ("shard", "ctx"), scatter_dimension=0, tiled=True),
            lax.psum_scatter(grad_down, ("shard", "ctx"), scatter_dimension=0, tiled=True),
        )
        grad_normed_two = lax.psum(
            jnp.einsum(
                "tcf,dcf->td", grad_gate_up, gate_up_full, preferred_element_type=jnp.float32
            ).astype(jnp.bfloat16),
            "tp",
        ).astype(jnp.float32)
        grad_input_two, gain_two, bias_two = norm_back(
            grad_normed_two, scaled_two, inverse_two, norm_gain[layer_index, 1]
        )
        grad_middle = grad_stream + grad_input_two
        branch = grad_middle.astype(jnp.bfloat16)
        grad_out_weight = jnp.einsum(
            "td,th->dh", branch, heads_low, preferred_element_type=jnp.float32
        )
        grad_heads = (
            jnp.einsum("td,dh->th", branch, out_full, preferred_element_type=jnp.float32)
            .astype(jnp.bfloat16)
            .reshape(row_count, head_count, head_size)
        )
        row_dots = jnp.einsum("rhe,rhe->hr", grad_heads.astype(jnp.float32), refined)
        grad_query, grad_keys, grad_values = attend_back(
            queries,
            keys_all,
            values_all,
            grad_heads,
            row_dots,
            log_total,
            seq_ids,
            query_pos,
            key_seq,
            key_pos,
            score_scale,
        )
        grad_key, grad_value = (
            lax.psum_scatter(
                grad_keys.astype(jnp.bfloat16), "ctx", scatter_dimension=0, tiled=True
            ).astype(jnp.float32),
            lax.psum_scatter(
                grad_values.astype(jnp.bfloat16), "ctx", scatter_dimension=0, tiled=True
            ).astype(jnp.float32),
        )
        grad_query = rotate(grad_query, cosine, -sine)
        grad_key = rotate(grad_key, cosine, -sine)
        grad_joined = (
            jnp.stack([grad_query, grad_key, grad_value], axis=1)
            .reshape(row_count, 3, local_width)
            .astype(jnp.bfloat16)
        )
        input_bias_list[layer_index] = jnp.sum(grad_joined.astype(jnp.float32), axis=0)
        grad_qkv_weight = jnp.einsum(
            "td,tch->dch", normed_low, grad_joined, preferred_element_type=jnp.float32
        )
        qkv_shards[layer_index], out_shards[layer_index] = (
            lax.psum_scatter(grad_qkv_weight, ("shard", "ctx"), scatter_dimension=0, tiled=True),
            lax.psum_scatter(grad_out_weight, ("shard", "ctx"), scatter_dimension=0, tiled=True),
        )
        grad_normed_one = lax.psum(
            jnp.einsum(
                "tch,dch->td", grad_joined, qkv_full, preferred_element_type=jnp.float32
            ).astype(jnp.bfloat16),
            "tp",
        ).astype(jnp.float32)
        grad_input_one, gain_one, bias_one = norm_back(
            grad_normed_one, scaled_one, inverse_one, norm_gain[layer_index, 0]
        )
        grad_stream = grad_middle + grad_input_one
        gain_list[layer_index] = jnp.stack([gain_one, gain_two])
        bias_list[layer_index] = jnp.stack([bias_one, bias_two])
    gain_total, bias_total, input_bias_total = lax.psum(
        (jnp.stack(gain_list), jnp.stack(bias_list), jnp.stack(input_bias_list)), ("shard", "ctx")
    )
    return (
        stream.astype(jnp.bfloat16),
        grad_stream,
        gain_total,
        bias_total,
        input_bias_total,
        jnp.stack(qkv_shards),
        jnp.stack(out_shards),
        jnp.stack(gate_up_shards),
        jnp.stack(down_shards),
    )


def solution(mesh):
    in_specs = (
        P(("shard", "ctx"), None),
        P(("shard", "ctx"), None),
        P("shard", None),
        P(),
        P(),
        P(None, None, "tp"),
        P(None, ("shard", "ctx"), None, "tp"),
        P(None, ("shard", "ctx"), "tp"),
        P(None, ("shard", "ctx"), None, "tp"),
        P(None, ("shard", "ctx"), "tp"),
    )
    out_specs = (
        P(("shard", "ctx"), None),
        P(("shard", "ctx"), None),
        P(),
        P(),
        P(None, None, "tp"),
        P(None, ("shard", "ctx"), None, "tp"),
        P(None, ("shard", "ctx"), "tp"),
        P(None, ("shard", "ctx"), None, "tp"),
        P(None, ("shard", "ctx"), "tp"),
    )
    return jax.shard_map(body, mesh=mesh, in_specs=in_specs, out_specs=out_specs, check_vma=False)
```

profile of v0, /device:TPU:8, one launch (start us, length us, event | category | flops | bytes accessed | tf_op | source)
XLA Modules:
  0.0 7009.4 jit_solution(5031960702310588644)
XLA Ops:
  17.1 145.5 %all-gather.27.cloned.1.call-done = bf16[1,2048,3,1024]{3,1,2,0:T(8,128)(2,1)} async-done(((bf16[1,128,3,1024]{3,1,2,0:T(8,128)(2,1)}), bf16[1,2048,3,1024]{3,1,2,0:T(8,128)(2,1)}) %all-gather.27.cloned.1.call-update) | async-done | bytes 12582928 | tf_op jit(solution)/shard_map/all_gather | solution.py:216
  191.9 46.8 all-gather.23.cloned.1.call-done
  244.1 75.8 %while.82 = (s32[]{:T(128)}, f32[16,512]{1,0:T(8,128)S(1)}, f32[16,512]{1,0:T(8,128)S(1)}, s32[512]{0:T(512)S(1)}, s32[4,512]{1,0:T(4,128)}, /*index=5*/s32[4,51...) while((s32[]{:T(128)}, f32[16,512]{1,0:T(8,128)S(1)}, ...), condition=%wide.region_9.10_spmd.clone, body=%wide.region_6.9_spmd.clone.sunk | while | flops 567058432 | bytes 36881016 | solution.py:112
  333.0 116.1 %while.83 = (s32[]{:T(128)}, f32[512,16,64]{0,2,1:T(8,128)S(1)}, f32[512,16,64]{0,2,1:T(8,128)}, bf16[4,512,16,64]{1,3,2,0:T(8,128)(2,1)}, s32[512]{0:T(512)S(1)...) while((s32[]{:T(128)}, f32[512,16,64]{0,2,1:T(8,128)S(1)}, ...), condition=%wide.region_11.12_spmd.clone, body=%wide.region_10.11_spmd.clone.sunk | while | flops 1659633664 | bytes 130893480 | solution.py:134
  466.7 20.0 all-reduce.11.cloned.1.call-done
  492.0 248.7 %all-gather.33.cloned.1.call-done = bf16[1,2048,2,2816]{3,1,2,0:T(8,128)(2,1)} async-done(((bf16[1,128,2,2816]{3,1,2,0:T(8,128)(2,1)}), bf16[1,2048,2,2816]{3,1,2,0:T(8,128)(2,1)}) %all-gather.33.cloned.1.call-update) | async-done | bytes 23068688 | tf_op jit(solution)/shard_map/all_gather | solution.py:218
  740.7 20.7 fusion.114
  766.7 117.5 %all-gather.35.cloned.1.call-done = bf16[1,2048,2816]{2,1,0:T(8,128)(2,1)} async-done(((bf16[1,128,2816]{2,1,0:T(8,128)(2,1)}), bf16[1,2048,2816]{2,1,0:T(8,128)(2,1)}) %all-gather.35.cloned.1.call-update) | async-done | bytes 11534352 | tf_op jit(solution)/shard_map/all_gather | solution.py:219
  895.0 20.9 all-reduce.13.cloned.1.call-done
  921.8 147.8 %all-gather.37.cloned.1.call-done = bf16[1,2048,3,1024]{3,1,2,0:T(8,128)(2,1)} async-done(((bf16[1,128,3,1024]{3,1,2,0:T(8,128)(2,1)}), bf16[1,2048,3,1024]{3,1,2,0:T(8,128)(2,1)}) %all-gather.37.cloned.1.call-update) | async-done | bytes 12582928 | tf_op jit(solution)/shard_map/all_gather | solution.py:216
  1069.6 13.2 broadcast_add_fusion
  1099.8 47.7 all-gather.25.cloned.1.call-done
  1152.2 75.9 %while.84 = (s32[]{:T(128)}, f32[16,512]{1,0:T(8,128)S(1)}, f32[16,512]{1,0:T(8,128)S(1)}, s32[512]{0:T(512)S(1)}, s32[4,512]{1,0:T(4,128)}, /*index=5*/s32[4,51...) while((s32[]{:T(128)}, f32[16,512]{1,0:T(8,128)S(1)}, ...), condition=%wide.region_21.22_spmd.clone, body=%wide.region_18.21_spmd.clone.sunk | while | flops 567058432 | bytes 36881016 | solution.py:112
  1241.3 116.2 %while.85 = (s32[]{:T(128)}, f32[512,16,64]{0,2,1:T(8,128)S(1)}, f32[512,16,64]{0,2,1:T(8,128)}, bf16[4,512,16,64]{1,3,2,0:T(8,128)(2,1)}, s32[512]{0:T(512)S(1)...) while((s32[]{:T(128)}, f32[512,16,64]{0,2,1:T(8,128)S(1)}, ...), condition=%wide.region_23.24_spmd.clone, body=%wide.region_22.23_spmd.clone.sunk | while | flops 1659633664 | bytes 130893480 | solution.py:134
  1280.8 13.0 bitcast_add_fusion.15
  1338.8 13.0 bitcast_add_fusion.15
  1369.4 25.6 all-reduce.15.cloned.1.call-done
  1401.5 247.4 %all-gather.43.cloned.1.call-done = bf16[1,2048,2,2816]{3,1,2,0:T(8,128)(2,1)} async-done(((bf16[1,128,2,2816]{3,1,2,0:T(8,128)(2,1)}), bf16[1,2048,2,2816]{3,1,2,0:T(8,128)(2,1)}) %all-gather.43.cloned.1.call-update) | async-done | bytes 23068688 | tf_op jit(solution)/shard_map/all_gather | solution.py:218
  1649.0 20.8 fusion.110
  1669.8 122.5 %all-gather.45.cloned.1.call-done = bf16[1,2048,2816]{2,1,0:T(8,128)(2,1)} async-done(((bf16[1,128,2816]{2,1,0:T(8,128)(2,1)}), bf16[1,2048,2816]{2,1,0:T(8,128)(2,1)}) %all-gather.45.cloned.1.call-update) | async-done | bytes 11534352 | tf_op jit(solution)/shard_map/all_gather | solution.py:219
  1792.3 15.5 fusion.199
  1807.8 19.3 bitcast_convert_fusion.3
  1827.2 21.6 all-reduce.17.cloned.1.call-done
  1873.5 172.0 %while.86 = (s32[]{:T(128)}, f32[512,16,64]{0,2,1:T(8,128)S(1)}, bf16[4,512,16,64]{1,3,2,0:T(8,128)(2,1)}, bf16[4,512,16,64]{1,3,2,0:T(8,128)(2,1)}, bf16[4,512,...) while((s32[]{:T(128)}, f32[512,16,64]{0,2,1:T(8,128)S(1)}, ...), condition=%wide.region_32.33_spmd.clone, body=%wide.region_31.32_spmd.clone.sunk | while | flops 2728656896 | bytes 129878744 | solution.py:177
  2057.6 46.6 reduce-scatter.13.cloned.1.call-done
  2108.4 51.6 reduce-scatter.15.cloned.1.call-done
  2172.7 21.6 all-reduce.19.cloned.1.call-done
  2202.8 15.9 fusion.200
  2218.7 19.5 bitcast_convert_fusion.1
  2238.4 22.3 all-reduce.21.cloned.1.call-done
  2284.9 172.5 %while.87 = (s32[]{:T(128)}, f32[512,16,64]{0,2,1:T(8,128)S(1)}, bf16[4,512,16,64]{1,3,2,0:T(8,128)(2,1)}, bf16[4,512,16,64]{1,3,2,0:T(8,128)(2,1)}, bf16[4,512,...) while((s32[]{:T(128)}, f32[512,16,64]{0,2,1:T(8,128)S(1)}, ...), condition=%wide.region_42.43_spmd.clone, body=%wide.region_41.42_spmd.clone.sunk | while | flops 2728656896 | bytes 129878744 | solution.py:177
  2480.9 35.1 reduce-scatter.17.cloned.1.call-done
  2520.2 52.3 reduce-scatter.19.cloned.1.call-done
  2592.5 22.1 all-reduce.25.cloned.1.call-done
  2637.4 13.1 convolution_bitcast_fusion
  2650.5 13.4 fusion.220
  2665.1 14.7 fusion.237
  2681.0 13.5 fusion.226
  2695.3 24.4 fusion.182
  2720.4 24.6 fusion.181
  2755.4 152.1 %reduce-scatter.27.cloned.1.call-done = f32[128,1024]{1,0:T(8,128)} async-done(((f32[2048,1024]{1,0:T(8,128)}), f32[128,1024]{1,0:T(8,128)}) %reduce-scatter.27.cloned.1.call-update) | async-done | bytes 524304 | tf_op jit(solution)/shard_map/reduce_scatter | solution.py:386
  2907.6 182.5 %reduce-scatter.25.cloned.1.call-done = f32[128,1024]{1,0:T(8,128)} async-done(((f32[2048,1024]{1,0:T(8,128)}), f32[128,1024]{1,0:T(8,128)}) %reduce-scatter.25.cloned.1.call-update) | async-done | bytes 524304 | tf_op jit(solution)/shard_map/reduce_scatter | solution.py:386
  3092.4 475.7 %reduce-scatter.35.cloned.1.call-done = f32[128,2816]{1,0:T(8,128)} async-done(((f32[2048,2816]{1,0:T(8,128)}), f32[128,2816]{1,0:T(8,128)}) %reduce-scatter.35.cloned.1.call-update) | async-done | bytes 1441808 | tf_op jit(solution)/shard_map/reduce_scatter | solution.py:330
  3568.0 482.2 %reduce-scatter.33.cloned.1.call-done = f32[128,2816]{1,0:T(8,128)} async-done(((f32[2048,2816]{1,0:T(8,128)}), f32[128,2816]{1,0:T(8,128)}) %reduce-scatter.33.cloned.1.call-update) | async-done | bytes 1441808 | tf_op jit(solution)/shard_map/reduce_scatter | solution.py:330
  4053.8 522.8 %reduce-scatter.23.cloned.1.call-done = f32[128,3,1024]{2,0,1:T(8,128)} async-done(((f32[2048,3,1024]{2,0,1:T(8,128)}), f32[128,3,1024]{2,0,1:T(8,128)}) %reduce-scatter.23.cloned.1.call-update) | async-done | bytes 1572880 | tf_op jit(solution)/shard_map/reduce_scatter | solution.py:385
  4576.6 524.7 %reduce-scatter.21.cloned.1.call-done = f32[128,3,1024]{2,0,1:T(8,128)} async-done(((f32[2048,3,1024]{2,0,1:T(8,128)}), f32[128,3,1024]{2,0,1:T(8,128)}) %reduce-scatter.21.cloned.1.call-update) | async-done | bytes 1572880 | tf_op jit(solution)/shard_map/reduce_scatter | solution.py:385
  5105.2 940.3 %reduce-scatter.31.cloned.1.call-done = f32[128,2,2816]{2,0,1:T(8,128)} async-done(((f32[2048,2,2816]{2,0,1:T(8,128)}), f32[128,2,2816]{2,0,1:T(8,128)}) %reduce-scatter.31.cloned.1.call-update) | async-done | bytes 2883600 | tf_op jit(solution)/shard_map/reduce_scatter | solution.py:329
  6045.5 945.8 %reduce-scatter.29.cloned.1.call-done = f32[128,2,2816]{2,0,1:T(8,128)} async-done(((f32[2048,2,2816]{2,0,1:T(8,128)}), f32[128,2,2816]{2,0,1:T(8,128)}) %reduce-scatter.29.cloned.1.call-update) | async-done | bytes 2883600 | tf_op jit(solution)/shard_map/reduce_scatter | solution.py:329
  (632 shorter events, 1048.3 us)
Async XLA Ops:
  7.2 155.4 %all-gather.27.cloned.1.call-start = ((), (), s32[]{:S(2)}) async-start(), calls=%async_computation.32 | async-start | bytes 13369344 | tf_op jit(solution)/shard_map/all_gather | solution.py:216
  10.1 228.6 %all-gather.23.cloned.1.call-start = ((), (), s32[]{:S(2)}) async-start(), calls=%async_computation.12 | async-start | bytes 5242880 | tf_op jit(solution)/shard_map/all_gather | solution.py:235
  14.3 159.7 %copy-start.89 = (f32[512]{0:T(512)}, f32[512]{0:T(512)S(1)}, u32[]{:S(2)}) copy-start(f32[512]{0:T(512)S(1)} %broadcast_multiply_fusion.13) | copy-start | bytes 6148
  15.0 159.0 %copy-start.91 = (f32[512]{0:T(512)}, f32[512]{0:T(512)S(1)}, u32[]{:S(2)}) copy-start(f32[512]{0:T(512)S(1)} %add_rsqrt_fusion.3) | copy-start | bytes 6148
  15.8 167.7 %copy-start.50 = (f32[512,8]{0,1:T(8,128)}, f32[512,8]{0,1:T(8,128)S(1)}, u32[]{:S(2)}) copy-start(f32[512,8]{0,1:T(8,128)S(1)} %get-tuple-element.1072) | copy-start | bytes 49156
  15.8 167.7 %copy-start.56 = (f32[512,8]{0,1:T(8,128)}, f32[512,8]{0,1:T(8,128)S(1)}, u32[]{:S(2)}) copy-start(f32[512,8]{0,1:T(8,128)S(1)} %get-tuple-element.1071) | copy-start | bytes 49156
  16.5 157.6 %copy-start.58 = (f32[1,1,2048]{2,1,0:T(1,128)}, f32[1,1,2048]{2,1,0:T(1,128)S(1)}, u32[]{:S(2)}) copy-start(f32[1,1,2048]{2,1,0:T(1,128)S(1)} %get-tuple-element.1058) | copy-start | bytes 24580
  17.1 157.0 %copy-start.107 = (f32[1,1,2048]{2,1,0:T(1,128)}, f32[1,1,2048]{2,1,0:T(1,128)S(1)}, u32[]{:S(2)}) copy-start(f32[1,1,2048]{2,1,0:T(1,128)S(1)} %get-tuple-element.1062) | copy-start | bytes 24580
  185.9 134.0 %all-gather.29.cloned.1.call-start = ((), (), s32[]{:S(2)}) async-start(), calls=%async_computation.33 | async-start | bytes 5242880 | tf_op jit(solution)/shard_map/all_gather | solution.py:236
  188.7 261.6 %all-gather.31.cloned.1.call-start = ((), (), s32[]{:S(2)}) async-start(), calls=%async_computation.34 | async-start | bytes 4456448 | tf_op jit(solution)/shard_map/all_gather | solution.py:217
  189.6 297.1 %all-reduce.11.cloned.1.call-start = ((), (), s32[]{:S(2)}) async-start(), calls=%async_computation.13 | async-start | bytes 8388608 | tf_op jit(solution)/shard_map/psum | solution.py:242
  457.5 283.3 %all-gather.33.cloned.1.call-start = ((), (), s32[]{:S(2)}) async-start(), calls=%async_computation.35 | async-start | bytes 24510464 | tf_op jit(solution)/shard_map/all_gather | solution.py:218
  463.6 420.6 %all-gather.35.cloned.1.call-start = ((), (), s32[]{:S(2)}) async-start(), calls=%async_computation.36 | async-start | bytes 12255232 | tf_op jit(solution)/shard_map/all_gather | solution.py:219
  466.7 449.2 %all-reduce.13.cloned.1.call-start = ((), (), s32[]{:S(2)}) async-start(), calls=%async_computation.14 | async-start | bytes 4194304 | tf_op jit(solution)/shard_map/psum | solution.py:254
  489.4 251.3 %copy-start.60 = (f32[1,1,2048]{2,1,0:T(1,128)S(1)}, f32[1,1,2048]{2,1,0:T(1,128)}, u32[]{:S(2)}) copy-start(f32[1,1,2048]{2,1,0:T(1,128)} %get-tuple-element.1057) | copy-start | bytes 24580
  489.4 251.3 %copy-start.103 = (f32[1,1,2048]{2,1,0:T(1,128)S(1)}, f32[1,1,2048]{2,1,0:T(1,128)}, u32[]{:S(2)}) copy-start(f32[1,1,2048]{2,1,0:T(1,128)} %get-tuple-element.1061) | copy-start | bytes 24580
  489.5 272.0 %copy-start.69 = (f32[512]{0:T(512)}, f32[512]{0:T(512)S(1)}, u32[]{:S(2)}) copy-start(f32[512]{0:T(512)S(1)} %broadcast_multiply_fusion.12) | copy-start | bytes 6148
  492.0 269.4 %copy-start.93 = (f32[512]{0:T(512)}, f32[512]{0:T(512)S(1)}, u32[]{:S(2)}) copy-start(f32[512]{0:T(512)S(1)} %add_rsqrt_fusion.2) | copy-start | bytes 6148
  894.2 175.4 %all-gather.37.cloned.1.call-start = ((), (), s32[]{:S(2)}) async-start(), calls=%async_computation.37 | async-start | bytes 13369344 | tf_op jit(solution)/shard_map/all_gather | solution.py:216
  895.0 252.5 %all-gather.25.cloned.1.call-start = ((), (), s32[]{:S(2)}) async-start(), calls=%async_computation.15 | async-start | bytes 5242880 | tf_op jit(solution)/shard_map/all_gather | solution.py:235
  919.3 163.5 %copy-start.72 = (f32[512]{0:T(512)}, f32[512]{0:T(512)S(1)}, u32[]{:S(2)}) copy-start(f32[512]{0:T(512)S(1)} %broadcast_multiply_fusion.11) | copy-start | bytes 6148
  921.8 161.0 %copy-start.96 = (f32[512]{0:T(512)}, f32[512]{0:T(512)S(1)}, u32[]{:S(2)}) copy-start(f32[512]{0:T(512)S(1)} %add_rsqrt_fusion.1) | copy-start | bytes 6148
  1094.7 133.5 %all-gather.39.cloned.1.call-start = ((), (), s32[]{:S(2)}) async-start(), calls=%async_computation.38 | async-start | bytes 5242880 | tf_op jit(solution)/shard_map/all_gather | solution.py:236
  1097.5 261.2 %all-gather.41.cloned.1.call-start = ((), (), s32[]{:S(2)}) async-start(), calls=%async_computation.39 | async-start | bytes 4456448 | tf_op jit(solution)/shard_map/all_gather | solution.py:217
  1098.1 296.9 %all-reduce.15.cloned.1.call-start = ((), (), s32[]{:S(2)}) async-start(), calls=%async_computation.16 | async-start | bytes 8388608 | tf_op jit(solution)/shard_map/psum | solution.py:242
  1365.7 283.2 %all-gather.43.cloned.1.call-start = ((), (), s32[]{:S(2)}) async-start(), calls=%async_computation.40 | async-start | bytes 24510464 | tf_op jit(solution)/shard_map/all_gather | solution.py:218
  1368.3 424.0 %all-gather.45.cloned.1.call-start = ((), (), s32[]{:S(2)}) async-start(), calls=%async_computation.41 | async-start | bytes 12255232 | tf_op jit(solution)/shard_map/all_gather | solution.py:219
  1368.9 479.9 %all-reduce.17.cloned.1.call-start = ((), (), s32[]{:S(2)}) async-start(), calls=%async_computation.17 | async-start | bytes 4194304 | tf_op jit(solution)/shard_map/psum | solution.py:332
  1399.0 250.0 %copy-start.63 = (f32[1,1,2048]{2,1,0:T(1,128)S(1)}, f32[1,1,2048]{2,1,0:T(1,128)}, u32[]{:S(2)}) copy-start(f32[1,1,2048]{2,1,0:T(1,128)} %get-tuple-element.1056) | copy-start | bytes 24580
  1399.0 250.0 %copy-start.105 = (f32[1,1,2048]{2,1,0:T(1,128)S(1)}, f32[1,1,2048]{2,1,0:T(1,128)}, u32[]{:S(2)}) copy-start(f32[1,1,2048]{2,1,0:T(1,128)} %get-tuple-element.1060) | copy-start | bytes 24580
  1399.0 455.2 %copy-start.75 = (f32[512]{0:T(512)}, f32[512]{0:T(512)S(1)}, u32[]{:S(2)}) copy-start(f32[512]{0:T(512)S(1)} %broadcast_multiply_fusion.10) | copy-start | bytes 6148
  1401.5 452.6 %copy-start.99 = (f32[512]{0:T(512)}, f32[512]{0:T(512)S(1)}, u32[]{:S(2)}) copy-start(f32[512]{0:T(512)S(1)} %add_rsqrt_fusion) | copy-start | bytes 6148
  1827.2 277.1 %reduce-scatter.13.cloned.1.call-start = ((), (), s32[]{:S(2)}) async-start(), calls=%async_computation.18 | async-start | bytes 5242880 | tf_op jit(solution)/shard_map/reduce_scatter | solution.py:366
  2050.5 109.5 %reduce-scatter.15.cloned.1.call-start = ((), (), s32[]{:S(2)}) async-start(), calls=%async_computation.19 | async-start | bytes 5242880 | tf_op jit(solution)/shard_map/reduce_scatter | solution.py:369
  2055.8 138.5 %all-reduce.19.cloned.1.call-start = ((), (), s32[]{:S(2)}) async-start(), calls=%async_computation.20 | async-start | bytes 4194304 | tf_op jit(solution)/shard_map/psum | solution.py:388
  2172.6 88.1 %all-reduce.21.cloned.1.call-start = ((), (), s32[]{:S(2)}) async-start(), calls=%async_computation.21 | async-start | bytes 4194304 | tf_op jit(solution)/shard_map/psum | solution.py:332
  2238.2 277.8 %reduce-scatter.17.cloned.1.call-start = ((), (), s32[]{:S(2)}) async-start(), calls=%async_computation.22 | async-start | bytes 5242880 | tf_op jit(solution)/shard_map/reduce_scatter | solution.py:366
  2462.3 110.2 %reduce-scatter.19.cloned.1.call-start = ((), (), s32[]{:S(2)}) async-start(), calls=%async_computation.23 | async-start | bytes 5242880 | tf_op jit(solution)/shard_map/reduce_scatter | solution.py:369
  2467.6 147.0 %all-reduce.25.cloned.1.call-start = ((), (), s32[]{:S(2)}) async-start(), calls=%async_computation.43 | async-start | bytes 8388608 | tf_op jit(solution)/shard_map/psum | solution.py:254
  2585.8 168.3 %all-reduce.23.cloned.1.call-start = ((), (), s32[]{:S(2)}) async-start(), calls=%async_computation.42 | async-start | bytes 196608 | tf_op jit(solution)/shard_map/psum | solution.py:400
  2620.0 287.5 %reduce-scatter.27.cloned.1.call-start = ((), (), s32[]{:S(2)}) async-start(), calls=%async_computation.27 | async-start | bytes 8912896 | tf_op jit(solution)/shard_map/reduce_scatter | solution.py:386
  2628.2 461.9 %reduce-scatter.25.cloned.1.call-start = ((), (), s32[]{:S(2)}) async-start(), calls=%async_computation.26 | async-start | bytes 8912896 | tf_op jit(solution)/shard_map/reduce_scatter | solution.py:386
  2637.3 930.7 %reduce-scatter.35.cloned.1.call-start = ((), (), s32[]{:S(2)}) async-start(), calls=%async_computation.31 | async-start | bytes 24510464 | tf_op jit(solution)/shard_map/reduce_scatter | solution.py:330
  2650.4 1399.8 %reduce-scatter.33.cloned.1.call-start = ((), (), s32[]{:S(2)}) async-start(), calls=%async_computation.30 | async-start | bytes 24510464 | tf_op jit(solution)/shard_map/reduce_scatter | solution.py:330
  2663.9 1912.7 %reduce-scatter.23.cloned.1.call-start = ((), (), s32[]{:S(2)}) async-start(), calls=%async_computation.25 | async-start | bytes 26738688 | tf_op jit(solution)/shard_map/reduce_scatter | solution.py:385
  2679.8 2421.4 %reduce-scatter.21.cloned.1.call-start = ((), (), s32[]{:S(2)}) async-start(), calls=%async_computation.24 | async-start | bytes 26738688 | tf_op jit(solution)/shard_map/reduce_scatter | solution.py:385
  2694.6 3350.9 %reduce-scatter.31.cloned.1.call-start = ((), (), s32[]{:S(2)}) async-start(), calls=%async_computation.29 | async-start | bytes 49020928 | tf_op jit(solution)/shard_map/reduce_scatter | solution.py:329
  2719.7 4271.6 %reduce-scatter.29.cloned.1.call-start = ((), (), s32[]{:S(2)}) async-start(), calls=%async_computation.28 | async-start | bytes 49020928 | tf_op jit(solution)/shard_map/reduce_scatter | solution.py:329
  (116 other events, 2056.2 us)
Sparse Core Ops, SparseCore 0:
  11.4 151.1 all-gather.26
  186.0 52.5 all-gather.22
  241.1 52.5 all-gather.28
  296.3 76.0 all-gather.30
  457.6 29.1 all-reduce.10
  490.3 250.3 all-gather.32
  743.8 140.3 all-gather.34
  894.3 21.4 all-reduce.12
  918.7 150.9 all-gather.36
  1094.8 52.5 all-gather.24
  1149.3 52.5 all-gather.38
  1204.5 76.0 all-gather.40
  1365.9 29.0 all-reduce.14
  1398.6 250.3 all-gather.42
  1651.9 140.3 all-gather.44
  1827.3 21.4 all-reduce.16
  2050.6 53.5 reduce-scatter.12
  2107.3 52.6 reduce-scatter.14
  2172.7 21.4 all-reduce.18
  2238.3 22.3 all-reduce.20
  2462.4 53.5 reduce-scatter.16
  2519.8 52.6 reduce-scatter.18
  2585.8 28.7 all-reduce.24
  2621.9 105.7 all-reduce.22
  2730.1 177.4 reduce-scatter.26
  2909.8 180.2 reduce-scatter.24
  3092.3 475.6 reduce-scatter.34
  3570.4 479.7 reduce-scatter.32
  4052.7 523.8 reduce-scatter.22
  4578.9 522.3 reduce-scatter.20
  5103.7 941.7 reduce-scatter.30
  6048.0 943.2 reduce-scatter.28
where the time goes:
time: 7030 us; the launch traced here: 7010 us
  waiting for transfers between devices  5690 us (81%)
  matrix products  923 us (13%)
  local copies, waits for them, and re-layouts  196 us (3%)
  other arithmetic  177 us (3%)
    reduce_scatter x2, waiting for transfers between devices, body(): lax.psum_scatter(grad_gate_weight, ('shard', 'ctx'), scatter_dimension=0,...  1890 us
    reduce_scatter x2, waiting for transfers between devices, body(): lax.psum_scatter(grad_qkv_weight, ('shard', 'ctx'), scatter_dimension=0,...  1050 us
    reduce_scatter x2, waiting for transfers between devices, body(): lax.psum_scatter(grad_down, ('shard', 'ctx'), scatter_dimension=0, tiled=...  958 us
    all_gather x2, waiting for transfers between devices, body(): lax.all_gather(gate_up_weight[layer_index], ('shard', 'ctx'), axis=0, til...  496 us
    reduce_scatter x2, waiting for transfers between devices, body(): lax.psum_scatter(grad_out_weight, ('shard', 'ctx'), scatter_dimension=0,...  335 us
    all_gather x2, waiting for transfers between devices, body(): lax.all_gather(input_projection[layer_index], ('shard', 'ctx'), axis=0, t...  293 us
    all_gather x2, waiting for transfers between devices, body(): lax.all_gather(down_weight[layer_index], ('shard', 'ctx'), axis=0, tiled=...  240 us
    dot_general x24, matrix products, masked_scores(): jnp.einsum('rhe,khe->hrk', queries, key_block, preferred_element_type=jnp...  221 us
  transfers between devices with their start and end apart: 32, of which 27 were waited for; matrix products, arithmetic and copies ran while one was open for 10% of the time, Pallas kernels for 0%

commit v1 on v0

v1 whole, which is shorter than its diff:
```python
import functools
import math

import jax
import jax.numpy as jnp
from jax import lax
from jax.experimental import pallas as pl
from jax.experimental.pallas import tpu as pltpu
from jax.sharding import PartitionSpec as P

HEAD = 64
ROT = 16
LANES = 128

norm_eps = 1e-05
rotary_base = 10000.0
blocked = -(2.0**100)
low = jnp.bfloat16
full = jnp.float32


def row_meta(seq_lengths, row_count):
    seq_ends = jnp.cumsum(seq_lengths, dtype=jnp.int32)
    row_index = jnp.arange(row_count, dtype=jnp.int32)
    seq_ids = jnp.sum(
        (row_index[:, None] >= seq_ends[None, :]).astype(jnp.int32), axis=1, dtype=jnp.int32
    )
    one_hot = (
        seq_ids[:, None] == jnp.arange(seq_lengths.shape[0], dtype=jnp.int32)[None, :]
    ).astype(jnp.int32)
    seq_start = jnp.sum(one_hot * (seq_ends - seq_lengths)[None, :], axis=1, dtype=jnp.int32)
    length = jnp.sum(one_hot * seq_lengths[None, :], axis=1, dtype=jnp.int32)
    return (seq_ids, length, row_index - seq_start)


def wide_rotary_tables(positions):
    half_rot = ROT // 2
    frequency = rotary_base ** (-(2.0 * jnp.arange(half_rot, dtype=full)) / ROT)
    lane = jnp.arange(LANES, dtype=jnp.int32) % HEAD
    lane_frequency = jnp.where(lane < ROT, jnp.tile(frequency, LANES // half_rot), 0.0)
    sign = jnp.where(lane < half_rot, -1.0, 1.0)
    angles = positions.astype(full)[:, None] * lane_frequency[None, :]
    return (jnp.cos(angles), jnp.sin(angles) * sign[None, :])


def norm_parts(stream, gain_row, bias_row):
    row_mean = jnp.mean(stream, axis=-1, keepdims=True)
    centered = stream - row_mean
    variance = jnp.mean(centered * centered, axis=-1, keepdims=True)
    inverse = lax.rsqrt(variance + norm_eps)
    scaled = centered * inverse
    return (scaled, inverse, scaled * gain_row + bias_row)


def norm_back(grad_normed, scaled, inverse, gain_row):
    grad_scaled = grad_normed * gain_row
    inner = (
        grad_scaled
        - jnp.mean(grad_scaled, axis=-1, keepdims=True)
        - scaled * jnp.mean(grad_scaled * scaled, axis=-1, keepdims=True)
    )
    return (inverse * inner, jnp.sum(grad_normed * scaled, axis=0), jnp.sum(grad_normed, axis=0))


def dot_nn(left, right):
    return lax.dot_general(left, right, (((1,), (0,)), ((), ())), preferred_element_type=full)


def dot_nt(left, right):
    return lax.dot_general(left, right, (((1,), (1,)), ((), ())), preferred_element_type=full)


def dot_tn(left, right):
    return lax.dot_general(left, right, (((0,), (0,)), ((), ())), preferred_element_type=full)


def partner(values, lane):
    near = pltpu.roll(values, LANES - ROT // 2, 1)
    far = pltpu.roll(values, ROT // 2, 1)
    return jnp.where(lane % HEAD < ROT // 2, near, far)


def attend_kernel(ctx_count, tp_count, slots, order_ref, *refs):
    normed_refs = refs[:slots]
    weight_ref, bias_ref, cos_ref, sin_ref, query_mark_ref, key_mark_ref = refs[slots : slots + 6]
    out_refs = refs[slots + 6 : 2 * slots + 6]
    fine_ref, total_ref, rotated_ref, key_wide = refs[2 * slots + 6 :]
    rows_all = rotated_ref.shape[0]
    block = rows_all // ctx_count
    part = block // tp_count
    slot_parts = ctx_count * tp_count // slots
    lane_part = lax.broadcasted_iota(jnp.int32, (part, LANES), 1)
    to_exponent = float(HEAD) ** (-0.5) * math.log2(math.e)

    for place in range(ctx_count * tp_count):
        slot, start = place // slot_parts, place % slot_parts * part
        source = slice(start, start + part)
        target = pl.ds(pl.multiple_of(order_ref[place] * part, part), part)
        mark = pl.ds(pl.multiple_of(lax.rem(order_ref[place], tp_count) * part, part), part)
        cosine = cos_ref[target, :]
        sine = sin_ref[target, :]
        joined = dot_nn(normed_refs[slot][source, :], weight_ref[...])
        for kind in range(3):
            columns = slice(kind * LANES, (kind + 1) * LANES)
            values = joined[:, columns] + bias_ref[0, kind : kind + 1, :]
            if kind < 2:
                values = values * cosine + partner(values, lane_part) * sine
            rotated_ref[target, columns] = values.astype(low)
        key_wide[target, :LANES] = rotated_ref[target, LANES : 2 * LANES]
        key_wide[target, LANES:] = key_mark_ref[mark, :]

    tile = min(256, block)
    lane_tile = lax.broadcasted_iota(jnp.int32, (tile, LANES), 1)
    row_index = lax.broadcasted_iota(jnp.int32, (tile, block), 0)
    column_index = lax.broadcasted_iota(jnp.int32, (tile, block), 1)
    for place in range(ctx_count):
        past = place * block
        for head in range(2):

            def step(sub, unused):
                start = pl.multiple_of(sub * tile, tile)
                rows = pl.ds(pl.multiple_of(past + sub * tile, tile), tile)
                own_lanes = lane_tile // HEAD == head
                query = rotated_ref[rows, :LANES]
                query = jnp.concatenate(
                    [
                        jnp.where(own_lanes, query, jnp.zeros_like(query)),
                        query_mark_ref[pl.ds(start, tile), :],
                    ],
                    axis=1,
                )
                near = dot_nt(query, key_wide[past : past + block, :])
                near = jnp.where(column_index <= row_index + start, near, blocked)
                top = jnp.max(near, axis=1, keepdims=True)
                if past:
                    far = dot_nt(query, key_wide[:past, :])
                    top = jnp.maximum(top, jnp.max(far, axis=1, keepdims=True))
                shift = top * to_exponent
                near = jnp.exp2(near * to_exponent - shift)
                total = jnp.sum(near, axis=1, keepdims=True)
                out = dot_nn(near.astype(low), rotated_ref[past : past + block, 2 * LANES :])
                if past:
                    far = jnp.exp2(far * to_exponent - shift)
                    total = total + jnp.sum(far, axis=1, keepdims=True)
                    out = out + dot_nn(far.astype(low), rotated_ref[:past, 2 * LANES :])
                out = out / total
                fine_ref[rows, :] = jnp.where(own_lanes, out, fine_ref[rows, :])
                log_total = jnp.broadcast_to(shift + jnp.log2(total), (tile, LANES))
                total_ref[0, head : head + 1, rows] = jnp.transpose(log_total)[:1, :]
                return unused

            lax.fori_loop(0, block // tile, step, 0)

    for place in range(ctx_count * tp_count):
        slot, start = place // slot_parts, place % slot_parts * part
        source = pl.ds(pl.multiple_of(order_ref[place] * part, part), part)
        out_refs[slot][start : start + part, :] = fine_ref[source, :].astype(low)


def attend_back_kernel(ctx_count, tp_count, slots, order_ref, rotated_ref, *refs):
    grad_refs = refs[:slots]
    fine_ref, total_ref, cos_ref, sin_ref, query_mark_ref, key_mark_ref = refs[slots : slots + 6]
    out_refs = refs[slots + 6 : 2 * slots + 6]
    (
        sum_ref,
        query_wide,
        key_wide,
        key_turned,
        grad_own,
        row_dots,
        grad_query,
        grad_key,
        grad_value,
        query_rows_grad,
    ) = refs[2 * slots + 6 :]
    rows_all = rotated_ref.shape[0]
    slot_parts = ctx_count * tp_count // slots
    block = rows_all // ctx_count
    part = block // tp_count
    score_scale = float(HEAD) ** (-0.5)
    to_exponent = score_scale * math.log2(math.e)
    lane_block = lax.broadcasted_iota(jnp.int32, (block, LANES), 1)
    lane_part = lax.broadcasted_iota(jnp.int32, (part, LANES), 1)
    head_row = lax.broadcasted_iota(jnp.int32, (LANES, block), 0)

    for place in range(ctx_count * tp_count):
        slot, start = place // slot_parts, place % slot_parts * part
        target = pl.ds(pl.multiple_of(order_ref[place] * part, part), part)
        grad_own[0, target, :] = grad_refs[slot][start : start + part, :]

    def prepare(place, unused):
        rows = pl.ds(pl.multiple_of(place * block, block), block)
        grad = grad_own[0, rows, :]
        product = jnp.transpose(grad.astype(full) * fine_ref[rows, :])
        turned = jnp.transpose(rotated_ref[rows, LANES : 2 * LANES].astype(full))
        query = rotated_ref[rows, :LANES]
        for head in range(2):
            own_lanes = lane_block // HEAD == head
            row_dots[head : head + 1, rows] = jnp.sum(
                product[head * HEAD : (head + 1) * HEAD, :], axis=0, keepdims=True
            )
            key_turned[head, :, rows] = jnp.where(head_row // HEAD == head, turned, 0.0).astype(low)
            query_wide[head, rows, :LANES] = jnp.where(own_lanes, query, jnp.zeros_like(query))
            query_wide[head, rows, LANES:] = query_mark_ref[...]
            grad_own[head, rows, :] = jnp.where(own_lanes, grad, jnp.zeros_like(grad))
        key_wide[rows, :LANES] = rotated_ref[rows, LANES : 2 * LANES]
        key_wide[rows, LANES:] = key_mark_ref[...]
        grad_query[:, rows] = jnp.zeros((LANES, block), full)
        grad_key[rows, :] = jnp.zeros((block, LANES), full)
        grad_value[rows, :] = jnp.zeros((block, LANES), full)
        return unused

    lax.fori_loop(0, ctx_count, prepare, 0)

    key_index = lax.broadcasted_iota(jnp.int32, (block, block), 0)
    query_index = lax.broadcasted_iota(jnp.int32, (block, block), 1)

    def pair(head, key_rows, query_rows, diagonal):
        query = query_wide[head, query_rows, :]
        scores = dot_nt(key_wide[key_rows, :], query)
        if diagonal:
            scores = jnp.where(key_index <= query_index, scores, blocked)
        probs = jnp.exp2(scores * to_exponent - total_ref[0, head : head + 1, query_rows])
        grad = grad_own[head, query_rows, :]
        grad_probs = dot_nt(rotated_ref[key_rows, 2 * LANES :], grad)
        grad_scores = (probs * (grad_probs - row_dots[head : head + 1, query_rows])).astype(low)
        grad_value[key_rows, :] += dot_nn(probs.astype(low), grad)
        grad_key[key_rows, :] += dot_nn(grad_scores, query[:, :LANES])
        grad_query[:, query_rows] += dot_nn(key_turned[head, :, key_rows], grad_scores)

    for head in range(2):

        def over_keys(key_place, unused, head=head):
            key_rows = pl.ds(pl.multiple_of(key_place * block, block), block)
            pair(head, key_rows, key_rows, True)

            def over_queries(query_place, inner):
                pair(head, key_rows, pl.ds(pl.multiple_of(query_place * block, block), block), False)
                return inner

            return lax.fori_loop(key_place + 1, ctx_count, over_queries, unused)

        lax.fori_loop(0, ctx_count, over_keys, 0)

    sum_ref[...] = jnp.zeros_like(sum_ref)

    def turn(place, unused):
        rows = pl.ds(pl.multiple_of(place * block, block), block)
        query_rows_grad[rows, :] = jnp.transpose(grad_query[:, rows])
        return unused

    lax.fori_loop(0, ctx_count, turn, 0)

    for place in range(ctx_count * tp_count):
        slot, start = place // slot_parts, place % slot_parts * part
        source = pl.ds(pl.multiple_of(order_ref[place] * part, part), part)
        cosine = cos_ref[source, :]
        sine = sin_ref[source, :]
        values = (
            query_rows_grad[source, :] * score_scale,
            grad_key[source, :] * score_scale,
            grad_value[source, :],
        )
        for kind in range(3):
            value = values[kind]
            if kind < 2:
                value = value * cosine - partner(value, lane_part) * sine
            value = value.astype(low)
            out_refs[slot][start : start + part, kind * LANES : (kind + 1) * LANES] = value
            sum_ref[0, kind : kind + 1, :] += jnp.sum(value.astype(full), axis=0, keepdims=True)


def whole(shape):
    return pl.BlockSpec(shape, lambda pair: (0,) * len(shape))


def attend(order, normed, weight, bias, tables, ctx_count, tp_count):
    slots = len(normed)
    slot_rows, features = normed[0].shape
    rows = slots * slot_rows
    pairs = bias.shape[0]
    width = pairs * 3 * LANES
    trio = pl.BlockSpec((rows, 3 * LANES), lambda pair: (0, pair))
    single = pl.BlockSpec((rows, LANES), lambda pair: (0, pair))
    slot_single = pl.BlockSpec((slot_rows, LANES), lambda pair: (0, pair))
    results = pl.pallas_call(
        functools.partial(attend_kernel, ctx_count, tp_count, slots),
        grid=(pairs,),
        in_specs=[pl.BlockSpec(memory_space=pltpu.SMEM)]
        + [whole((slot_rows, features))] * slots
        + [pl.BlockSpec((features, 3 * LANES), lambda pair: (0, pair))]
        + [pl.BlockSpec((1, 3, LANES), lambda pair: (pair, 0, 0))]
        + [whole(table.shape) for table in tables],
        out_specs=[slot_single] * slots
        + [
            single,
            pl.BlockSpec((1, 8, rows), lambda pair: (pair, 0, 0)),
            trio,
        ],
        out_shape=[jax.ShapeDtypeStruct((slot_rows, pairs * LANES), low)] * slots
        + [
            jax.ShapeDtypeStruct((rows, pairs * LANES), full),
            jax.ShapeDtypeStruct((pairs, 8, rows), full),
            jax.ShapeDtypeStruct((rows, width), low),
        ],
        scratch_shapes=[pltpu.VMEM((rows, 2 * LANES), low)],
        compiler_params=pltpu.CompilerParams(vmem_limit_bytes=52 * 2**20),
        cost_estimate=pl.CostEstimate(flops=0, bytes_accessed=0, transcendentals=0),
        name="attend",
    )(order, *normed, weight, bias, *tables)
    return (results[:slots], *results[slots:])


def attend_back(order, rotated, grads, fine, totals, tables, ctx_count, tp_count):
    slots = len(grads)
    rows, width = rotated.shape
    slot_rows = rows // slots
    pairs = width // (3 * LANES)
    trio = pl.BlockSpec((rows, 3 * LANES), lambda pair: (0, pair))
    single = pl.BlockSpec((rows, LANES), lambda pair: (0, pair))
    slot_trio = pl.BlockSpec((slot_rows, 3 * LANES), lambda pair: (0, pair))
    slot_single = pl.BlockSpec((slot_rows, LANES), lambda pair: (0, pair))
    results = pl.pallas_call(
        functools.partial(attend_back_kernel, ctx_count, tp_count, slots),
        grid=(pairs,),
        in_specs=[pl.BlockSpec(memory_space=pltpu.SMEM), trio]
        + [slot_single] * slots
        + [single, pl.BlockSpec((1, 8, rows), lambda pair: (pair, 0, 0))]
        + [whole(table.shape) for table in tables],
        out_specs=[slot_trio] * slots + [pl.BlockSpec((1, 8, LANES), lambda pair: (pair, 0, 0))],
        out_shape=[jax.ShapeDtypeStruct((slot_rows, width), low)] * slots
        + [jax.ShapeDtypeStruct((pairs, 8, LANES), full)],
        scratch_shapes=[
            pltpu.VMEM((2, rows, 2 * LANES), low),
            pltpu.VMEM((rows, 2 * LANES), low),
            pltpu.VMEM((2, LANES, rows), low),
            pltpu.VMEM((2, rows, LANES), low),
            pltpu.VMEM((8, rows), full),
            pltpu.VMEM((LANES, rows), full),
            pltpu.VMEM((rows, LANES), full),
            pltpu.VMEM((rows, LANES), full),
            pltpu.VMEM((rows, LANES), full),
        ],
        compiler_params=pltpu.CompilerParams(vmem_limit_bytes=52 * 2**20),
        cost_estimate=pl.CostEstimate(flops=0, bytes_accessed=0, transcendentals=0),
        name="attend_back",
    )(order, rotated, *grads, fine, totals, *tables)
    return (results[:slots], results[slots])


def cut_kernel(ctx_count, with_heads, ctx_ref, *refs):
    gate_up_ref, down_ref, sent_ref = refs[-3:]
    units = down_ref.shape[1] // ctx_count
    for kind in range(3):
        weight = down_ref[...] if kind == 2 else gate_up_ref[kind]
        turned = jnp.transpose(weight.astype(full)).astype(low)
        for place in range(ctx_count):
            sent_ref[ctx_ref[0] ^ place, kind * units : (kind + 1) * units, :] = turned[
                place * units : (place + 1) * units
            ]
    if not with_heads:
        return
    qkv_ref, out_weight_ref = refs[:2]
    width = out_weight_ref.shape[1] // ctx_count
    for place in range(ctx_count):
        start = 3 * units
        for kinds in (range(3), (None,)):
            for pair in range(width // LANES):
                columns = slice(place * width + pair * LANES, place * width + (pair + 1) * LANES)
                for kind in kinds:
                    tile = (
                        out_weight_ref[:, columns] if kind is None else qkv_ref[kind, :, columns]
                    )
                    sent_ref[ctx_ref[0] ^ place, start : start + LANES, :] = tile
                    start += LANES


def join_kernel(ctx_count, unit_outs, ctx_ref, *refs):
    parts, outs = refs[:ctx_count], refs[ctx_count:]
    for step in range(ctx_count):
        place = pl.ds(pl.multiple_of((ctx_ref[0] ^ step) * LANES, LANES), LANES)
        start = 0
        for out in outs[:unit_outs]:
            out[:, place] = parts[step][start : start + out.shape[0], :]
            start += out.shape[0]
        for out in outs[unit_outs:]:
            for tile in range(out.shape[1] // LANES):
                out[place, tile * LANES : (tile + 1) * LANES] = parts[step][
                    start : start + LANES, :
                ]
                start += LANES


def join_units_kernel(ctx_count, ctx_ref, *refs):
    parts, (gate_up_ref, down_ref, held) = refs[:ctx_count], refs[-3:]
    units = down_ref.shape[2] // ctx_count
    for kind in range(3):
        for step in range(ctx_count):
            rows = pl.ds(pl.multiple_of((ctx_ref[0] ^ step) * units, 16), units)
            held[rows, :] = parts[step][kind * units : (kind + 1) * units, :]
        turned = jnp.transpose(held[...].astype(full))
        if kind == 2:
            down_ref[0] = turned
        else:
            gate_up_ref[0, :, kind, :] = turned


def join_heads_kernel(ctx_count, ctx_ref, *refs):
    parts, (qkv_ref, out_ref) = refs[:ctx_count], refs[-2:]
    width = out_ref.shape[2] // ctx_count
    for step in range(ctx_count):
        place = (ctx_ref[0] ^ step) * width
        start = parts[step].shape[0] - 4 * width
        for kinds in (range(3), (None,)):
            for pair in range(width // LANES):
                columns = pl.ds(pl.multiple_of(place + pair * LANES, LANES), LANES)
                for kind in kinds:
                    tile = jnp.transpose(parts[step][start : start + LANES, :].astype(full))
                    if kind is None:
                        out_ref[0, :, columns] = tile
                    else:
                        qkv_ref[0, kind, :, columns] = tile
                    start += LANES


def weight_grad_kernel(piece_counts, *refs):
    count = sum(piece_counts)
    lefts, rights, (out_ref, turned_ref) = refs[:count], refs[count : 2 * count], refs[2 * count :]
    rows = lefts[0].shape[0]

    @pl.when(pl.program_id(0) == 0)
    def turn():
        start = first = 0
        for pieces in piece_counts:
            width = lefts[first].shape[1]
            for piece in range(pieces):
                turned = jnp.transpose(lefts[first + piece][...].astype(full)).astype(low)
                turned_ref[start : start + width, piece * rows : (piece + 1) * rows] = turned
            first += pieces
            start += width

    start = first = 0
    for pieces in piece_counts:
        width = lefts[first].shape[1]
        total = None
        for piece in range(pieces):
            product = dot_nn(
                turned_ref[start : start + width, piece * rows : (piece + 1) * rows],
                rights[first + piece][...],
            )
            total = product if total is None else total + product
        out_ref[start : start + width, :] = total.astype(low)
        first += pieces
        start += width


def weight_grads(groups, columns_all=None, start=0, earlier=None):
    lefts = [left for group_lefts, unused in groups for left in group_lefts]
    rights = [right for unused, group_rights in groups for right in group_rights]
    columns = sum(group_lefts[0].shape[1] for group_lefts, unused in groups)
    rows, features = rights[0].shape
    pieces = [len(group_lefts) for group_lefts, unused in groups]
    block = 512
    kept = [] if earlier is None else [earlier]

    def kernel(*refs):
        weight_grad_kernel(pieces, *refs[: 2 * sum(pieces)], *refs[-2:])

    return pl.pallas_call(
        kernel,
        grid=(features // block,),
        in_specs=[pl.BlockSpec(left.shape, lambda i: (0, 0)) for left in lefts]
        + [pl.BlockSpec((rows, block), lambda i: (0, i)) for right in rights]
        + [pl.BlockSpec(memory_space=pl.ANY)] * len(kept),
        out_specs=pl.BlockSpec((columns, block), lambda i: (start // columns, i)),
        out_shape=jax.ShapeDtypeStruct((columns_all or columns, features), low),
        input_output_aliases={2 * sum(pieces): 0} if kept else {},
        scratch_shapes=[pltpu.VMEM((columns, max(pieces) * rows), low)],
        compiler_params=pltpu.CompilerParams(vmem_limit_bytes=56 * 2**20),
        cost_estimate=pl.CostEstimate(
            flops=2 * columns * features * max(pieces) * rows,
            bytes_accessed=columns * features * 4,
            transcendentals=0,
        ),
        name="weight_grads",
    )(*lefts, *rights, *kept)


def start_copies(pairs, sems):
    copies = [
        pltpu.make_async_copy(source, target, sems.at[i])
        for i, (source, target) in enumerate(pairs)
    ]
    for copy in copies:
        copy.start()
    return copies


def weight_pairs(weights_hbm, held_refs):
    units = held_refs[0].shape[0]
    return [
        (weights_hbm.at[i * units : (i + 1) * units, :], held) for i, held in enumerate(held_refs)
    ]


def units_kernel(
    mine_in,
    other_in,
    weights_hbm,
    mine_out,
    other_out,
    mine_gate,
    other_gate,
    mine_up,
    other_up,
    mine_units,
    other_units,
    rows_in,
    gate_w,
    up_w,
    down_w,
    sems,
):
    rows = other_out.shape[0]
    copies = start_copies(
        [(other_in, rows_in.at[:rows, :]), (mine_in, rows_in.at[rows:, :])]
        + weight_pairs(weights_hbm, (gate_w, up_w, down_w)),
        sems,
    )
    copies[0].wait()
    copies[1].wait()
    copies[2].wait()
    gate = dot_nt(rows_in[...], gate_w[...])
    other_gate[...] = gate[:rows]
    mine_gate[...] = gate[rows:]
    copies[3].wait()
    up = dot_nt(rows_in[...], up_w[...])
    other_up[...] = up[:rows]
    mine_up[...] = up[rows:]
    units = (gate / (1.0 + jnp.exp(-gate)) * up).astype(low)
    other_units[...] = units[:rows]
    mine_units[...] = units[rows:]
    copies[4].wait()
    out = dot_nn(units, down_w[...])
    other_out[...] = out[:rows].astype(low)
    mine_out[...] = out[rows:]


def last_units_kernel(
    mine_in,
    other_in,
    mine_grad,
    other_grad,
    weights_hbm,
    mine_out,
    other_out,
    mine_gate,
    other_gate,
    mine_up,
    other_up,
    mine_units,
    other_units,
    rows_in,
    gate_w,
    up_w,
    down_w,
    grad_in,
    sems,
):
    rows = other_out.shape[0]
    copies = start_copies(
        [(other_in, rows_in.at[:rows, :]), (mine_in, rows_in.at[rows:, :])]
        + weight_pairs(weights_hbm, (gate_w, up_w, down_w))
        + [(other_grad, grad_in.at[:rows, :]), (mine_grad, grad_in.at[rows:, :])],
        sems,
    )
    copies[0].wait()
    copies[1].wait()
    copies[2].wait()
    gate = dot_nt(rows_in[...], gate_w[...])
    sigmoid = 1.0 / (1.0 + jnp.exp(-gate))
    copies[3].wait()
    up = dot_nt(rows_in[...], up_w[...])
    copies[4].wait()
    copies[5].wait()
    copies[6].wait()
    grad = dot_nt(grad_in[...], down_w[...])
    silu = gate * sigmoid
    units = (silu * up).astype(low)
    grad_up = (grad * silu).astype(low)
    grad_gate = (grad * up * (sigmoid * (1.0 + gate * (1.0 - sigmoid)))).astype(low)
    other_units[...] = units[:rows]
    mine_units[...] = units[rows:]
    other_up[...] = grad_up[:rows]
    mine_up[...] = grad_up[rows:]
    other_gate[...] = grad_gate[:rows]
    mine_gate[...] = grad_gate[rows:]
    out = dot_nn(grad_gate, gate_w[...]) + dot_nn(grad_up, up_w[...])
    other_out[...] = out[:rows].astype(low)
    mine_out[...] = out[rows:]


def units_call(kernel, pieces, weights):
    rows, features = pieces[0].shape
    units = weights.shape[0] // 3
    inside = pl.BlockSpec(memory_space=pltpu.VMEM)
    outside = pl.BlockSpec(memory_space=pl.ANY)
    kept = full if len(pieces) == 2 else low
    out_shape = (
        [jax.ShapeDtypeStruct((rows, features), kind) for kind in (full, low)]
        + [jax.ShapeDtypeStruct((rows, units), kept)] * 4
        + [jax.ShapeDtypeStruct((rows, units), low)] * 2
    )
    held = pltpu.VMEM((2 * rows, features), low)
    done = pl.pallas_call(
        kernel,
        in_specs=[outside] * (len(pieces) + 1),
        out_specs=[inside] * len(out_shape),
        out_shape=out_shape,
        scratch_shapes=[held]
        + [pltpu.VMEM((units, features), low)] * 3
        + [held] * (len(pieces) // 2 - 1)
        + [pltpu.SemaphoreType.DMA((3 + len(pieces),))],
        compiler_params=pltpu.CompilerParams(vmem_limit_bytes=52 * 2**20),
        cost_estimate=pl.CostEstimate(flops=0, bytes_accessed=0, transcendentals=0),
        name="units",
    )(*pieces, weights)
    return (done[:2], done[2:4], done[4:6], done[6:8])


def local_kernel(kernel, ctx, arrays, out_shape):
    inside = pl.BlockSpec(memory_space=pltpu.VMEM)
    return pl.pallas_call(
        kernel,
        in_specs=[pl.BlockSpec(memory_space=pltpu.SMEM)] + [inside] * len(arrays),
        out_specs=jax.tree.map(lambda unused: inside, out_shape),
        out_shape=out_shape,
        compiler_params=pltpu.CompilerParams(vmem_limit_bytes=40 * 2**20),
        cost_estimate=pl.CostEstimate(flops=0, bytes_accessed=0, transcendentals=0),
    )(ctx.reshape(1).astype(jnp.int32), *arrays)


def stacked_kernel(kernel, ctx, arrays, layer, layer_total, shapes, earlier, scratch=()):
    inside = pl.BlockSpec(memory_space=pltpu.VMEM)
    earlier = [] if earlier is None else list(earlier)
    return pl.pallas_call(
        kernel,
        grid=(1,),
        in_specs=[pl.BlockSpec(memory_space=pltpu.SMEM)]
        + [inside] * len(arrays)
        + [pl.BlockSpec(memory_space=pl.ANY)] * len(earlier),
        out_specs=[
            pl.BlockSpec((1,) + shape, lambda i, rank=len(shape): (layer,) + (0,) * rank)
            for shape in shapes
        ],
        out_shape=[jax.ShapeDtypeStruct((layer_total,) + shape, full) for shape in shapes],
        input_output_aliases={1 + len(arrays) + i: i for i in range(len(earlier))},
        scratch_shapes=list(scratch),
        compiler_params=pltpu.CompilerParams(vmem_limit_bytes=40 * 2**20),
        cost_estimate=pl.CostEstimate(flops=0, bytes_accessed=0, transcendentals=0),
    )(ctx.reshape(1).astype(jnp.int32), *arrays, *earlier)


def tied(first, second):
    return lax.optimization_barrier((first, second))


class Group:
    def __init__(self, width, hidden_width, depth, rows):
        self.ctx_count = lax.axis_size("ctx")
        self.tp_count = lax.axis_size("tp")
        self.shard_count = lax.axis_size("shard")
        self.ctx = lax.axis_index("ctx")
        self.tp = lax.axis_index("tp")
        self.paired = (
            self.ctx_count == 4
            and self.shard_count in (2, 4)
            and self.tp_count == 2
            and width % LANES == 0
            and hidden_width % 16 == 0
            and depth == LANES
            and rows % 32 == 0
        )

    def order(self):
        places = jnp.arange(self.ctx_count * self.tp_count, dtype=jnp.int32)
        if not self.paired:
            return places
        away = (places // self.tp_count) ^ self.ctx
        return away * self.tp_count + ((places % self.tp_count) ^ self.tp)

    def across(self, value, step):
        return lax.ppermute(value, "ctx", [(i, i ^ step) for i in range(self.ctx_count)])

    def swap(self, value):
        return lax.ppermute(value, "tp", [(0, 1), (1, 0)])

    def send_rows(self, own):
        if not self.paired:
            return [lax.all_gather(own, ("ctx", "tp"), axis=0, tiled=True)]
        return [own, self.across(own, 1), self.across(own, 2)]

    def receive_rows(self, arrived, work):
        if not self.paired:
            return [work((arrived[0],), 0)[0]]
        own, first, second = arrived
        half = own.shape[0] // 2
        far_top = self.across(first[:half], 2)
        far_end = self.across(second[half:], 1)
        results = []
        behind = None
        for step in range(4):
            here = (own, first, second, None)[step]
            if step == 3:
                here = jnp.concatenate([far_top, far_end], axis=0)
            if behind is not None:
                here = tied(here, behind)[0]
            done, behind = work((here, self.swap(here)), step)
            results.append(done)
        return results

    def receive_pieces(self, arrived):
        slots = self.receive_rows(arrived, lambda pieces, slot: (pieces, None))
        return [piece for pieces in slots for piece in pieces]

    def gather_direct(self, own):
        if not self.paired:
            return self.send_rows(own)
        slots = [self.across(own, step) if step else own for step in range(4)]
        return [piece for here in slots for piece in (here, self.swap(here))]

    def chip_sums(self, pieces):
        if not self.paired:
            return pieces
        return [
            mine + self.swap(other.astype(low)).astype(full)
            for mine, other in zip(pieces[::2], pieces[1::2])
        ]

    def reduce_rows(self, sums, first_fill=None, second_fill=None):
        if not self.paired:
            return lax.psum_scatter(
                sums[0].astype(low), ("ctx", "tp"), scatter_dimension=0, tiled=True
            ).astype(full)
        own, first, second, far = sums
        half = own.shape[0] // 2
        far = far.astype(low)
        early = [
            self.across(far[:half], 1),
            self.across(far[half:], 2),
            self.across(first[:half].astype(low), 1),
            self.across(second[half:].astype(low), 2),
        ]
        if first_fill is not None:
            early, first_fill = tied(early, first_fill)
        far_top, far_end, first_top, second_end = [part.astype(full) for part in early]
        late = [(second[:half] + far_top).astype(low), (first[half:] + far_end).astype(low)]
        if second_fill is not None:
            late, first_fill = tied(late, first_fill)
        late = [self.across(late[0], 2), self.across(late[1], 1)]
        if second_fill is not None:
            fill = second_fill(first_fill)
            late, fill = tied(late, fill)
        second_top, first_end = [part.astype(full) for part in late]
        result = own + jnp.concatenate([first_top + second_top, first_end + second_end], axis=0)
        return result if second_fill is None else (result, fill)

    def send_sums(self, sums):
        if not self.paired:
            return sums
        return [sums[0]] + [self.across(sums[step].astype(low), step) for step in range(1, 4)]

    def add_sums(self, arrived):
        if not self.paired:
            return self.reduce_rows(arrived)
        return sum([part.astype(full) for part in arrived[1:]], arrived[0])

    def both_halves(self, value):
        if not self.paired:
            return lax.all_gather(value, "tp", axis=0, tiled=True)
        other = self.swap(value)
        return jnp.where(
            self.tp == 0,
            jnp.concatenate([value, other], axis=0),
            jnp.concatenate([other, value], axis=0),
        )

    def exchange(self, value, axis, count):
        parts = [value] + [
            lax.ppermute(value, axis, [(i, i ^ step) for i in range(count)])
            for step in range(1, count)
        ]
        while len(parts) > 1:
            parts = [left + right for left, right in zip(parts[::2], parts[1::2])]
        return parts[0]

    def total(self, norms, biases):
        if not self.paired:
            return (lax.psum(norms, ("shard", "ctx", "tp")), lax.psum(biases, ("shard", "ctx")))
        flat = self.exchange(norms.reshape(-1, LANES), "tp", self.tp_count)
        count = flat.shape[0]
        flat = jnp.concatenate([flat, biases.reshape(-1, LANES)], axis=0)
        flat = self.exchange(flat, "ctx", self.ctx_count)
        flat = self.exchange(flat, "shard", self.shard_count)
        return (flat[:count].reshape(norms.shape), flat[count:].reshape(biases.shape))


    def send_heads(self, qkv, out):
        size = out.shape[1] // self.ctx_count
        parts = []
        for step in range(self.ctx_count):
            start = (self.ctx ^ step) * size
            piece = jnp.concatenate(
                [
                    pair_columns(lax.dynamic_slice_in_dim(qkv, start, size, 2)),
                    lax.dynamic_slice_in_dim(out, start, size, 1),
                ],
                axis=1,
            )
            piece = jnp.moveaxis(piece.reshape(LANES, -1, LANES), 1, 0).reshape(-1, LANES)
            parts.append(self.across(piece, step) if step else piece)
        return parts

    def cut_layer(self, heads, gate_up, down):
        arrays = [jnp.moveaxis(gate_up, 1, 0), down]
        rows = 3 * down.shape[1] // self.ctx_count
        if heads is not None:
            qkv, out = heads
            arrays = [jnp.moveaxis(qkv, 1, 0), out] + arrays
            rows += 4 * out.shape[1] // self.ctx_count
        return local_kernel(
            functools.partial(cut_kernel, self.ctx_count, heads is not None),
            self.ctx,
            arrays,
            jax.ShapeDtypeStruct((self.ctx_count, rows, LANES), low),
        )

    def send_cut(self, cut):
        return [self.across(cut[k], k) if k else cut[k] for k in range(self.ctx_count)]

    def join_parts(self, parts, units, columns):
        features = LANES * self.ctx_count
        return local_kernel(
            functools.partial(join_kernel, self.ctx_count, len(units)),
            self.ctx,
            parts,
            [jax.ShapeDtypeStruct((size, features), low) for size in units]
            + [jax.ShapeDtypeStruct((features, size), low) for size in columns],
        )

    def split_send(self, value):
        if not self.paired:
            return [value]
        parts = []
        for step in range(self.ctx_count):
            piece = lax.dynamic_slice_in_dim(value, (self.ctx ^ step) * LANES, LANES, 1)
            parts.append(self.across(piece, step) if step else piece)
        return parts

    def join_units(self, parts, tp_units, layer, layer_total, earlier):
        units = tp_units // self.ctx_count
        if not self.paired:
            gate_up = parts[0][: 2 * units].reshape(2, units, -1)
            gate_up = self.spread(gate_up, 2, 1)
            down = self.spread(parts[0][2 * units : 3 * units], 1, 0)
            values = (jnp.transpose(gate_up, (2, 0, 1)), jnp.transpose(down))
            return self.stack_layer(values, layer, layer_total, earlier)
        return stacked_kernel(
            functools.partial(join_units_kernel, self.ctx_count),
            self.ctx,
            parts,
            layer,
            layer_total,
            [(LANES, 2, tp_units), (LANES, tp_units)],
            earlier,
            [pltpu.VMEM((tp_units, LANES), low)],
        )

    def join_heads(self, parts, width, layer, layer_total, earlier):
        if not self.paired:
            columns = 4 * (-(-width // LANES) * LANES)
            qkv = unpair_columns(parts[0][-columns : -columns // 4].T, width)
            out = parts[0][-columns // 4 :].T[:, :width]
            values = (jnp.swapaxes(self.spread(qkv, 0, 2), 0, 1), self.spread(out, 0, 1))
            return self.stack_layer(values, layer, layer_total, earlier)
        tp_width = width * self.ctx_count
        return stacked_kernel(
            functools.partial(join_heads_kernel, self.ctx_count),
            self.ctx,
            parts,
            layer,
            layer_total,
            [(3, LANES, tp_width), (LANES, tp_width)],
            earlier,
        )


    def stack_layer(self, values, layer, layer_total, earlier):
        if earlier is None:
            earlier = [jnp.zeros((layer_total,) + value.shape, full) for value in values]
        return [stack.at[layer].set(value.astype(full)) for stack, value in zip(earlier, values)]

    def spread(self, value, split_axis, join_axis):
        return lax.all_to_all(value, "ctx", split_axis, join_axis, tiled=True)

    def spread_layer(self, qkv, out, gate_up, down):
        gate_up = self.spread(jnp.transpose(gate_up, (1, 2, 0)), 1, 2)
        return (
            over_shard(pair_columns(self.spread(qkv, 2, 0)), 0),
            over_shard(pad_columns(self.spread(out, 1, 0)), 0),
            over_shard(gate_up.reshape(-1, gate_up.shape[2]), 1),
            over_shard(self.spread(jnp.transpose(down), 0, 1), 1),
        )


def pair_columns(weight):
    width = weight.shape[-1]
    pairs = -(-width // LANES)
    if pairs * LANES != width:
        weight = jnp.pad(weight, [(0, 0)] * (weight.ndim - 1) + [(0, pairs * LANES - width)])
    lead = weight.shape[:-2]
    weight = weight.reshape(lead + (3, pairs, LANES))
    return jnp.moveaxis(weight, -2, -3).reshape(lead + (pairs * 3 * LANES,))


def unpair_columns(value, width):
    lead = value.shape[:-1]
    pairs = value.shape[-1] // (3 * LANES)
    value = jnp.moveaxis(value.reshape(lead + (pairs, 3, LANES)), -3, -2)
    return value.reshape(lead + (3, pairs * LANES))[..., :width]


def pad_columns(weight):
    width = weight.shape[-1]
    filled = -(-width // LANES) * LANES
    return weight if filled == width else jnp.pad(weight, [(0, 0), (0, filled - width)])


def sum_dots(groups):
    return jnp.concatenate([dot_tn(lefts[0], rights[0]) for lefts, rights in groups]).astype(low)


def flat_pieces(slots_done):
    return [[piece for pieces in kind for piece in pieces] for kind in zip(*slots_done)]


def unit_grads(rows_in, gate, up, weights):
    gate_weight, up_weight, down = weights
    grad_hidden = dot_nt(rows_in, down)
    sigmoid = jax.nn.sigmoid(gate)
    grad_gate = (grad_hidden * up * (sigmoid * (1.0 + gate * (1.0 - sigmoid)))).astype(low)
    grad_up = (grad_hidden * (gate * sigmoid)).astype(low)
    return (grad_gate, grad_up, dot_nn(grad_gate, gate_weight) + dot_nn(grad_up, up_weight))


def over_shard(value, axis):
    return lax.all_gather(value, "shard", axis=axis, tiled=True)


def sum_shard(value, axis):
    return lax.psum_scatter(value, "shard", scatter_dimension=axis, tiled=True)


def body(
    tokens,
    cotangent,
    lengths,
    norm_gain,
    norm_bias,
    input_bias,
    input_projection,
    output_projection,
    gate_up_weight,
    down_weight,
):
    held_rows = tokens.shape[0]
    layer_total = input_projection.shape[0]
    tp_width = input_bias.shape[2]
    ctx_count, tp_count = lax.axis_size("ctx"), lax.axis_size("tp")
    width = tp_width // ctx_count
    hidden_width = down_weight.shape[2] // ctx_count
    rows = held_rows // tp_count
    group = Group(width, hidden_width, input_projection.shape[1], rows)
    seq_ids, length, offset = row_meta(lengths[0], held_rows)
    positions = (
        jnp.arange(ctx_count, dtype=jnp.int32)[:, None] * length[None, :] + offset[None, :]
    ).reshape(-1)
    lane = jnp.arange(LANES, dtype=jnp.int32)[None, :]
    same = lane == seq_ids[:, None]
    named = lane < lengths.shape[1]
    query_mark = jnp.where(named & ~same, blocked, 0.0).astype(low)
    key_mark = jnp.where(same, 1.0, 0.0).astype(low)
    tables = wide_rotary_tables(positions) + (query_mark, key_mark)
    order = group.order()
    bias_own = lax.dynamic_slice_in_dim(input_bias, group.ctx * width, width, 2)
    bias_pairs = pair_columns(bias_own).reshape(layer_total, -1, 3, LANES)

    def own_rows(value):
        return lax.dynamic_slice_in_dim(value, group.tp * rows, rows, 0)

    def sources(index):
        return (
            input_projection[index],
            output_projection[index],
            gate_up_weight[index],
            down_weight[index],
        )

    def norm_one(index, stream):
        scaled, inverse, normed = norm_parts(stream, norm_gain[index, 0], norm_bias[index, 0])
        return (scaled, inverse, group.send_rows(normed.astype(low)))

    stream = own_rows(tokens).astype(full)
    qkv_columns = 3 * width

    def split_heads(heads_full):
        return (heads_full, heads_full[:, qkv_columns:])

    def split_units(units_full):
        return (
            units_full[:hidden_width],
            units_full[hidden_width : 2 * hidden_width],
            units_full[2 * hidden_width :],
        )

    if group.paired:
        (heads_part,) = group.join_parts(
            group.send_heads(*sources(0)[:2]), [], [qkv_columns + width]
        )
        heads_full = over_shard(heads_part, 0)
        first_norm = norm_one(0, stream)
        cut = tied(group.cut_layer(None, *sources(0)[2:]), first_norm[2])[0]
        (units_part,) = group.join_parts(group.send_cut(cut), [3 * hidden_width], [])
        weights = [split_heads(heads_full) + (over_shard(units_part, 1),)]
    else:
        first_norm = norm_one(0, stream)
        weights = []
        for index in range(layer_total):
            qkv_full, out_full, gate_up_full, down_full = group.spread_layer(*sources(index))
            weights.append(
                (qkv_full, out_full)
                + (jnp.concatenate([gate_up_full, down_full], axis=0),)
            )

    saved = []
    last_branch = None
    for index in range(layer_total):
        last = index + 1 == layer_total
        qkv_weight, out_weight, units_full = weights[index]
        gate_weight, up_weight, down = split_units(units_full)
        scaled_one, inverse_one, arrived = norm_one(index, stream) if index else first_norm
        normed_one = group.receive_pieces(arrived)
        travel = None
        if group.paired and not last:
            travel = group.send_cut(
                tied(
                    group.cut_layer(sources(index + 1)[:2], *sources(index + 1)[2:]), normed_one
                )[0]
            )
        heads, fine, totals, rotated = attend(
            order, normed_one, qkv_weight, bias_pairs[index], tables, ctx_count, tp_count
        )
        if travel is not None:
            heads, travel = tied(heads, travel)
        if group.paired and not last:
            units_part, heads_part = group.join_parts(
                travel, [3 * hidden_width], [qkv_columns + width]
            )
            heads = tied(heads, (units_part, heads_part))[0]
            weights.append(
                split_heads(over_shard(heads_part, 0)) + (over_shard(units_part, 1),)
            )
        attention = group.reduce_rows(
            group.chip_sums([dot_nt(rows_in, out_weight) for rows_in in heads])
        )
        middle = stream + attention
        scaled_two, inverse_two, normed_two = norm_parts(
            middle, norm_gain[index, 1], norm_bias[index, 1]
        )

        def forward_units(pieces, slot):
            if group.paired:
                feeds, gates, ups, hidden = units_call(units_kernel, pieces, units_full)
                return ((pieces, gates, ups, hidden, feeds), feeds)
            gates = [dot_nt(rows_in, gate_weight) for rows_in in pieces]
            ups = [dot_nt(rows_in, up_weight) for rows_in in pieces]
            hidden = [(jax.nn.silu(gate) * up).astype(low) for gate, up in zip(gates, ups)]
            feeds = [dot_nn(units, down) for units in hidden]
            return ((pieces, gates, ups, hidden, feeds), hidden)

        def last_units(pieces, slot):
            size = len(pieces)
            grads = last_branch[slot * size : (slot + 1) * size]
            if group.paired:
                partials, grad_gates, grad_ups, hidden = units_call(
                    last_units_kernel, (*pieces, *grads), units_full
                )
                return ((pieces, grad_gates, grad_ups, hidden, partials), partials)
            gate, up = dot_nt(pieces[0], gate_weight), dot_nt(pieces[0], up_weight)
            hidden = (jax.nn.silu(gate) * up).astype(low)
            grad_gate, grad_up, partial = unit_grads(
                grads[0], gate, up, (gate_weight, up_weight, down)
            )
            return ((pieces, [grad_gate], [grad_up], [hidden], [partial]), None)

        arrived = group.send_rows(normed_two.astype(low))
        if last:
            if last_branch is None:
                last_branch = group.receive_pieces(group.send_rows(own_rows(cotangent)))
            slots_done = group.receive_rows(arrived, last_units)
            normed_two, gates, ups, hidden, last_partials = flat_pieces(slots_done)
        else:
            pieces = lax.optimization_barrier(group.receive_pieces(arrived))
            if index + 2 == layer_total:
                last_branch = group.gather_direct(tied(own_rows(cotangent), pieces)[0])
            size = len(pieces) // (4 if group.paired else 1)
            slots_done = [
                forward_units(pieces[i : i + size], i // size)[0]
                for i in range(0, len(pieces), size)
            ]
            normed_two, gates, ups, hidden, feeds = flat_pieces(slots_done)
            feeds = group.chip_sums(feeds)
            if index + 2 == layer_total:
                feeds, last_branch = tied(feeds, last_branch)
            if group.paired:
                feeds = tied(feeds, weights[index + 1][0])[0]
            stream = middle + group.reduce_rows(feeds)
        saved.append(
            (
                scaled_one,
                inverse_one,
                normed_one,
                heads,
                fine,
                totals,
                rotated,
                scaled_two,
                inverse_two,
                normed_two,
                gates,
                ups,
                hidden,
            )
        )

    grad_stream = own_rows(cotangent).astype(full)
    norm_list = [None] * layer_total
    input_bias_list = [None] * layer_total
    head_stacks = None
    unit_stacks = None
    waiting = None
    for index in reversed(range(layer_total)):
        last = index + 1 == layer_total
        (
            scaled_one,
            inverse_one,
            normed_one,
            heads,
            fine,
            totals,
            rotated,
            scaled_two,
            inverse_two,
            normed_two,
            gates,
            ups,
            hidden,
        ) = saved[index]
        qkv_weight, out_weight, units_full = weights[index]
        gate_weight, up_weight, down = split_units(units_full)


        def backward_units(pieces, slot):
            grad_gates, grad_ups, partials = [], [], []
            for place, rows_in in enumerate(pieces, slot * len(pieces)):
                grad_gate, grad_up, partial = unit_grads(
                    rows_in, gates[place], ups[place], (gate_weight, up_weight, down)
                )
                grad_gates.append(grad_gate)
                grad_ups.append(grad_up)
                partials.append(partial)
            return ((pieces, grad_gates, grad_ups, partials), (grad_gates, grad_ups))

        if last:
            branch, grad_gates, grad_ups, partials = last_branch, gates, ups, last_partials
        else:
            slots_done = group.receive_rows(
                group.send_rows(grad_stream.astype(low)), backward_units
            )
            branch, grad_gates, grad_ups, partials = flat_pieces(slots_done)
        sums = group.chip_sums(partials)
        (branch, grad_gates, grad_ups, hidden), unused = tied(
            (branch, grad_gates, grad_ups, hidden), sums
        )
        if group.paired:
            down_grad = weight_grads([(hidden, branch)], 3 * hidden_width, 2 * hidden_width)
            grad_normed_two, units_grad = group.reduce_rows(
                sums,
                down_grad,
                lambda earlier: weight_grads(
                    [(grad_gates, normed_two), (grad_ups, normed_two)],
                    3 * hidden_width,
                    0,
                    earlier,
                ),
            )
        else:
            units_grad = sum_dots(
                [(grad_gates, normed_two), (grad_ups, normed_two), (hidden, branch)]
            )
            grad_normed_two = group.reduce_rows(sums)
        units_part = sum_shard(units_grad, 1)
        if last:
            feeds = group.chip_sums([dot_nn(units, down) for units in hidden])
        grad_input_two, gain_two, bias_two = norm_back(
            grad_normed_two, scaled_two, inverse_two, norm_gain[index, 1]
        )
        grad_middle = grad_stream + grad_input_two
        branch = group.receive_pieces(group.send_rows(grad_middle.astype(low)))
        grad_heads = [dot_nn(rows_in, out_weight).astype(low) for rows_in in branch]
        if last:
            travel = group.send_sums(tied(feeds, grad_heads)[0])
        else:
            travel = group.split_send(tied(waiting, grad_heads)[0])
        grad_qkv, bias_sums = attend_back(
            order, rotated, grad_heads, fine, totals, tables, ctx_count, tp_count
        )
        grad_qkv, travel, branch = lax.optimization_barrier((grad_qkv, travel, branch))
        if last:
            result = (middle + group.add_sums(travel)).astype(low)
        else:
            unit_stacks = group.join_units(
                travel, hidden_width * ctx_count, index + 1, layer_total, unit_stacks
            )
            head_stacks = group.join_heads(travel, width, index + 1, layer_total, head_stacks)
        sums = group.chip_sums(
            [dot_nt(rows_in, qkv_weight[:, : rows_in.shape[1]]) for rows_in in grad_qkv]
        )
        if group.paired:
            grad_normed_one, heads_grad = group.reduce_rows(
                sums,
                (grad_qkv, branch),
                lambda held: weight_grads([(held[0], normed_one), (heads, held[1])]),
            )
        else:
            heads_grad = sum_dots([(grad_qkv, normed_one), (heads, branch)])
            grad_normed_one = group.reduce_rows(sums)
        grad_normed_one = tied(grad_normed_one, units_part)[0]
        heads_part = sum_shard(heads_grad, 1)
        if index:
            waiting = jnp.concatenate([units_part, heads_part], axis=0)
        bias_sums = bias_sums[:, :3, :].transpose(1, 0, 2).reshape(3, -1)[:, :width]
        input_bias_list[index] = lax.dynamic_update_slice_in_dim(
            jnp.zeros((3, tp_width), full), bias_sums, group.ctx * width, 1
        )
        grad_input_one, gain_one, bias_one = norm_back(
            grad_normed_one, scaled_one, inverse_one, norm_gain[index, 0]
        )
        grad_stream = grad_middle + grad_input_one
        norm_list[index] = jnp.stack([gain_one, gain_two, bias_one, bias_two])
    unit_stacks = group.join_units(
        group.split_send(units_part), hidden_width * ctx_count, 0, layer_total, unit_stacks
    )
    norm_total, bias_total = group.total(jnp.stack(norm_list), jnp.stack(input_bias_list))
    result = group.both_halves(result)
    tokens_grad = group.both_halves(grad_stream)
    heads_part = tied(heads_part, (unit_stacks, norm_total, bias_total, result, tokens_grad))[0]
    head_stacks = group.join_heads(
        group.split_send(heads_part), width, 0, layer_total, head_stacks
    )
    return (
        result,
        tokens_grad,
        norm_total[:, :2],
        norm_total[:, 2:],
        bias_total,
        jnp.moveaxis(head_stacks[0], 1, 2),
        head_stacks[1],
        unit_stacks[0],
        unit_stacks[1],
    )


def solution(mesh):
    in_specs = (
        P(("shard", "ctx"), None),
        P(("shard", "ctx"), None),
        P("shard", None),
        P(),
        P(),
        P(None, None, "tp"),
        P(None, ("shard", "ctx"), None, "tp"),
        P(None, ("shard", "ctx"), "tp"),
        P(None, ("shard", "ctx"), None, "tp"),
        P(None, ("shard", "ctx"), "tp"),
    )
    out_specs = (
        P(("shard", "ctx"), None),
        P(("shard", "ctx"), None),
        P(),
        P(),
        P(None, None, "tp"),
        P(None, ("shard", "ctx"), None, "tp"),
        P(None, ("shard", "ctx"), "tp"),
        P(None, ("shard", "ctx"), None, "tp"),
        P(None, ("shard", "ctx"), "tp"),
    )
    return jax.shard_map(body, mesh=mesh, in_specs=in_specs, out_specs=out_specs, check_vma=False)
```

time: 7030 us -> 1240 us (0.18)
  waiting for transfers between devices: 5690 us -> 441 us
  matrix products: 923 us -> 97.9 us
  Pallas kernels: 0 us -> 395 us
  local copies, waits for them, and re-layouts: 196 us -> 56.7 us
  starting transfers between devices: 4.34 us -> 129 us
  other arithmetic: 177 us -> 91.9 us
    reduce_scatter x12 -> x4, waiting for transfers between devices: 4410 us -> 11.5 us  [sum_shard(): return lax.psum_scatter(value, 'shard', scatter_dimension=axis, tiled=True)]
    all_gather x12 -> x4, waiting for transfers between devices: 1120 us -> 7.33 us  [over_shard(): return lax.all_gather(value, 'shard', axis=axis, tiled=True)]
    dot_general x96 -> x80, matrix products: 923 us -> 97.9 us  [the longest x40 49 us: dot_nt(): lax.dot_general(left, right, (((1,), (1,)), ((), ())), preferred_element_...]
    ppermute x0 -> x167, waiting for transfers between devices: none -> 422 us  [the longest x94 398 us: across(): lax.ppermute(value, 'ctx', [(i, i ^ step) for i in range(self.ctx_count)])]
    pallas_call x0 -> x27, Pallas kernels: none -> 395 us  [the longest x8 109 us: units_call(): pl.pallas_call(kernel, in_specs=[outside] * (len(pieces) + 1), out_specs=...]
    psum x8 -> x0, waiting for transfers between devices: 154 us -> none  [the longest x2 45.6 us: body(): lax.psum(jnp.einsum('th,dh->td', heads_low, out_full, preferred_element_t...]
    ppermute x0 -> x167, starting transfers between devices: none -> 128 us  [the longest x94 106 us: across(): lax.ppermute(value, 'ctx', [(i, i ^ step) for i in range(self.ctx_count)])]
    reduce_sum x10 -> x0, other arithmetic: 78.6 us -> none  [the longest x8 73.7 us: running(): jnp.sum(jnp.exp(scores - new_max[..., None]), axis=-1)]
  transfers between devices with their start and end apart: 32 -> 175, of which waited for: 27 -> 74; matrix products, arithmetic and copies ran while one was open for 10% -> 16% of each run, Pallas kernels for 0% -> 32%
where the time goes in v1:
time: 1240 us; the launch traced here: 1230 us
  waiting for transfers between devices  441 us (36%)
  Pallas kernels  395 us (32%)
  starting transfers between devices  129 us (10%)
  matrix products  97.9 us (8%)
  other arithmetic  91.9 us (7%)
  local copies, waits for them, and re-layouts  56.7 us (5%)
  between operations  19.1 us (2%)
    ppermute x94, waiting for transfers between devices, across(): lax.ppermute(value, 'ctx', [(i, i ^ step) for i in range(self.ctx_count)])  398 us
    pallas_call x8, Pallas kernels, units_call(): pl.pallas_call(kernel, in_specs=[outside] * (len(pieces) + 1), out_specs=...  109 us
    ppermute x94, starting transfers between devices, across(): lax.ppermute(value, 'ctx', [(i, i ^ step) for i in range(self.ctx_count)])  106 us
    pallas_call x6, Pallas kernels, weight_grads(): pl.pallas_call(kernel, grid=(features // block,), in_specs=[pl.BlockSpec(...  94.3 us
    pallas_call x2, Pallas kernels, attend_back(): pl.pallas_call(functools.partial(attend_back_kernel, ctx_count, tp_count,...  88.7 us
    pallas_call x2, Pallas kernels, attend(): pl.pallas_call(functools.partial(attend_kernel, ctx_count, tp_count, slot...  85.7 us
    dot_general x40, matrix products, dot_nt(): lax.dot_general(left, right, (((1,), (1,)), ((), ())), preferred_element_...  49 us
    dot_general x40, matrix products, dot_nn(): lax.dot_general(left, right, (((1,), (0,)), ((), ())), preferred_element_...  48.9 us
  transfers between devices with their start and end apart: 175, of which 74 were waited for; matrix products, arithmetic and copies ran while one was open for 16% of the time, Pallas kernels for 32%

profile of v1, /device:TPU:8, one launch (start us, length us, event | category | flops | bytes accessed | tf_op | source)
XLA Modules:
  0.0 1230.7 jit_solution(13549790860333024779)
XLA Ops:
  35.8 17.7 %collective-permute-done.1.refs_2_.refs_18_ = bf16[256,2048]{1,0:T(8,128)(2,1)S(1)} collective-permute-done((bf16[256,2048]{1,0:T(8,128)(2,1)S(1)}, bf16[256,2048]{1,0:T(8,128)(2,1)S(1)}, u32[]{:S(2)}, u32[]{:S(2)}) %collective-permute-start.1) | collective-permute-done | bytes 1048608 | tf_op jit(solution)/shard_map/ppermute | solution.py:693
  59.3 11.7 collective-permute-done.32.refs_1_
  71.0 9.2 collective-permute-done.33.refs_2_
  89.6 10.2 collective-permute-done.5
  117.0 43.2 %attend.2 = (bf16[256,256]{1,0:T(8,128)(2,1)S(1)}, bf16[256,256]{1,0:T(8,128)(2,1)S(1)}, bf16[256,256]{1,0:T(8,128)(2,1)S(1)}, bf16[256,256]{1,0:T(8,128)(2,1)S(...) custom-call(s32[8]{0:T(128)S(1)} %fusion.124.order_ref, ...), custom_call_target="tpu_custom_call" | custom-call | tf_op jit(solution)/shard_map/attend/pallas_call | solution.py:286
  175.3 8.9 collective-permute-done.19
  188.5 6.9 collective-permute-done.16
  195.4 13.6 %collective-permute-done.20 = bf16[128,2048]{1,0:T(8,128)(2,1)S(1)} collective-permute-done((bf16[128,2048]{1,0:T(8,128)(2,1)S(1)}, bf16[128,2048]{1,0:T(8,128)(2,1)S(1)}, u32[]{:S(2)}, u32[]{:S(2)}) %collective-permute-start.20) | collective-permute-done | bytes 524320 | tf_op jit(solution)/shard_map/ppermute | solution.py:693
  213.8 22.0 %collective-permute-done.25.mine_in.refs_18_.refs_26_ = bf16[256,2048]{1,0:T(8,128)(2,1)S(1)} collective-permute-done((bf16[256,2048]{1,0:T(8,128)(2,1)S(1)}, bf16[256,2048]{1,0:T(8,128)(2,1)S(1)}, u32[]{:S(2)}, u32[]{:S(2)}) %collective-permute-start.25) | collective-permute-done | bytes 1048608 | tf_op jit(solution)/shard_map/ppermute | solution.py:693
  238.6 9.7 collective-permute-done.29
  252.2 7.0 all-gather.7.cloned.1.call-done.weights_hbm
  259.2 11.1 units.10
  272.0 11.4 units.9
  287.8 11.5 units.11
  300.8 11.3 units.8
  320.2 12.9 %collective-permute-done.42.mine_grad.refs_12_ = bf16[256,2048]{1,0:T(8,128)(2,1)S(1)} collective-permute-done((bf16[256,2048]{1,0:T(8,128)(2,1)S(1)}, bf16[256,2048]{1,0:T(8,128)(2,1)S(1)}, u32[]{:S(2)}, u32[]{:S(2)}) %collective-permute-start.42) | collective-permute-done | bytes 1048608 | tf_op jit(solution)/shard_map/ppermute | solution.py:693
  347.2 9.2 collective-permute-done.47
  367.8 11.5 collective-permute-done.48
  385.2 21.7 %collective-permute-done.53.refs_2_.refs_18_ = bf16[256,2048]{1,0:T(8,128)(2,1)S(1)} collective-permute-done((bf16[256,2048]{1,0:T(8,128)(2,1)S(1)}, bf16[256,2048]{1,0:T(8,128)(2,1)S(1)}, u32[]{:S(2)}, u32[]{:S(2)}) %collective-permute-start.53) | collective-permute-done | bytes 1048608 | tf_op jit(solution)/shard_map/ppermute | solution.py:693
  409.6 9.0 collective-permute-done.57
  423.8 42.4 %attend.3 = (bf16[256,256]{1,0:T(8,128)(2,1)S(1)}, bf16[256,256]{1,0:T(8,128)(2,1)S(1)}, bf16[256,256]{1,0:T(8,128)(2,1)S(1)}, bf16[256,256]{1,0:T(8,128)(2,1)S(...) custom-call(s32[8]{0:T(128)S(1)} %fusion.124.order_ref, ...), custom_call_target="tpu_custom_call" | custom-call | tf_op jit(solution)/shard_map/attend/pallas_call | solution.py:286
  476.4 8.6 collective-permute-done.65
  496.2 13.7 %collective-permute-done.66 = bf16[128,2048]{1,0:T(8,128)(2,1)S(1)} collective-permute-done((bf16[128,2048]{1,0:T(8,128)(2,1)S(1)}, bf16[128,2048]{1,0:T(8,128)(2,1)S(1)}, u32[]{:S(2)}, u32[]{:S(2)}) %collective-permute-start.66) | collective-permute-done | bytes 524320 | tf_op jit(solution)/shard_map/ppermute | solution.py:693
  515.2 16.0 %units.12 = (f32[256,2048]{1,0:T(8,128)}, bf16[256,2048]{1,0:T(8,128)(2,1)}, bf16[256,704]{1,0:T(8,128)(2,1)S(1)}, bf16[256,704]{1,0:T(8,128)(2,1)S(1)}, bf16[25...) custom-call(bf16[256,2048]{1,0:T(8,128)(2,1)} %copy-done.94, ...), custom_call_target="tpu_custom_call" | custom-call | tf_op jit(solution)/shard_map/units/pallas_call | solution.py:615
  542.0 15.6 %units.13 = (f32[256,2048]{1,0:T(8,128)}, bf16[256,2048]{1,0:T(8,128)(2,1)}, bf16[256,704]{1,0:T(8,128)(2,1)S(1)}, bf16[256,704]{1,0:T(8,128)(2,1)S(1)}, bf16[25...) custom-call(bf16[256,2048]{1,0:T(8,128)(2,1)} %collective-permute-do, ...), custom_call_target="tpu_custom_call" | custom-call | tf_op jit(solution)/shard_map/units/pallas_call | solution.py:615
  567.5 11.8 collective-permute-done.73
  581.4 16.1 %units.14 = (f32[256,2048]{1,0:T(8,128)}, bf16[256,2048]{1,0:T(8,128)(2,1)}, bf16[256,704]{1,0:T(8,128)(2,1)S(1)}, bf16[256,704]{1,0:T(8,128)(2,1)S(1)}, bf16[25...) custom-call(bf16[256,2048]{1,0:T(8,128)(2,1)} %copy-done.101, ...), custom_call_target="tpu_custom_call" | custom-call | tf_op jit(solution)/shard_map/units/pallas_call | solution.py:615
  602.0 15.8 %units.15 = (f32[256,2048]{1,0:T(8,128)}, bf16[256,2048]{1,0:T(8,128)(2,1)}, bf16[256,704]{1,0:T(8,128)(2,1)S(1)}, bf16[256,704]{1,0:T(8,128)(2,1)S(1)}, bf16[25...) custom-call(bf16[256,2048]{1,0:T(8,128)(2,1)} %copy-done.92, ...), custom_call_target="tpu_custom_call" | custom-call | tf_op jit(solution)/shard_map/units/pallas_call | solution.py:615
  626.3 11.4 weight_grads.6.refs_32_
  637.7 6.8 collective-permute-done.80
  653.5 20.0 %weight_grads.7 = bf16[2112,2048]{1,0:T(8,128)(2,1)} custom-call(bf16[256,704]{1,0:T(8,128)(2,1)} %copy-done.52, bf16[256,704]{1,0:T(8,128)(2,1)} %copy-done.53, bf16[256,704]{1,0:T(8,128)(2,1)} %copy-done.56, bf16[256,704]{1,0:T(8,128)(2,1)} %copy-done.57, bf16[256,704]{1,0:T(8,128)(2,1)} %copy-done.60, ...), custom_call_target="tpu_custom_call", output_to_operand_aliasing={{}: (32, {})} | custom-call | flops 11811160064 | bytes 11534336 | tf_op jit(solution)/shard_map/weight_grads/pallas_call | solution.py:469
  704.4 14.2 %collective-permute-done.89.refs_26_ = bf16[256,2048]{1,0:T(8,128)(2,1)S(1)} collective-permute-done((bf16[256,2048]{1,0:T(8,128)(2,1)S(1)}, bf16[256,2048]{1,0:T(8,128)(2,1)S(1)}, u32[]{:S(2)}, u32[]{:S(2)}) %collective-permute-start.89) | collective-permute-done | bytes 1048608 | tf_op jit(solution)/shard_map/ppermute | solution.py:693
  722.3 9.9 collective-permute-done.93
  740.9 44.3 %attend_back.2 = (bf16[256,768]{1,0:T(8,128)(2,1)S(1)}, bf16[256,768]{1,0:T(8,128)(2,1)}, bf16[256,768]{1,0:T(8,128)(2,1)}, bf16[256,768]{1,0:T(8,128)(2,1)}, bf...) custom-call(s32[8]{0:T(128)S(1)} %fusion.124.order_ref, ...), custom_call_target="tpu_custom_call" | custom-call | tf_op jit(solution)/shard_map/attend_back/pallas_call | solution.py:323
  809.7 10.5 collective-permute-done.106
  823.9 15.3 %weight_grads.8 = bf16[1024,2048]{1,0:T(8,128)(2,1)} custom-call(bf16[256,768]{1,0:T(8,128)(2,1)} %copy-done.5, bf16[256,768]{1,0:T(8,128)(2,1)} %get-tuple-element.599.refs_1_, bf16[256,768]{1,0:T(8,128)(2,1)} %get-tuple-element.600.refs_2_, bf16[256,768]{1,0:T(8,128)(2,1)} %get-tuple-element.601.refs_3_, bf16[256,768]{1,0:T(8,128)(2,1)} %get-tuple-element.602.refs_4_, ...), custom_call_target="tpu_custom_call" | custom-call | flops 8589934592 | bytes 8388608 | tf_op jit(solution)/shard_map/weight_grads/pallas_call | solution.py:469
  867.4 12.1 collective-permute-done.116.refs_10_
  886.6 7.3 collective-permute-done.117
  922.9 12.0 weight_grads.9.refs_32_
  935.1 9.3 collective-permute-done.125
  947.7 19.9 %weight_grads.10 = bf16[2112,2048]{1,0:T(8,128)(2,1)} custom-call(bf16[256,704]{1,0:T(8,128)(2,1)} %copy-done.116, bf16[256,704]{1,0:T(8,128)(2,1)} %copy-done.118, bf16[256,704]{1,0:T(8,128)(2,1)} %copy-done.160, bf16[256,704]{1,0:T(8,128)(2,1)} %copy-done.164, bf16[256,704]{1,0:T(8,128)(2,1)} %copy-done.161, ...), custom_call_target="tpu_custom_call", output_to_operand_aliasing={{}: (32, {})} | custom-call | flops 11811160064 | bytes 11534336 | tf_op jit(solution)/shard_map/weight_grads/pallas_call | solution.py:469
  980.7 18.4 %collective-permute-done.133.refs_26_ = bf16[256,2048]{1,0:T(8,128)(2,1)S(1)} collective-permute-done((bf16[256,2048]{1,0:T(8,128)(2,1)S(1)}, bf16[256,2048]{1,0:T(8,128)(2,1)S(1)}, u32[]{:S(2)}, u32[]{:S(2)}) %collective-permute-start.133) | collective-permute-done | bytes 1048608 | tf_op jit(solution)/shard_map/ppermute | solution.py:693
  1021.7 44.4 %attend_back.3 = (bf16[256,768]{1,0:T(8,128)(2,1)S(1)}, bf16[256,768]{1,0:T(8,128)(2,1)}, bf16[256,768]{1,0:T(8,128)(2,1)}, bf16[256,768]{1,0:T(8,128)(2,1)}, bf...) custom-call(s32[8]{0:T(128)S(1)} %fusion.124.order_ref, ...), custom_call_target="tpu_custom_call" | custom-call | tf_op jit(solution)/shard_map/attend_back/pallas_call | solution.py:323
  1078.9 8.2 collective-permute-done.150
  1089.3 10.5 collective-permute-done.145
  1103.8 15.7 %weight_grads.11 = bf16[1024,2048]{1,0:T(8,128)(2,1)} custom-call(bf16[256,768]{1,0:T(8,128)(2,1)} %copy-done.3, bf16[256,768]{1,0:T(8,128)(2,1)} %get-tuple-element.739.refs_1_, bf16[256,768]{1,0:T(8,128)(2,1)} %get-tuple-element.740.refs_2_, bf16[256,768]{1,0:T(8,128)(2,1)} %get-tuple-element.741.refs_3_, bf16[256,768]{1,0:T(8,128)(2,1)} %get-tuple-element.742.refs_4_, ...), custom_call_target="tpu_custom_call" | custom-call | flops 8589934592 | bytes 8388608 | tf_op jit(solution)/shard_map/weight_grads/pallas_call | solution.py:469
  1187.6 6.6 maximum_select_fusion
  1194.2 11.5 reduce-scatter.11.cloned.1.call-done
  (1089 shorter events, 493.2 us)
Async XLA Ops:
  7.2 109.8 %all-gather.5.cloned.1.call-start = ((), (), s32[]{:S(2)}) async-start(), calls=%async_computation.4 | async-start | bytes 5242880 | tf_op jit(solution)/shard_map/all_gather | solution.py:957
  25.6 233.6 %all-gather.7.cloned.1.call-start = ((), (), s32[]{:S(2)}) async-start(), calls=%async_computation.5 | async-start | bytes 10813440 | tf_op jit(solution)/shard_map/all_gather | solution.py:957
  28.5 25.0 %collective-permute-start.1 = (bf16[256,2048]{1,0:T(8,128)(2,1)S(1)}, bf16[256,2048]{1,0:T(8,128)(2,1)S(1)}, u32[]{:S(2)}, u32[]{:S(2)}) collective-permute-start(bf16[256,2048]{1,0:T(8,128)(2,1)S(1)} %fusion.24.refs_0_.refs_16_), channel_id=1, source_target_pairs={{0,2},{2,0},{4,6},{6,4},{1,3},{3,1},{5,7},{7,5},{8,10},{10,8},{12,... | collective-permute-start | bytes 3145736 | tf_op jit(solution)/shard_map/ppermute | solution.py:693
  30.1 24.7 %collective-permute-start.3 = (bf16[256,2048]{1,0:T(8,128)(2,1)S(1)}, bf16[256,2048]{1,0:T(8,128)(2,1)S(1)}, u32[]{:S(2)}, u32[]{:S(2)}) collective-permute-start(bf16[256,2048]{1,0:T(8,128)(2,1)S(1)} %fusion.24.refs_0_.refs_16_), channel_id=1, source_target_pairs={{0,4},{2,6},{4,0},{6,2},{1,5},{3,7},{5,1},{7,3},{8,12},{10,14},{12... | collective-permute-start | bytes 3145736 | tf_op jit(solution)/shard_map/ppermute | solution.py:693
  83.2 256.9 %all-gather.9.cloned.1.call-start = ((), (), s32[]{:S(2)}) async-start(), calls=%async_computation.6 | async-start | bytes 5242880 | tf_op jit(solution)/shard_map/all_gather | solution.py:957
  107.3 53.0 %collective-permute-start.11 = (bf16[3136,128]{1,0:T(8,128)(2,1)}, bf16[3136,128]{1,0:T(8,128)(2,1)S(1)}, u32[]{:S(2)}, u32[]{:S(2)}) collective-permute-start(bf16[3136,128]{1,0:T(8,128)(2,1)} %get-tuple-element.836), channel_id=1, source_target_pairs={{0,2},{2,0},{4,6},{6,4},{1,3},{3,1},{5,7},{7,5},{8,10},{10,8},{12,... | collective-permute-start | bytes 2408456 | tf_op jit(solution)/shard_map/ppermute | solution.py:693
  108.3 52.0 %collective-permute-start.12 = (bf16[3136,128]{1,0:T(8,128)(2,1)}, bf16[3136,128]{1,0:T(8,128)(2,1)S(1)}, u32[]{:S(2)}, u32[]{:S(2)}) collective-permute-start(bf16[3136,128]{1,0:T(8,128)(2,1)} %get-tuple-element.835), channel_id=1, source_target_pairs={{0,4},{2,6},{4,0},{6,2},{1,5},{3,7},{5,1},{7,3},{8,12},{10,14},{12... | collective-permute-start | bytes 2408456 | tf_op jit(solution)/shard_map/ppermute | solution.py:693
  109.4 50.9 %collective-permute-start.13 = (bf16[3136,128]{1,0:T(8,128)(2,1)}, bf16[3136,128]{1,0:T(8,128)(2,1)S(1)}, u32[]{:S(2)}, u32[]{:S(2)}) collective-permute-start(bf16[3136,128]{1,0:T(8,128)(2,1)} %get-tuple-element.834), channel_id=1, source_target_pairs={{0,6},{2,4},{4,2},{6,0},{1,7},{3,5},{5,3},{7,1},{8,14},{10,12},{12... | collective-permute-start | bytes 2408456 | tf_op jit(solution)/shard_map/ppermute | solution.py:693
  166.5 42.8 %collective-permute-start.14 = (bf16[256,2048]{1,0:T(8,128)(2,1)S(1)}, bf16[256,2048]{1,0:T(8,128)(2,1)S(1)}, u32[]{:S(2)}, u32[]{:S(2)}) collective-permute-start(bf16[256,2048]{1,0:T(8,128)(2,1)S(1)} %convolution_convert_fusion.11), channel_id=1, source_target_pairs={{0,1},{1,0},{2,3},{3,2},{4,5},{5,4},{6,7},{7,6},{8,9},{9,8},{10,11... | collective-permute-start | bytes 3145736 | tf_op jit(solution)/shard_map/ppermute | solution.py:696
  174.3 34.8 %collective-permute-start.23 = (bf16[128,2048]{1,0:T(8,128)(2,1)S(1)}, bf16[128,2048]{1,0:T(8,128)(2,1)S(1)}, u32[]{:S(2)}, u32[]{:S(2)}) collective-permute-start(bf16[128,2048]{1,0:T(8,128)(2,1)S(1)} %slice.732), channel_id=1, source_target_pairs={{0,4},{2,6},{4,0},{6,2},{1,5},{3,7},{5,1},{7,3},{8,12},{10,14},{12... | collective-permute-start | bytes 1572872 | tf_op jit(solution)/shard_map/ppermute | solution.py:693
  184.3 24.7 %collective-permute-start.20 = (bf16[128,2048]{1,0:T(8,128)(2,1)S(1)}, bf16[128,2048]{1,0:T(8,128)(2,1)S(1)}, u32[]{:S(2)}, u32[]{:S(2)}) collective-permute-start(bf16[128,2048]{1,0:T(8,128)(2,1)S(1)} %fusion.44), channel_id=1, source_target_pairs={{0,4},{2,6},{4,0},{6,2},{1,5},{3,7},{5,1},{7,3},{8,12},{10,14},{12... | collective-permute-start | bytes 1572872 | tf_op jit(solution)/shard_map/ppermute | solution.py:693
  211.4 24.4 %collective-permute-start.25 = (bf16[256,2048]{1,0:T(8,128)(2,1)S(1)}, bf16[256,2048]{1,0:T(8,128)(2,1)S(1)}, u32[]{:S(2)}, u32[]{:S(2)}) collective-permute-start(bf16[256,2048]{1,0:T(8,128)(2,1)S(1)} %add_convert_fusion.3.mine_in.refs_16_.refs_24_), channel_id=1, source_target_pairs={{0,2},{2,0},{4,6},{6,4},{1,3},{3,1},{5,7},{7,5},{8,10},{10,8},{12,... | collective-permute-start | bytes 3145736 | tf_op jit(solution)/shard_map/ppermute | solution.py:693
  212.3 301.5 %all-gather.11.cloned.1.call-start = ((), (), s32[]{:S(2)}) async-start(), calls=%async_computation.7 | async-start | bytes 10813440 | tf_op jit(solution)/shard_map/all_gather | solution.py:957
  212.6 24.5 %collective-permute-start.27 = (bf16[256,2048]{1,0:T(8,128)(2,1)S(1)}, bf16[256,2048]{1,0:T(8,128)(2,1)S(1)}, u32[]{:S(2)}, u32[]{:S(2)}) collective-permute-start(bf16[256,2048]{1,0:T(8,128)(2,1)S(1)} %add_convert_fusion.3.mine_in.refs_16_.refs_24_), channel_id=1, source_target_pairs={{0,4},{2,6},{4,0},{6,2},{1,5},{3,7},{5,1},{7,3},{8,12},{10,14},{12... | collective-permute-start | bytes 3145736 | tf_op jit(solution)/shard_map/ppermute | solution.py:693
  272.0 40.2 %collective-permute-start.37 = (bf16[256,2048]{1,0:T(8,128)(2,1)}, bf16[256,2048]{1,0:T(8,128)(2,1)S(1)}, u32[]{:S(2)}, u32[]{:S(2)}) collective-permute-start(bf16[256,2048]{1,0:T(8,128)(2,1)} %get-tuple-element.435), channel_id=1, source_target_pairs={{0,1},{1,0},{2,3},{3,2},{4,5},{5,4},{6,7},{7,6},{8,9},{9,8},{10,11... | collective-permute-start | bytes 3145736 | tf_op jit(solution)/shard_map/ppermute | solution.py:696
  283.5 32.9 %collective-permute-start.36 = (bf16[256,2048]{1,0:T(8,128)(2,1)}, bf16[256,2048]{1,0:T(8,128)(2,1)}, u32[]{:S(2)}, u32[]{:S(2)}) collective-permute-start(bf16[256,2048]{1,0:T(8,128)(2,1)} %get-tuple-element.431), channel_id=1, source_target_pairs={{0,1},{1,0},{2,3},{3,2},{4,5},{5,4},{6,7},{7,6},{8,9},{9,8},{10,11... | collective-permute-start | bytes 3145736 | tf_op jit(solution)/shard_map/ppermute | solution.py:696
  284.2 35.4 %collective-permute-start.40 = (bf16[256,2048]{1,0:T(8,128)(2,1)S(1)}, bf16[256,2048]{1,0:T(8,128)(2,1)S(1)}, u32[]{:S(2)}, u32[]{:S(2)}) collective-permute-start(bf16[256,2048]{1,0:T(8,128)(2,1)S(1)} %constant_dynamic-slice_fusion.12.mine_grad.refs_8_), channel_id=1, source_target_pairs={{0,2},{2,0},{4,6},{6,4},{1,3},{3,1},{5,7},{7,5},{8,10},{10,8},{12,... | collective-permute-start | bytes 3145736 | tf_op jit(solution)/shard_map/ppermute | solution.py:693
  285.8 47.3 %collective-permute-start.42 = (bf16[256,2048]{1,0:T(8,128)(2,1)S(1)}, bf16[256,2048]{1,0:T(8,128)(2,1)S(1)}, u32[]{:S(2)}, u32[]{:S(2)}) collective-permute-start(bf16[256,2048]{1,0:T(8,128)(2,1)S(1)} %constant_dynamic-slice_fusion.12.mine_grad.refs_8_), channel_id=1, source_target_pairs={{0,4},{2,6},{4,0},{6,2},{1,5},{3,7},{5,1},{7,3},{8,12},{10,14},{12... | collective-permute-start | bytes 3145736 | tf_op jit(solution)/shard_map/ppermute | solution.py:693
  287.3 45.8 %collective-permute-start.44 = (bf16[256,2048]{1,0:T(8,128)(2,1)S(1)}, bf16[256,2048]{1,0:T(8,128)(2,1)S(1)}, u32[]{:S(2)}, u32[]{:S(2)}) collective-permute-start(bf16[256,2048]{1,0:T(8,128)(2,1)S(1)} %constant_dynamic-slice_fusion.12.mine_grad.refs_8_), channel_id=1, source_target_pairs={{0,6},{2,4},{4,2},{6,0},{1,7},{3,5},{5,3},{7,1},{8,14},{10,12},{12... | collective-permute-start | bytes 3145736 | tf_op jit(solution)/shard_map/ppermute | solution.py:693
  346.7 33.8 %collective-permute-start.51 = (bf16[128,2048]{1,0:T(8,128)(2,1)S(1)}, bf16[128,2048]{1,0:T(8,128)(2,1)S(1)}, u32[]{:S(2)}, u32[]{:S(2)}) collective-permute-start(bf16[128,2048]{1,0:T(8,128)(2,1)S(1)} %slice.730), channel_id=1, source_target_pairs={{0,4},{2,6},{4,0},{6,2},{1,5},{3,7},{5,1},{7,3},{8,12},{10,14},{12... | collective-permute-start | bytes 1572872 | tf_op jit(solution)/shard_map/ppermute | solution.py:693
  361.4 484.7 %reduce-scatter.5.cloned.1.call-start = ((), (), s32[]{:S(2)}) async-start(), calls=%async_computation.8 | async-start | bytes 10813440 | tf_op jit(solution)/shard_map/reduce_scatter | solution.py:961
  383.6 24.8 %collective-permute-start.55 = (bf16[256,2048]{1,0:T(8,128)(2,1)S(1)}, bf16[256,2048]{1,0:T(8,128)(2,1)S(1)}, u32[]{:S(2)}, u32[]{:S(2)}) collective-permute-start(bf16[256,2048]{1,0:T(8,128)(2,1)S(1)} %add_convert_fusion.2.refs_0_.refs_16_), channel_id=1, source_target_pairs={{0,4},{2,6},{4,0},{6,2},{1,5},{3,7},{5,1},{7,3},{8,12},{10,14},{12... | collective-permute-start | bytes 3145736 | tf_op jit(solution)/shard_map/ppermute | solution.py:693
  467.5 42.6 %collective-permute-start.60 = (bf16[256,2048]{1,0:T(8,128)(2,1)S(1)}, bf16[256,2048]{1,0:T(8,128)(2,1)S(1)}, u32[]{:S(2)}, u32[]{:S(2)}) collective-permute-start(bf16[256,2048]{1,0:T(8,128)(2,1)S(1)} %convolution_convert_fusion.7), channel_id=1, source_target_pairs={{0,1},{1,0},{2,3},{3,2},{4,5},{5,4},{6,7},{7,6},{8,9},{9,8},{10,11... | collective-permute-start | bytes 3145736 | tf_op jit(solution)/shard_map/ppermute | solution.py:696
  475.4 34.6 %collective-permute-start.69 = (bf16[128,2048]{1,0:T(8,128)(2,1)S(1)}, bf16[128,2048]{1,0:T(8,128)(2,1)S(1)}, u32[]{:S(2)}, u32[]{:S(2)}) collective-permute-start(bf16[128,2048]{1,0:T(8,128)(2,1)S(1)} %slice.728), channel_id=1, source_target_pairs={{0,4},{2,6},{4,0},{6,2},{1,5},{3,7},{5,1},{7,3},{8,12},{10,14},{12... | collective-permute-start | bytes 1572872 | tf_op jit(solution)/shard_map/ppermute | solution.py:693
  485.1 24.8 %collective-permute-start.66 = (bf16[128,2048]{1,0:T(8,128)(2,1)S(1)}, bf16[128,2048]{1,0:T(8,128)(2,1)S(1)}, u32[]{:S(2)}, u32[]{:S(2)}) collective-permute-start(bf16[128,2048]{1,0:T(8,128)(2,1)S(1)} %fusion.42), channel_id=1, source_target_pairs={{0,4},{2,6},{4,0},{6,2},{1,5},{3,7},{5,1},{7,3},{8,12},{10,14},{12... | collective-permute-start | bytes 1572872 | tf_op jit(solution)/shard_map/ppermute | solution.py:693
  512.4 25.7 %collective-permute-start.72 = (bf16[256,2048]{1,0:T(8,128)(2,1)S(1)}, bf16[256,2048]{1,0:T(8,128)(2,1)}, u32[]{:S(2)}, u32[]{:S(2)}) collective-permute-start(bf16[256,2048]{1,0:T(8,128)(2,1)S(1)} %add_convert_fusion.1.mine_in.refs_16_.refs_24_), channel_id=1, source_target_pairs={{0,2},{2,0},{4,6},{6,4},{1,3},{3,1},{5,7},{7,5},{8,10},{10,8},{12,... | collective-permute-start | bytes 3145736 | tf_op jit(solution)/shard_map/ppermute | solution.py:693
  538.1 25.8 %collective-permute-start.74 = (bf16[256,2048]{1,0:T(8,128)(2,1)}, bf16[256,2048]{1,0:T(8,128)(2,1)S(1)}, u32[]{:S(2)}, u32[]{:S(2)}) collective-permute-start(bf16[256,2048]{1,0:T(8,128)(2,1)} %copy-done.94), channel_id=1, source_target_pairs={{0,4},{2,6},{4,0},{6,2},{1,5},{3,7},{5,1},{7,3},{8,12},{10,14},{12... | collective-permute-start | bytes 3145736 | tf_op jit(solution)/shard_map/ppermute | solution.py:693
  567.5 30.7 %collective-permute-start.71 = (bf16[256,2048]{1,0:T(8,128)(2,1)}, bf16[256,2048]{1,0:T(8,128)(2,1)S(1)}, u32[]{:S(2)}, u32[]{:S(2)}) collective-permute-start(bf16[256,2048]{1,0:T(8,128)(2,1)} %get-tuple-element.461), channel_id=1, source_target_pairs={{0,1},{1,0},{2,3},{3,2},{4,5},{5,4},{6,7},{7,6},{8,9},{9,8},{10,11... | collective-permute-start | bytes 3145736 | tf_op jit(solution)/shard_map/ppermute | solution.py:696
  673.5 303.6 %reduce-scatter.7.cloned.1.call-start = ((), (), s32[]{:S(2)}) async-start(), calls=%async_computation.9 | async-start | bytes 5242880 | tf_op jit(solution)/shard_map/reduce_scatter | solution.py:961
  693.1 25.5 %collective-permute-start.89 = (bf16[256,2048]{1,0:T(8,128)(2,1)S(1)}, bf16[256,2048]{1,0:T(8,128)(2,1)S(1)}, u32[]{:S(2)}, u32[]{:S(2)}) collective-permute-start(bf16[256,2048]{1,0:T(8,128)(2,1)S(1)} %get-tuple-element.606.refs_24_), channel_id=1, source_target_pairs={{0,2},{2,0},{4,6},{6,4},{1,3},{3,1},{5,7},{7,5},{8,10},{10,8},{12,... | collective-permute-start | bytes 3145736 | tf_op jit(solution)/shard_map/ppermute | solution.py:693
  694.3 25.3 %collective-permute-start.91 = (bf16[256,2048]{1,0:T(8,128)(2,1)S(1)}, bf16[256,2048]{1,0:T(8,128)(2,1)S(1)}, u32[]{:S(2)}, u32[]{:S(2)}) collective-permute-start(bf16[256,2048]{1,0:T(8,128)(2,1)S(1)} %get-tuple-element.606.refs_24_), channel_id=1, source_target_pairs={{0,4},{2,6},{4,0},{6,2},{1,5},{3,7},{5,1},{7,3},{8,12},{10,14},{12... | collective-permute-start | bytes 3145736 | tf_op jit(solution)/shard_map/ppermute | solution.py:693
  697.0 36.1 %collective-permute-start.88 = (bf16[256,2048]{1,0:T(8,128)(2,1)S(1)}, bf16[256,2048]{1,0:T(8,128)(2,1)S(1)}, u32[]{:S(2)}, u32[]{:S(2)}) collective-permute-start(bf16[256,2048]{1,0:T(8,128)(2,1)S(1)} %get-tuple-element.606.refs_24_), channel_id=1, source_target_pairs={{0,1},{1,0},{2,3},{3,2},{4,5},{5,4},{6,7},{7,6},{8,9},{9,8},{10,11... | collective-permute-start | bytes 3145736 | tf_op jit(solution)/shard_map/ppermute | solution.py:696
  737.4 47.9 %collective-permute-start.100 = (bf16[256,2048]{1,0:T(8,128)(2,1)}, bf16[256,2048]{1,0:T(8,128)(2,1)S(1)}, u32[]{:S(2)}, u32[]{:S(2)}) collective-permute-start(bf16[256,2048]{1,0:T(8,128)(2,1)} %convert_add_fusion.3), channel_id=1, source_target_pairs={{0,2},{2,0},{4,6},{6,4},{1,3},{3,1},{5,7},{7,5},{8,10},{10,8},{12,... | collective-permute-start | bytes 3145736 | tf_op jit(solution)/shard_map/ppermute | solution.py:693
  738.7 47.6 %collective-permute-start.101 = (bf16[256,2048]{1,0:T(8,128)(2,1)}, bf16[256,2048]{1,0:T(8,128)(2,1)S(1)}, u32[]{:S(2)}, u32[]{:S(2)}) collective-permute-start(bf16[256,2048]{1,0:T(8,128)(2,1)} %convert_add_fusion.2), channel_id=1, source_target_pairs={{0,4},{2,6},{4,0},{6,2},{1,5},{3,7},{5,1},{7,3},{8,12},{10,14},{12... | collective-permute-start | bytes 3145736 | tf_op jit(solution)/shard_map/ppermute | solution.py:693
  739.6 46.7 %collective-permute-start.102 = (bf16[256,2048]{1,0:T(8,128)(2,1)}, bf16[256,2048]{1,0:T(8,128)(2,1)S(1)}, u32[]{:S(2)}, u32[]{:S(2)}) collective-permute-start(bf16[256,2048]{1,0:T(8,128)(2,1)} %convert_add_fusion.1), channel_id=1, source_target_pairs={{0,6},{2,4},{4,2},{6,0},{1,7},{3,5},{5,3},{7,1},{8,14},{10,12},{12... | collective-permute-start | bytes 3145736 | tf_op jit(solution)/shard_map/ppermute | solution.py:693
  801.2 40.6 %collective-permute-start.104 = (bf16[256,2048]{1,0:T(8,128)(2,1)}, bf16[256,2048]{1,0:T(8,128)(2,1)S(1)}, u32[]{:S(2)}, u32[]{:S(2)}) collective-permute-start(bf16[256,2048]{1,0:T(8,128)(2,1)} %convolution_convert_fusion.19), channel_id=1, source_target_pairs={{0,1},{1,0},{2,3},{3,2},{4,5},{5,4},{6,7},{7,6},{8,9},{9,8},{10,11... | collective-permute-start | bytes 3145736 | tf_op jit(solution)/shard_map/ppermute | solution.py:696
  853.4 278.1 %reduce-scatter.9.cloned.1.call-start = ((), (), s32[]{:S(2)}) async-start(), calls=%async_computation.10 | async-start | bytes 10813440 | tf_op jit(solution)/shard_map/reduce_scatter | solution.py:961
  853.8 25.6 %collective-permute-start.116 = (bf16[256,2048]{1,0:T(8,128)(2,1)S(1)}, bf16[256,2048]{1,0:T(8,128)(2,1)S(1)}, u32[]{:S(2)}, u32[]{:S(2)}) collective-permute-start(bf16[256,2048]{1,0:T(8,128)(2,1)S(1)} %get-tuple-element.654.refs_8_), channel_id=1, source_target_pairs={{0,2},{2,0},{4,6},{6,4},{1,3},{3,1},{5,7},{7,5},{8,10},{10,8},{12,... | collective-permute-start | bytes 3145736 | tf_op jit(solution)/shard_map/ppermute | solution.py:693
  855.1 25.6 %collective-permute-start.118 = (bf16[256,2048]{1,0:T(8,128)(2,1)S(1)}, bf16[256,2048]{1,0:T(8,128)(2,1)S(1)}, u32[]{:S(2)}, u32[]{:S(2)}) collective-permute-start(bf16[256,2048]{1,0:T(8,128)(2,1)S(1)} %get-tuple-element.654.refs_8_), channel_id=1, source_target_pairs={{0,4},{2,6},{4,0},{6,2},{1,5},{3,7},{5,1},{7,3},{8,12},{10,14},{12... | collective-permute-start | bytes 3145736 | tf_op jit(solution)/shard_map/ppermute | solution.py:693
  909.5 25.4 %collective-permute-start.127 = (bf16[128,2048]{1,0:T(8,128)(2,1)S(1)}, bf16[128,2048]{1,0:T(8,128)(2,1)}, u32[]{:S(2)}, u32[]{:S(2)}) collective-permute-start(bf16[128,2048]{1,0:T(8,128)(2,1)S(1)} %slice.723), channel_id=1, source_target_pairs={{0,2},{2,0},{4,6},{6,4},{1,3},{3,1},{5,7},{7,5},{8,10},{10,8},{12,... | collective-permute-start | bytes 1572872 | tf_op jit(solution)/shard_map/ppermute | solution.py:693
  968.5 237.2 %reduce-scatter.11.cloned.1.call-start = ((), (), s32[]{:S(2)}) async-start(), calls=%async_computation.11 | async-start | bytes 5242880 | tf_op jit(solution)/shard_map/reduce_scatter | solution.py:961
  976.1 24.2 %collective-permute-start.135 = (bf16[256,2048]{1,0:T(8,128)(2,1)S(1)}, bf16[256,2048]{1,0:T(8,128)(2,1)}, u32[]{:S(2)}, u32[]{:S(2)}) collective-permute-start(bf16[256,2048]{1,0:T(8,128)(2,1)S(1)} %get-tuple-element.746.refs_24_), channel_id=1, source_target_pairs={{0,4},{2,6},{4,0},{6,2},{1,5},{3,7},{5,1},{7,3},{8,12},{10,14},{12... | collective-permute-start | bytes 3145736 | tf_op jit(solution)/shard_map/ppermute | solution.py:693
  979.4 34.1 %collective-permute-start.132 = (bf16[256,2048]{1,0:T(8,128)(2,1)S(1)}, bf16[256,2048]{1,0:T(8,128)(2,1)S(1)}, u32[]{:S(2)}, u32[]{:S(2)}) collective-permute-start(bf16[256,2048]{1,0:T(8,128)(2,1)S(1)} %get-tuple-element.746.refs_24_), channel_id=1, source_target_pairs={{0,1},{1,0},{2,3},{3,2},{4,5},{5,4},{6,7},{7,6},{8,9},{9,8},{10,11... | collective-permute-start | bytes 3145736 | tf_op jit(solution)/shard_map/ppermute | solution.py:696
  1018.2 47.9 %collective-permute-start.140 = (bf16[3136,128]{1,0:T(8,128)(2,1)S(1)}, bf16[3136,128]{1,0:T(8,128)(2,1)S(1)}, u32[]{:S(2)}, u32[]{:S(2)}) collective-permute-start(bf16[3136,128]{1,0:T(8,128)(2,1)S(1)} %get-tuple-element.832), channel_id=1, source_target_pairs={{0,2},{2,0},{4,6},{6,4},{1,3},{3,1},{5,7},{7,5},{8,10},{10,8},{12,... | collective-permute-start | bytes 2408456 | tf_op jit(solution)/shard_map/ppermute | solution.py:693
  1019.3 46.8 %collective-permute-start.141 = (bf16[3136,128]{1,0:T(8,128)(2,1)S(1)}, bf16[3136,128]{1,0:T(8,128)(2,1)S(1)}, u32[]{:S(2)}, u32[]{:S(2)}) collective-permute-start(bf16[3136,128]{1,0:T(8,128)(2,1)S(1)} %get-tuple-element.831), channel_id=1, source_target_pairs={{0,4},{2,6},{4,0},{6,2},{1,5},{3,7},{5,1},{7,3},{8,12},{10,14},{12... | collective-permute-start | bytes 2408456 | tf_op jit(solution)/shard_map/ppermute | solution.py:693
  1020.4 45.7 %collective-permute-start.142 = (bf16[3136,128]{1,0:T(8,128)(2,1)S(1)}, bf16[3136,128]{1,0:T(8,128)(2,1)S(1)}, u32[]{:S(2)}, u32[]{:S(2)}) collective-permute-start(bf16[3136,128]{1,0:T(8,128)(2,1)S(1)} %get-tuple-element.830), channel_id=1, source_target_pairs={{0,6},{2,4},{4,2},{6,0},{1,7},{3,5},{5,3},{7,1},{8,14},{10,12},{12... | collective-permute-start | bytes 2408456 | tf_op jit(solution)/shard_map/ppermute | solution.py:693
  1124.6 33.9 %collective-permute-start.103 = (bf16[256,2048]{1,0:T(8,128)(2,1)}, bf16[256,2048]{1,0:T(8,128)(2,1)}, u32[]{:S(2)}, u32[]{:S(2)}) collective-permute-start(bf16[256,2048]{1,0:T(8,128)(2,1)} %add_convert_fusion), channel_id=1, source_target_pairs={{0,1},{1,0},{2,3},{3,2},{4,5},{5,4},{6,7},{7,6},{8,9},{9,8},{10,11... | collective-permute-start | bytes 3145736 | tf_op jit(solution)/shard_map/ppermute | solution.py:696
  1138.9 48.7 %collective-permute-start.153 = (f32[256,2048]{1,0:T(8,128)}, f32[256,2048]{1,0:T(8,128)}, u32[]{:S(2)}, u32[]{:S(2)}) collective-permute-start(f32[256,2048]{1,0:T(8,128)} %fusion.28), channel_id=1, source_target_pairs={{0,1},{1,0},{2,3},{3,2},{4,5},{5,4},{6,7},{7,6},{8,9},{9,8},{10,11... | collective-permute-start | bytes 6291464 | tf_op jit(solution)/shard_map/ppermute | solution.py:696
  (362 other events, 3456.9 us)
Sparse Core Ops, SparseCore 0:
  25.7 79.1 all-gather.4
  107.1 152.1 all-gather.6
  260.8 79.2 all-gather.8
  361.5 150.1 all-gather.10
  673.6 148.7 reduce-scatter.4
  853.5 77.5 reduce-scatter.6
  968.6 149.0 reduce-scatter.8
  1120.1 85.5 reduce-scatter.10

commit v2 on v1

--- a/solution.py
+++ b/solution.py
@@ -212,8 +212,9 @@
 
     lax.fori_loop(0, ctx_count, prepare, 0)
 
-    key_index = lax.broadcasted_iota(jnp.int32, (block, block), 0)
-    query_index = lax.broadcasted_iota(jnp.int32, (block, block), 1)
+    small = min(256, block)
+    key_index = lax.broadcasted_iota(jnp.int32, (small, small), 0)
+    query_index = lax.broadcasted_iota(jnp.int32, (small, small), 1)
 
     def pair(head, key_rows, query_rows, diagonal):
         query = query_wide[head, query_rows, :]
@@ -232,7 +233,13 @@
 
         def over_keys(key_place, unused, head=head):
             key_rows = pl.ds(pl.multiple_of(key_place * block, block), block)
-            pair(head, key_rows, key_rows, True)
+            for key_part in range(block // small):
+                for query_part in range(key_part, block // small):
+                    small_rows = [
+                        pl.ds(pl.multiple_of(key_place * block + part * small, small), small)
+                        for part in (key_part, query_part)
+                    ]
+                    pair(head, *small_rows, key_part == query_part)
 
             def over_queries(query_place, inner):
                 pair(head, key_rows, pl.ds(pl.multiple_of(query_place * block, block), block), False)
@@ -305,7 +312,9 @@
         ],
         scratch_shapes=[pltpu.VMEM((rows, 2 * LANES), low)],
         compiler_params=pltpu.CompilerParams(vmem_limit_bytes=52 * 2**20),
-        cost_estimate=pl.CostEstimate(flops=0, bytes_accessed=0, transcendentals=0),
+        cost_estimate=pl.CostEstimate(
+            flops=pairs * rows * rows * LANES * 32, bytes_accessed=0, transcendentals=0
+        ),
         name="attend",
     )(order, *normed, weight, bias, *tables)
     return (results[:slots], *results[slots:])
@@ -342,7 +351,9 @@
             pltpu.VMEM((rows, LANES), full),
         ],
         compiler_params=pltpu.CompilerParams(vmem_limit_bytes=52 * 2**20),
-        cost_estimate=pl.CostEstimate(flops=0, bytes_accessed=0, transcendentals=0),
+        cost_estimate=pl.CostEstimate(
+            flops=pairs * rows * rows * LANES * 32, bytes_accessed=0, transcendentals=0
+        ),
         name="attend_back",
     )(order, rotated, *grads, fine, totals, *tables)
     return (results[:slots], results[slots])
@@ -486,21 +497,15 @@
     )(*lefts, *rights, *kept)
 
 
-def start_copies(pairs, sems):
+def start_weights(weights_hbm, held_refs, sems):
+    units = held_refs[0].shape[0]
     copies = [
-        pltpu.make_async_copy(source, target, sems.at[i])
-        for i, (source, target) in enumerate(pairs)
+        pltpu.make_async_copy(weights_hbm.at[i * units : (i + 1) * units, :], held, sems.at[i])
+        for i, held in enumerate(held_refs)
     ]
     for copy in copies:
         copy.start()
     return copies
-
-
-def weight_pairs(weights_hbm, held_refs):
-    units = held_refs[0].shape[0]
-    return [
-        (weights_hbm.at[i * units : (i + 1) * units, :], held) for i, held in enumerate(held_refs)
-    ]
 
 
 def units_kernel(
@@ -515,113 +520,48 @@
     other_up,
     mine_units,
     other_units,
-    rows_in,
     gate_w,
     up_w,
     down_w,
     sems,
 ):
-    rows = other_out.shape[0]
-    copies = start_copies(
-        [(other_in, rows_in.at[:rows, :]), (mine_in, rows_in.at[rows:, :])]
-        + weight_pairs(weights_hbm, (gate_w, up_w, down_w)),
-        sems,
+    copies = start_weights(weights_hbm, (gate_w, up_w, down_w), sems)
+    work = (
+        (other_in, other_out, other_gate, other_up, other_units),
+        (mine_in, mine_out, mine_gate, mine_up, mine_units),
     )
-    copies[0].wait()
-    copies[1].wait()
-    copies[2].wait()
-    gate = dot_nt(rows_in[...], gate_w[...])
-    other_gate[...] = gate[:rows]
-    mine_gate[...] = gate[rows:]
-    copies[3].wait()
-    up = dot_nt(rows_in[...], up_w[...])
-    other_up[...] = up[:rows]
-    mine_up[...] = up[rows:]
-    units = (gate / (1.0 + jnp.exp(-gate)) * up).astype(low)
-    other_units[...] = units[:rows]
-    mine_units[...] = units[rows:]
-    copies[4].wait()
-    out = dot_nn(units, down_w[...])
-    other_out[...] = out[:rows].astype(low)
-    mine_out[...] = out[rows:]
-
-
-def last_units_kernel(
-    mine_in,
-    other_in,
-    mine_grad,
-    other_grad,
-    weights_hbm,
-    mine_out,
-    other_out,
-    mine_gate,
-    other_gate,
-    mine_up,
-    other_up,
-    mine_units,
-    other_units,
-    rows_in,
-    gate_w,
-    up_w,
-    down_w,
-    grad_in,
-    sems,
-):
-    rows = other_out.shape[0]
-    copies = start_copies(
-        [(other_in, rows_in.at[:rows, :]), (mine_in, rows_in.at[rows:, :])]
-        + weight_pairs(weights_hbm, (gate_w, up_w, down_w))
-        + [(other_grad, grad_in.at[:rows, :]), (mine_grad, grad_in.at[rows:, :])],
-        sems,
-    )
-    copies[0].wait()
-    copies[1].wait()
-    copies[2].wait()
-    gate = dot_nt(rows_in[...], gate_w[...])
-    sigmoid = 1.0 / (1.0 + jnp.exp(-gate))
-    copies[3].wait()
-    up = dot_nt(rows_in[...], up_w[...])
-    copies[4].wait()
-    copies[5].wait()
-    copies[6].wait()
-    grad = dot_nt(grad_in[...], down_w[...])
-    silu = gate * sigmoid
-    units = (silu * up).astype(low)
-    grad_up = (grad * silu).astype(low)
-    grad_gate = (grad * up * (sigmoid * (1.0 + gate * (1.0 - sigmoid)))).astype(low)
-    other_units[...] = units[:rows]
-    mine_units[...] = units[rows:]
-    other_up[...] = grad_up[:rows]
-    mine_up[...] = grad_up[rows:]
-    other_gate[...] = grad_gate[:rows]
-    mine_gate[...] = grad_gate[rows:]
-    out = dot_nn(grad_gate, gate_w[...]) + dot_nn(grad_up, up_w[...])
-    other_out[...] = out[:rows].astype(low)
-    mine_out[...] = out[rows:]
-
-
-def units_call(kernel, pieces, weights):
+    for place, (rows_in, out, gate_out, up_out, units_out) in enumerate(work):
+        if place == 0:
+            copies[0].wait()
+        gate = dot_nt(rows_in[...], gate_w[...])
+        gate_out[...] = gate
+        if place == 0:
+            copies[1].wait()
+        up = dot_nt(rows_in[...], up_w[...])
+        up_out[...] = up
+        units = (gate / (1.0 + jnp.exp(-gate)) * up).astype(low)
+        units_out[...] = units
+        if place == 0:
+            copies[2].wait()
+        out[...] = dot_nn(units, down_w[...]).astype(out.dtype)
+
+
+def units_call(pieces, weights):
     rows, features = pieces[0].shape
     units = weights.shape[0] // 3
     inside = pl.BlockSpec(memory_space=pltpu.VMEM)
-    outside = pl.BlockSpec(memory_space=pl.ANY)
-    kept = full if len(pieces) == 2 else low
     out_shape = (
         [jax.ShapeDtypeStruct((rows, features), kind) for kind in (full, low)]
-        + [jax.ShapeDtypeStruct((rows, units), kept)] * 4
+        + [jax.ShapeDtypeStruct((rows, units), full)] * 4
         + [jax.ShapeDtypeStruct((rows, units), low)] * 2
     )
-    held = pltpu.VMEM((2 * rows, features), low)
     done = pl.pallas_call(
-        kernel,
-        in_specs=[outside] * (len(pieces) + 1),
+        units_kernel,
+        in_specs=[inside] * 2 + [pl.BlockSpec(memory_space=pl.ANY)],
         out_specs=[inside] * len(out_shape),
         out_shape=out_shape,
-        scratch_shapes=[held]
-        + [pltpu.VMEM((units, features), low)] * 3
-        + [held] * (len(pieces) // 2 - 1)
-        + [pltpu.SemaphoreType.DMA((3 + len(pieces),))],
-        compiler_params=pltpu.CompilerParams(vmem_limit_bytes=52 * 2**20),
+        scratch_shapes=[pltpu.VMEM((units, features), low)] * 3 + [pltpu.SemaphoreType.DMA((3,))],
+        compiler_params=pltpu.CompilerParams(vmem_limit_bytes=48 * 2**20),
         cost_estimate=pl.CostEstimate(flops=0, bytes_accessed=0, transcendentals=0),
         name="units",
     )(*pieces, weights)
@@ -723,11 +663,15 @@
         slots = self.receive_rows(arrived, lambda pieces, slot: (pieces, None))
         return [piece for pieces in slots for piece in pieces]
 
-    def gather_direct(self, own):
+    def send_direct(self, own):
         if not self.paired:
             return self.send_rows(own)
-        slots = [self.across(own, step) if step else own for step in range(4)]
-        return [piece for here in slots for piece in (here, self.swap(here))]
+        return [self.across(own, step) if step else own for step in range(4)]
+
+    def direct_pieces(self, arrived):
+        if not self.paired:
+            return arrived
+        return [piece for here in arrived for piece in (here, self.swap(here))]
 
     def chip_sums(self, pieces):
         if not self.paired:
@@ -751,8 +695,8 @@
             self.across(first[:half].astype(low), 1),
             self.across(second[half:].astype(low), 2),
         ]
-        if first_fill is not None:
-            early, first_fill = tied(early, first_fill)
+        if second_fill is not None:
+            early[:2], first_fill = tied(early[:2], first_fill)
         far_top, far_end, first_top, second_end = [part.astype(full) for part in early]
         late = [(second[:half] + far_top).astype(low), (first[half:] + far_end).astype(low)]
         if second_fill is not None:
@@ -942,15 +886,6 @@
 
 def flat_pieces(slots_done):
     return [[piece for pieces in kind for piece in pieces] for kind in zip(*slots_done)]
-
-
-def unit_grads(rows_in, gate, up, weights):
-    gate_weight, up_weight, down = weights
-    grad_hidden = dot_nt(rows_in, down)
-    sigmoid = jax.nn.sigmoid(gate)
-    grad_gate = (grad_hidden * up * (sigmoid * (1.0 + gate * (1.0 - sigmoid)))).astype(low)
-    grad_up = (grad_hidden * (gate * sigmoid)).astype(low)
-    return (grad_gate, grad_up, dot_nn(grad_gate, gate_weight) + dot_nn(grad_up, up_weight))
 
 
 def over_shard(value, axis):
@@ -1043,7 +978,6 @@
             )
 
     saved = []
-    last_branch = None
     for index in range(layer_total):
         last = index + 1 == layer_total
         qkv_weight, out_weight, units_full = weights[index]
@@ -1051,7 +985,10 @@
         scaled_one, inverse_one, arrived = norm_one(index, stream) if index else first_norm
         normed_one = group.receive_pieces(arrived)
         travel = None
-        if group.paired and not last:
+        if last:
+            grad_own, normed_one = tied(own_rows(cotangent), normed_one)
+            travel = group.send_direct(grad_own)
+        elif group.paired:
             travel = group.send_cut(
                 tied(
                     group.cut_layer(sources(index + 1)[:2], *sources(index + 1)[2:]), normed_one
@@ -1074,45 +1011,32 @@
             group.chip_sums([dot_nt(rows_in, out_weight) for rows_in in heads])
         )
         middle = stream + attention
+        if last:
+            (last_branch, units_full), middle = tied(
+                (group.direct_pieces(travel), units_full), middle
+            )
+            gate_weight, up_weight, down = split_units(units_full)
+            weights[index] = (qkv_weight, out_weight, units_full)
         scaled_two, inverse_two, normed_two = norm_parts(
             middle, norm_gain[index, 1], norm_bias[index, 1]
         )
 
         def forward_units(pieces, slot):
-            if group.paired:
-                feeds, gates, ups, hidden = units_call(units_kernel, pieces, units_full)
+            if group.paired and not last:
+                feeds, gates, ups, hidden = units_call(pieces, units_full)
                 return ((pieces, gates, ups, hidden, feeds), feeds)
             gates = [dot_nt(rows_in, gate_weight) for rows_in in pieces]
             ups = [dot_nt(rows_in, up_weight) for rows_in in pieces]
             hidden = [(jax.nn.silu(gate) * up).astype(low) for gate, up in zip(gates, ups)]
-            feeds = [dot_nn(units, down) for units in hidden]
+            feeds = [dot_nn(units, down) for units in hidden if not last]
             return ((pieces, gates, ups, hidden, feeds), hidden)
-
-        def last_units(pieces, slot):
-            size = len(pieces)
-            grads = last_branch[slot * size : (slot + 1) * size]
-            if group.paired:
-                partials, grad_gates, grad_ups, hidden = units_call(
-                    last_units_kernel, (*pieces, *grads), units_full
-                )
-                return ((pieces, grad_gates, grad_ups, hidden, partials), partials)
-            gate, up = dot_nt(pieces[0], gate_weight), dot_nt(pieces[0], up_weight)
-            hidden = (jax.nn.silu(gate) * up).astype(low)
-            grad_gate, grad_up, partial = unit_grads(
-                grads[0], gate, up, (gate_weight, up_weight, down)
-            )
-            return ((pieces, [grad_gate], [grad_up], [hidden], [partial]), None)
 
         arrived = group.send_rows(normed_two.astype(low))
         if last:
-            if last_branch is None:
-                last_branch = group.receive_pieces(group.send_rows(own_rows(cotangent)))
-            slots_done = group.receive_rows(arrived, last_units)
-            normed_two, gates, ups, hidden, last_partials = flat_pieces(slots_done)
+            slots_done = group.receive_rows(arrived, forward_units)
+            normed_two, gates, ups, hidden, feeds = flat_pieces(slots_done)
         else:
             pieces = lax.optimization_barrier(group.receive_pieces(arrived))
-            if index + 2 == layer_total:
-                last_branch = group.gather_direct(tied(own_rows(cotangent), pieces)[0])
             size = len(pieces) // (4 if group.paired else 1)
             slots_done = [
                 forward_units(pieces[i : i + size], i // size)[0]
@@ -1120,11 +1044,10 @@
             ]
             normed_two, gates, ups, hidden, feeds = flat_pieces(slots_done)
             feeds = group.chip_sums(feeds)
-            if index + 2 == layer_total:
-                feeds, last_branch = tied(feeds, last_branch)
+            stream = middle + group.reduce_rows(feeds)
             if group.paired:
-                feeds = tied(feeds, weights[index + 1][0])[0]
-            stream = middle + group.reduce_rows(feeds)
+                stream, heads_full = tied(stream, weights[index + 1][0])
+                weights[index + 1] = split_heads(heads_full) + weights[index + 1][2:]
         saved.append(
             (
                 scaled_one,
@@ -1173,21 +1096,31 @@
         def backward_units(pieces, slot):
             grad_gates, grad_ups, partials = [], [], []
             for place, rows_in in enumerate(pieces, slot * len(pieces)):
-                grad_gate, grad_up, partial = unit_grads(
-                    rows_in, gates[place], ups[place], (gate_weight, up_weight, down)
+                gate, up = gates[place], ups[place]
+                grad_hidden = dot_nt(rows_in, down)
+                sigmoid_gate = jax.nn.sigmoid(gate)
+                grad_gates.append(
+                    (
+                        grad_hidden * up * (sigmoid_gate * (1.0 + gate * (1.0 - sigmoid_gate)))
+                    ).astype(low)
                 )
-                grad_gates.append(grad_gate)
-                grad_ups.append(grad_up)
-                partials.append(partial)
+                grad_ups.append((grad_hidden * (gate * sigmoid_gate)).astype(low))
+                partials.append(
+                    dot_nn(grad_gates[-1], gate_weight) + dot_nn(grad_ups[-1], up_weight)
+                )
             return ((pieces, grad_gates, grad_ups, partials), (grad_gates, grad_ups))
 
         if last:
-            branch, grad_gates, grad_ups, partials = last_branch, gates, ups, last_partials
+            size = len(last_branch) // (4 if group.paired else 1)
+            slots_done = [
+                backward_units(last_branch[i : i + size], i // size)[0]
+                for i in range(0, len(last_branch), size)
+            ]
         else:
             slots_done = group.receive_rows(
                 group.send_rows(grad_stream.astype(low)), backward_units
             )
-            branch, grad_gates, grad_ups, partials = flat_pieces(slots_done)
+        branch, grad_gates, grad_ups, partials = flat_pieces(slots_done)
         sums = group.chip_sums(partials)
         (branch, grad_gates, grad_ups, hidden), unused = tied(
             (branch, grad_gates, grad_ups, hidden), sums

time: 1240 us -> 1190 us (0.960)
  waiting for transfers between devices: 441 us -> 370 us
  Pallas kernels: 395 us -> 331 us
  matrix products: 97.9 us -> 161 us
  local copies, waits for them, and re-layouts: 56.7 us -> 77.1 us
    pallas_call x8 -> x4, Pallas kernels: 109 us -> 42.9 us  [units_call(): pl.pallas_call(units_kernel, in_specs=[inside] * 2 + [pl.BlockSpec(memory...]
    ppermute x94, waiting for transfers between devices: 398 us -> 345 us  [across(): lax.ppermute(value, 'ctx', [(i, i ^ step) for i in range(self.ctx_count)])]
    dot_general x40 -> x64, matrix products: 49 us -> 94.5 us  [dot_nt(): lax.dot_general(left, right, (((1,), (1,)), ((), ())), preferred_element_...]
    dot_general x40 -> x56, matrix products: 48.9 us -> 66.7 us  [dot_nn(): lax.dot_general(left, right, (((1,), (0,)), ((), ())), preferred_element_...]
    unnamed x483 -> x479, local copies, waits for them, and re-layouts: 32.3 us -> 38.4 us
  transfers between devices with their start and end apart: 175 -> 175, of which waited for: 74 -> 65; matrix products, arithmetic and copies ran while one was open for 16% -> 24% of each run, Pallas kernels for 32% -> 28%
where the time goes in v2:
time: 1190 us; the launch traced here: 1180 us
  waiting for transfers between devices  370 us (31%)
  Pallas kernels  331 us (28%)
  matrix products  161 us (14%)
  starting transfers between devices  132 us (11%)
  other arithmetic  89.7 us (8%)
  local copies, waits for them, and re-layouts  77.1 us (6%)
  between operations  19 us (2%)
    ppermute x94, waiting for transfers between devices, across(): lax.ppermute(value, 'ctx', [(i, i ^ step) for i in range(self.ctx_count)])  345 us
    ppermute x94, starting transfers between devices, across(): lax.ppermute(value, 'ctx', [(i, i ^ step) for i in range(self.ctx_count)])  108 us
    dot_general x64, matrix products, dot_nt(): lax.dot_general(left, right, (((1,), (1,)), ((), ())), preferred_element_...  94.5 us
    pallas_call x6, Pallas kernels, weight_grads(): pl.pallas_call(kernel, grid=(features // block,), in_specs=[pl.BlockSpec(...  94.2 us
    pallas_call x2, Pallas kernels, attend_back(): pl.pallas_call(functools.partial(attend_back_kernel, ctx_count, tp_count,...  91 us
    pallas_call x2, Pallas kernels, attend(): pl.pallas_call(functools.partial(attend_kernel, ctx_count, tp_count, slot...  85.8 us
    dot_general x56, matrix products, dot_nn(): lax.dot_general(left, right, (((1,), (0,)), ((), ())), preferred_element_...  66.7 us
    pallas_call x4, Pallas kernels, units_call(): pl.pallas_call(units_kernel, in_specs=[inside] * 2 + [pl.BlockSpec(memory...  42.9 us
  transfers between devices with their start and end apart: 175, of which 65 were waited for; matrix products, arithmetic and copies ran while one was open for 24% of the time, Pallas kernels for 28%

profile of v2, /device:TPU:8, one launch (start us, length us, event | category | flops | bytes accessed | tf_op | source)
XLA Modules:
  0.0 1179.6 jit_solution(11727896018787592657)
XLA Ops:
  21.5 4.5 collective-permute-done.8.refs_1_
  39.6 15.4 %collective-permute-done.1.refs_2_.refs_18_ = bf16[256,2048]{1,0:T(8,128)(2,1)} collective-permute-done((bf16[256,2048]{1,0:T(8,128)(2,1)}, bf16[256,2048]{1,0:T(8,128)(2,1)}, u32[]{:S(2)}, u32[]{:S(2)}) %collective-permute-start.1) | collective-permute-done | bytes 1048608 | tf_op jit(solution)/shard_map/ppermute | solution.py:633
  70.6 5.2 collective-permute-done.32.refs_1_
  75.8 17.8 %collective-permute-done.33.refs_2_ = bf16[2112,128]{1,0:T(8,128)(2,1)} collective-permute-done((bf16[2112,128]{1,0:T(8,128)(2,1)}, bf16[2112,128]{1,0:T(8,128)(2,1)}, u32[]{:S(2)}, u32[]{:S(2)}) %collective-permute-start.33) | collective-permute-done | bytes 540704 | tf_op jit(solution)/shard_map/ppermute | solution.py:633
  101.6 5.5 fusion.40
  114.2 43.1 %attend.2 = (bf16[256,256]{1,0:T(8,128)(2,1)S(1)}, bf16[256,256]{1,0:T(8,128)(2,1)S(1)}, bf16[256,256]{1,0:T(8,128)(2,1)S(1)}, bf16[256,256]{1,0:T(8,128)(2,1)S(...) custom-call(s32[8]{0:T(128)S(1)} %fusion.122.order_ref, ...), custom_call_target="tpu_custom_call" | custom-call | flops 34359738368 | tf_op jit(solution)/shard_map/attend/pallas_call | solution.py:293
  173.2 8.5 collective-permute-done.19
  186.0 6.9 collective-permute-done.16
  192.9 14.2 %collective-permute-done.20 = bf16[128,2048]{1,0:T(8,128)(2,1)S(1)} collective-permute-done((bf16[128,2048]{1,0:T(8,128)(2,1)S(1)}, bf16[128,2048]{1,0:T(8,128)(2,1)S(1)}, u32[]{:S(2)}, u32[]{:S(2)}) %collective-permute-start.20) | collective-permute-done | bytes 524320 | tf_op jit(solution)/shard_map/ppermute | solution.py:633
  211.7 22.3 %collective-permute-done.25.mine_in.refs_18_.refs_26_ = bf16[256,2048]{1,0:T(8,128)(2,1)S(1)} collective-permute-done((bf16[256,2048]{1,0:T(8,128)(2,1)S(1)}, bf16[256,2048]{1,0:T(8,128)(2,1)S(1)}, u32[]{:S(2)}, u32[]{:S(2)}) %collective-permute-start.25) | collective-permute-done | bytes 1048608 | tf_op jit(solution)/shard_map/ppermute | solution.py:633
  238.1 9.7 collective-permute-done.29
  252.7 8.3 all-gather.7.cloned.1.call-done.weights_hbm
  262.1 10.4 units.7
  277.7 10.4 units.5
  293.8 10.7 units.4
  307.0 11.3 units.6
  325.9 8.5 collective-permute-done.40
  339.8 6.0 collective-permute-done.37
  345.8 14.2 %collective-permute-done.41 = bf16[128,2048]{1,0:T(8,128)(2,1)} collective-permute-done((bf16[128,2048]{1,0:T(8,128)(2,1)}, bf16[128,2048]{1,0:T(8,128)(2,1)}, u32[]{:S(2)}, u32[]{:S(2)}) %collective-permute-start.41) | collective-permute-done | bytes 524320 | tf_op jit(solution)/shard_map/ppermute | solution.py:633
  373.3 22.4 %collective-permute-done.46.refs_2_.refs_18_ = bf16[256,2048]{1,0:T(8,128)(2,1)S(1)} collective-permute-done((bf16[256,2048]{1,0:T(8,128)(2,1)S(1)}, bf16[256,2048]{1,0:T(8,128)(2,1)S(1)}, u32[]{:S(2)}, u32[]{:S(2)}) %collective-permute-start.46) | collective-permute-done | bytes 1048608 | tf_op jit(solution)/shard_map/ppermute | solution.py:633
  398.6 9.6 collective-permute-done.50
  415.9 42.7 %attend.3 = (bf16[256,256]{1,0:T(8,128)(2,1)S(1)}, bf16[256,256]{1,0:T(8,128)(2,1)S(1)}, bf16[256,256]{1,0:T(8,128)(2,1)S(1)}, bf16[256,256]{1,0:T(8,128)(2,1)S(...) custom-call(s32[8]{0:T(128)S(1)} %fusion.122.order_ref, ...), custom_call_target="tpu_custom_call" | custom-call | flops 34359738368 | tf_op jit(solution)/shard_map/attend/pallas_call | solution.py:293
  470.1 9.2 collective-permute-done.65
  484.2 6.3 collective-permute-done.62
  493.5 10.1 collective-permute-done.66
  595.9 11.4 weight_grads.6.refs_32_
  608.5 6.4 collective-permute-done.84
  620.0 19.9 %weight_grads.7 = bf16[2112,2048]{1,0:T(8,128)(2,1)} custom-call(bf16[256,704]{1,0:T(8,128)(2,1)} %copy-done.127, bf16[256,704]{1,0:T(8,128)(2,1)} %copy-done.133, bf16[256,704]{1,0:T(8,128)(2,1)} %copy-done.128, bf16[256,704]{1,0:T(8,128)(2,1)} %copy-done.135, bf16[256,704]{1,0:T(8,128)(2,1)} %copy-done.130, ...), custom_call_target="tpu_custom_call", output_to_operand_aliasing={{}: (32, {})} | custom-call | flops 11811160064 | bytes 11534336 | tf_op jit(solution)/shard_map/weight_grads/pallas_call | solution.py:480
  669.1 13.3 %collective-permute-done.89.refs_26_ = bf16[256,2048]{1,0:T(8,128)(2,1)S(1)} collective-permute-done((bf16[256,2048]{1,0:T(8,128)(2,1)S(1)}, bf16[256,2048]{1,0:T(8,128)(2,1)S(1)}, u32[]{:S(2)}, u32[]{:S(2)}) %collective-permute-start.89) | collective-permute-done | bytes 1048608 | tf_op jit(solution)/shard_map/ppermute | solution.py:633
  686.4 9.1 collective-permute-done.93
  704.2 45.5 %attend_back.2 = (bf16[256,768]{1,0:T(8,128)(2,1)S(1)}, bf16[256,768]{1,0:T(8,128)(2,1)}, bf16[256,768]{1,0:T(8,128)(2,1)}, bf16[256,768]{1,0:T(8,128)(2,1)}, bf...) custom-call(s32[8]{0:T(128)S(1)} %fusion.122.order_ref, ...), custom_call_target="tpu_custom_call" | custom-call | flops 34359738368 | tf_op jit(solution)/shard_map/attend_back/pallas_call | solution.py:332
  766.7 6.8 collective-permute-done.109
  778.4 15.3 %weight_grads.8 = bf16[1024,2048]{1,0:T(8,128)(2,1)} custom-call(bf16[256,768]{1,0:T(8,128)(2,1)} %copy-done.34, bf16[256,768]{1,0:T(8,128)(2,1)} %get-tuple-element.556.refs_1_, bf16[256,768]{1,0:T(8,128)(2,1)} %get-tuple-element.557.refs_2_, bf16[256,768]{1,0:T(8,128)(2,1)} %get-tuple-element.558.refs_3_, bf16[256,768]{1,0:T(8,128)(2,1)} %get-tuple-element.559.refs_4_, ...), custom_call_target="tpu_custom_call" | custom-call | flops 8589934592 | bytes 8388608 | tf_op jit(solution)/shard_map/weight_grads/pallas_call | solution.py:480
  825.0 12.5 %collective-permute-done.116.refs_10_ = bf16[256,2048]{1,0:T(8,128)(2,1)S(1)} collective-permute-done((bf16[256,2048]{1,0:T(8,128)(2,1)}, bf16[256,2048]{1,0:T(8,128)(2,1)S(1)}, u32[]{:S(2)}, u32[]{:S(2)}) %collective-permute-start.116) | collective-permute-done | bytes 1048608 | tf_op jit(solution)/shard_map/ppermute | solution.py:633
  844.3 7.7 collective-permute-done.123
  878.9 11.8 %weight_grads.9.refs_32_ = bf16[2112,2048]{1,0:T(8,128)(2,1)} custom-call(bf16[256,704]{1,0:T(8,128)(2,1)} %copy-done.70, bf16[256,704]{1,0:T(8,128)(2,1)} %copy-done.71, bf16[256,704]{1,0:T(8,128)(2,1)} %copy-done.68, bf16[256,704]{1,0:T(8,128)(2,1)} %copy-done.69, bf16[256,704]{1,0:T(8,128)(2,1)} %copy-done.72, bf16[256,704]{1,0:T(8,128)(2,1)} %copy-done.73, ...), custom_call_target="tpu_custom_call" | custom-call | flops 5905580032 | bytes 5767168 | tf_op jit(solution)/shard_map/weight_grads/pallas_call | solution.py:480
  895.7 20.2 %weight_grads.10 = bf16[2112,2048]{1,0:T(8,128)(2,1)} custom-call(bf16[256,704]{1,0:T(8,128)(2,1)} %copy-done.105, bf16[256,704]{1,0:T(8,128)(2,1)} %copy-done.108, bf16[256,704]{1,0:T(8,128)(2,1)} %copy-done.129, bf16[256,704]{1,0:T(8,128)(2,1)} %copy-done.136, bf16[256,704]{1,0:T(8,128)(2,1)} %copy-done.106, ...), custom_call_target="tpu_custom_call", output_to_operand_aliasing={{}: (32, {})} | custom-call | flops 11811160064 | bytes 11534336 | tf_op jit(solution)/shard_map/weight_grads/pallas_call | solution.py:480
  919.4 9.2 collective-permute-done.119
  939.7 17.4 %collective-permute-done.133.refs_26_ = bf16[256,2048]{1,0:T(8,128)(2,1)} collective-permute-done((bf16[256,2048]{1,0:T(8,128)(2,1)S(1)}, bf16[256,2048]{1,0:T(8,128)(2,1)}, u32[]{:S(2)}, u32[]{:S(2)}) %collective-permute-start.133) | collective-permute-done | bytes 1048608 | tf_op jit(solution)/shard_map/ppermute | solution.py:633
  978.9 45.5 %attend_back.3 = (bf16[256,768]{1,0:T(8,128)(2,1)S(1)}, bf16[256,768]{1,0:T(8,128)(2,1)}, bf16[256,768]{1,0:T(8,128)(2,1)}, bf16[256,768]{1,0:T(8,128)(2,1)}, bf...) custom-call(s32[8]{0:T(128)S(1)} %fusion.122.order_ref, ...), custom_call_target="tpu_custom_call" | custom-call | flops 34359738368 | tf_op jit(solution)/shard_map/attend_back/pallas_call | solution.py:332
  1035.1 9.9 collective-permute-done.148
  1049.5 15.5 %weight_grads.11 = bf16[1024,2048]{1,0:T(8,128)(2,1)} custom-call(bf16[256,768]{1,0:T(8,128)(2,1)} %copy-done.32, bf16[256,768]{1,0:T(8,128)(2,1)} %get-tuple-element.692.refs_1_, bf16[256,768]{1,0:T(8,128)(2,1)} %get-tuple-element.693.refs_2_, bf16[256,768]{1,0:T(8,128)(2,1)} %get-tuple-element.694.refs_3_, bf16[256,768]{1,0:T(8,128)(2,1)} %get-tuple-element.695.refs_4_, ...), custom_call_target="tpu_custom_call" | custom-call | flops 8589934592 | bytes 8388608 | tf_op jit(solution)/shard_map/weight_grads/pallas_call | solution.py:480
  1065.2 5.0 add_convert_fusion
  1076.9 9.0 collective-permute-done.145
  1096.5 4.3 fusion.36
  1126.6 4.7 maximum_select_fusion.1
  1138.5 6.5 collective-permute-done.162.refs_2_
  1150.3 6.7 maximum_select_fusion
  (1120 shorter events, 513.4 us)
Async XLA Ops:
  7.2 105.2 %all-gather.5.cloned.1.call-start = ((), (), s32[]{:S(2)}) async-start(), calls=%async_computation.4 | async-start | bytes 5242880 | tf_op jit(solution)/shard_map/all_gather | solution.py:892
  27.3 233.7 %all-gather.7.cloned.1.call-start = ((), (), s32[]{:S(2)}) async-start(), calls=%async_computation.5 | async-start | bytes 10813440 | tf_op jit(solution)/shard_map/all_gather | solution.py:892
  31.6 27.3 %collective-permute-start.3 = (bf16[256,2048]{1,0:T(8,128)(2,1)}, bf16[256,2048]{1,0:T(8,128)(2,1)}, u32[]{:S(2)}, u32[]{:S(2)}) collective-permute-start(bf16[256,2048]{1,0:T(8,128)(2,1)} %fusion.32.refs_0_.refs_16_), channel_id=1, source_target_pairs={{0,4},{2,6},{4,0},{6,2},{1,5},{3,7},{5,1},{7,3},{8,12},{10,14},{12... | collective-permute-start | bytes 3145736 | tf_op jit(solution)/shard_map/ppermute | solution.py:633
  56.8 40.7 %collective-permute-start.5 = (bf16[128,2048]{1,0:T(8,128)(2,1)}, bf16[128,2048]{1,0:T(8,128)(2,1)}, u32[]{:S(2)}, u32[]{:S(2)}) collective-permute-start(bf16[128,2048]{1,0:T(8,128)(2,1)} %slice.426), channel_id=1, source_target_pairs={{0,4},{2,6},{4,0},{6,2},{1,5},{3,7},{5,1},{7,3},{8,12},{10,14},{12... | collective-permute-start | bytes 1572872 | tf_op jit(solution)/shard_map/ppermute | solution.py:633
  61.8 31.9 %collective-permute-start.33 = (bf16[2112,128]{1,0:T(8,128)(2,1)}, bf16[2112,128]{1,0:T(8,128)(2,1)}, u32[]{:S(2)}, u32[]{:S(2)}) collective-permute-start(bf16[2112,128]{1,0:T(8,128)(2,1)} %get-tuple-element.795), channel_id=1, source_target_pairs={{0,4},{2,6},{4,0},{6,2},{1,5},{3,7},{5,1},{7,3},{8,12},{10,14},{12... | collective-permute-start | bytes 1622024 | tf_op jit(solution)/shard_map/ppermute | solution.py:633
  61.8 31.9 %collective-permute-start.34 = (bf16[2112,128]{1,0:T(8,128)(2,1)}, bf16[2112,128]{1,0:T(8,128)(2,1)}, u32[]{:S(2)}, u32[]{:S(2)}) collective-permute-start(bf16[2112,128]{1,0:T(8,128)(2,1)} %get-tuple-element.794), channel_id=1, source_target_pairs={{0,6},{2,4},{4,2},{6,0},{1,7},{3,5},{5,3},{7,1},{8,14},{10,12},{12... | collective-permute-start | bytes 1622024 | tf_op jit(solution)/shard_map/ppermute | solution.py:633
  69.1 29.5 %collective-permute-start.6 = (bf16[128,2048]{1,0:T(8,128)(2,1)}, bf16[128,2048]{1,0:T(8,128)(2,1)}, u32[]{:S(2)}, u32[]{:S(2)}) collective-permute-start(bf16[128,2048]{1,0:T(8,128)(2,1)} %slice.427), channel_id=1, source_target_pairs={{0,2},{2,0},{4,6},{6,4},{1,3},{3,1},{5,7},{7,5},{8,10},{10,8},{12,... | collective-permute-start | bytes 1572872 | tf_op jit(solution)/shard_map/ppermute | solution.py:633
  75.8 31.3 %collective-permute-start = (bf16[256,2048]{1,0:T(8,128)(2,1)}, bf16[256,2048]{1,0:T(8,128)(2,1)}, u32[]{:S(2)}, u32[]{:S(2)}) collective-permute-start(bf16[256,2048]{1,0:T(8,128)(2,1)} %fusion.32.refs_0_.refs_16_), channel_id=1, source_target_pairs={{0,1},{1,0},{2,3},{3,2},{4,5},{5,4},{6,7},{7,6},{8,9},{9,8},{10,11... | collective-permute-start | bytes 3145736 | tf_op jit(solution)/shard_map/ppermute | solution.py:636
  97.3 268.7 %all-gather.9.cloned.1.call-start = ((), (), s32[]{:S(2)}) async-start(), calls=%async_computation.6 | async-start | bytes 5242880 | tf_op jit(solution)/shard_map/all_gather | solution.py:892
  108.9 48.5 %collective-permute-start.11 = (bf16[3136,128]{1,0:T(8,128)(2,1)}, bf16[3136,128]{1,0:T(8,128)(2,1)S(1)}, u32[]{:S(2)}, u32[]{:S(2)}) collective-permute-start(bf16[3136,128]{1,0:T(8,128)(2,1)} %get-tuple-element.786), channel_id=1, source_target_pairs={{0,2},{2,0},{4,6},{6,4},{1,3},{3,1},{5,7},{7,5},{8,10},{10,8},{12,... | collective-permute-start | bytes 2408456 | tf_op jit(solution)/shard_map/ppermute | solution.py:633
  110.4 47.0 %collective-permute-start.12 = (bf16[3136,128]{1,0:T(8,128)(2,1)}, bf16[3136,128]{1,0:T(8,128)(2,1)S(1)}, u32[]{:S(2)}, u32[]{:S(2)}) collective-permute-start(bf16[3136,128]{1,0:T(8,128)(2,1)} %get-tuple-element.785), channel_id=1, source_target_pairs={{0,4},{2,6},{4,0},{6,2},{1,5},{3,7},{5,1},{7,3},{8,12},{10,14},{12... | collective-permute-start | bytes 2408456 | tf_op jit(solution)/shard_map/ppermute | solution.py:633
  112.1 45.3 %collective-permute-start.13 = (bf16[3136,128]{1,0:T(8,128)(2,1)}, bf16[3136,128]{1,0:T(8,128)(2,1)S(1)}, u32[]{:S(2)}, u32[]{:S(2)}) collective-permute-start(bf16[3136,128]{1,0:T(8,128)(2,1)} %get-tuple-element.784), channel_id=1, source_target_pairs={{0,6},{2,4},{4,2},{6,0},{1,7},{3,5},{5,3},{7,1},{8,14},{10,12},{12... | collective-permute-start | bytes 2408456 | tf_op jit(solution)/shard_map/ppermute | solution.py:633
  164.0 43.3 %collective-permute-start.14 = (bf16[256,2048]{1,0:T(8,128)(2,1)S(1)}, bf16[256,2048]{1,0:T(8,128)(2,1)S(1)}, u32[]{:S(2)}, u32[]{:S(2)}) collective-permute-start(bf16[256,2048]{1,0:T(8,128)(2,1)S(1)} %convolution_convert_fusion.11), channel_id=1, source_target_pairs={{0,1},{1,0},{2,3},{3,2},{4,5},{5,4},{6,7},{7,6},{8,9},{9,8},{10,11... | collective-permute-start | bytes 3145736 | tf_op jit(solution)/shard_map/ppermute | solution.py:636
  173.0 34.2 %collective-permute-start.23 = (bf16[128,2048]{1,0:T(8,128)(2,1)S(1)}, bf16[128,2048]{1,0:T(8,128)(2,1)S(1)}, u32[]{:S(2)}, u32[]{:S(2)}) collective-permute-start(bf16[128,2048]{1,0:T(8,128)(2,1)S(1)} %slice.817), channel_id=1, source_target_pairs={{0,4},{2,6},{4,0},{6,2},{1,5},{3,7},{5,1},{7,3},{8,12},{10,14},{12... | collective-permute-start | bytes 1572872 | tf_op jit(solution)/shard_map/ppermute | solution.py:633
  181.8 25.3 %collective-permute-start.20 = (bf16[128,2048]{1,0:T(8,128)(2,1)S(1)}, bf16[128,2048]{1,0:T(8,128)(2,1)S(1)}, u32[]{:S(2)}, u32[]{:S(2)}) collective-permute-start(bf16[128,2048]{1,0:T(8,128)(2,1)S(1)} %fusion.54), channel_id=1, source_target_pairs={{0,4},{2,6},{4,0},{6,2},{1,5},{3,7},{5,1},{7,3},{8,12},{10,14},{12... | collective-permute-start | bytes 1572872 | tf_op jit(solution)/shard_map/ppermute | solution.py:633
  210.0 27.0 %collective-permute-start.27 = (bf16[256,2048]{1,0:T(8,128)(2,1)S(1)}, bf16[256,2048]{1,0:T(8,128)(2,1)S(1)}, u32[]{:S(2)}, u32[]{:S(2)}) collective-permute-start(bf16[256,2048]{1,0:T(8,128)(2,1)S(1)} %add_convert_fusion.4.mine_in.refs_16_.refs_24_), channel_id=1, source_target_pairs={{0,4},{2,6},{4,0},{6,2},{1,5},{3,7},{5,1},{7,3},{8,12},{10,14},{12... | collective-permute-start | bytes 3145736 | tf_op jit(solution)/shard_map/ppermute | solution.py:633
  236.6 269.8 %all-gather.11.cloned.1.call-start = ((), (), s32[]{:S(2)}) async-start(), calls=%async_computation.7 | async-start | bytes 10813440 | tf_op jit(solution)/shard_map/all_gather | solution.py:892
  277.7 41.3 %collective-permute-start.39 = (bf16[256,2048]{1,0:T(8,128)(2,1)S(1)}, bf16[256,2048]{1,0:T(8,128)(2,1)S(1)}, u32[]{:S(2)}, u32[]{:S(2)}) collective-permute-start(bf16[256,2048]{1,0:T(8,128)(2,1)S(1)} %get-tuple-element.415), channel_id=1, source_target_pairs={{0,1},{1,0},{2,3},{3,2},{4,5},{5,4},{6,7},{7,6},{8,9},{9,8},{10,11... | collective-permute-start | bytes 3145736 | tf_op jit(solution)/shard_map/ppermute | solution.py:636
  293.3 28.2 %collective-permute-start.36 = (bf16[256,2048]{1,0:T(8,128)(2,1)S(1)}, bf16[256,2048]{1,0:T(8,128)(2,1)S(1)}, u32[]{:S(2)}, u32[]{:S(2)}) collective-permute-start(bf16[256,2048]{1,0:T(8,128)(2,1)S(1)} %get-tuple-element.407), channel_id=1, source_target_pairs={{0,1},{1,0},{2,3},{3,2},{4,5},{5,4},{6,7},{7,6},{8,9},{9,8},{10,11... | collective-permute-start | bytes 3145736 | tf_op jit(solution)/shard_map/ppermute | solution.py:636
  306.9 55.8 %collective-permute-start.35 = (bf16[256,2048]{1,0:T(8,128)(2,1)}, bf16[256,2048]{1,0:T(8,128)(2,1)}, u32[]{:S(2)}, u32[]{:S(2)}) collective-permute-start(bf16[256,2048]{1,0:T(8,128)(2,1)} %get-tuple-element.403), channel_id=1, source_target_pairs={{0,1},{1,0},{2,3},{3,2},{4,5},{5,4},{6,7},{7,6},{8,9},{9,8},{10,11... | collective-permute-start | bytes 3145736 | tf_op jit(solution)/shard_map/ppermute | solution.py:636
  325.3 36.0 %collective-permute-start.44 = (bf16[128,2048]{1,0:T(8,128)(2,1)S(1)}, bf16[128,2048]{1,0:T(8,128)(2,1)}, u32[]{:S(2)}, u32[]{:S(2)}) collective-permute-start(bf16[128,2048]{1,0:T(8,128)(2,1)S(1)} %slice.815), channel_id=1, source_target_pairs={{0,4},{2,6},{4,0},{6,2},{1,5},{3,7},{5,1},{7,3},{8,12},{10,14},{12... | collective-permute-start | bytes 1572872 | tf_op jit(solution)/shard_map/ppermute | solution.py:633
  339.7 463.4 %reduce-scatter.5.cloned.1.call-start = ((), (), s32[]{:S(2)}) async-start(), calls=%async_computation.8 | async-start | bytes 10813440 | tf_op jit(solution)/shard_map/reduce_scatter | solution.py:896
  371.7 25.6 %collective-permute-start.48 = (bf16[256,2048]{1,0:T(8,128)(2,1)S(1)}, bf16[256,2048]{1,0:T(8,128)(2,1)S(1)}, u32[]{:S(2)}, u32[]{:S(2)}) collective-permute-start(bf16[256,2048]{1,0:T(8,128)(2,1)S(1)} %add_convert_fusion.2.refs_0_.refs_16_), channel_id=1, source_target_pairs={{0,4},{2,6},{4,0},{6,2},{1,5},{3,7},{5,1},{7,3},{8,12},{10,14},{12... | collective-permute-start | bytes 3145736 | tf_op jit(solution)/shard_map/ppermute | solution.py:633
  412.3 46.3 %collective-permute-start.53 = (bf16[256,2048]{1,0:T(8,128)(2,1)}, bf16[256,2048]{1,0:T(8,128)(2,1)}, u32[]{:S(2)}, u32[]{:S(2)}) collective-permute-start(bf16[256,2048]{1,0:T(8,128)(2,1)} %constant_dynamic-slice_fusion.21.refs_8_), channel_id=1, source_target_pairs={{0,2},{2,0},{4,6},{6,4},{1,3},{3,1},{5,7},{7,5},{8,10},{10,8},{12,... | collective-permute-start | bytes 3145736 | tf_op jit(solution)/shard_map/ppermute | solution.py:633
  413.0 47.7 %collective-permute-start.54 = (bf16[256,2048]{1,0:T(8,128)(2,1)}, bf16[256,2048]{1,0:T(8,128)(2,1)}, u32[]{:S(2)}, u32[]{:S(2)}) collective-permute-start(bf16[256,2048]{1,0:T(8,128)(2,1)} %constant_dynamic-slice_fusion.21.refs_8_), channel_id=1, source_target_pairs={{0,4},{2,6},{4,0},{6,2},{1,5},{3,7},{5,1},{7,3},{8,12},{10,14},{12... | collective-permute-start | bytes 3145736 | tf_op jit(solution)/shard_map/ppermute | solution.py:633
  414.0 46.7 %collective-permute-start.55 = (bf16[256,2048]{1,0:T(8,128)(2,1)}, bf16[256,2048]{1,0:T(8,128)(2,1)}, u32[]{:S(2)}, u32[]{:S(2)}) collective-permute-start(bf16[256,2048]{1,0:T(8,128)(2,1)} %constant_dynamic-slice_fusion.21.refs_8_), channel_id=1, source_target_pairs={{0,6},{2,4},{4,2},{6,0},{1,7},{3,5},{5,3},{7,1},{8,14},{10,12},{12... | collective-permute-start | bytes 3145736 | tf_op jit(solution)/shard_map/ppermute | solution.py:633
  512.7 25.4 %collective-permute-start.72 = (bf16[256,2048]{1,0:T(8,128)(2,1)S(1)}, bf16[256,2048]{1,0:T(8,128)(2,1)S(1)}, u32[]{:S(2)}, u32[]{:S(2)}) collective-permute-start(bf16[256,2048]{1,0:T(8,128)(2,1)S(1)} %add_convert_fusion.1.refs_16_.refs_24_), channel_id=1, source_target_pairs={{0,2},{2,0},{4,6},{6,4},{1,3},{3,1},{5,7},{7,5},{8,10},{10,8},{12,... | collective-permute-start | bytes 3145736 | tf_op jit(solution)/shard_map/ppermute | solution.py:633
  513.7 27.3 %collective-permute-start.76 = (bf16[256,2048]{1,0:T(8,128)(2,1)S(1)}, bf16[256,2048]{1,0:T(8,128)(2,1)S(1)}, u32[]{:S(2)}, u32[]{:S(2)}) collective-permute-start(bf16[256,2048]{1,0:T(8,128)(2,1)S(1)} %add_convert_fusion.1.refs_16_.refs_24_), channel_id=1, source_target_pairs={{0,4},{2,6},{4,0},{6,2},{1,5},{3,7},{5,1},{7,3},{8,12},{10,14},{12... | collective-permute-start | bytes 3145736 | tf_op jit(solution)/shard_map/ppermute | solution.py:633
  577.1 73.0 %collective-permute-start.75 = (bf16[128,2048]{1,0:T(8,128)(2,1)S(1)}, bf16[128,2048]{1,0:T(8,128)(2,1)}, u32[]{:S(2)}, u32[]{:S(2)}) collective-permute-start(bf16[128,2048]{1,0:T(8,128)(2,1)S(1)} %slice.812), channel_id=1, source_target_pairs={{0,2},{2,0},{4,6},{6,4},{1,3},{3,1},{5,7},{7,5},{8,10},{10,8},{12,... | collective-permute-start | bytes 1572872 | tf_op jit(solution)/shard_map/ppermute | solution.py:633
  588.9 63.1 %collective-permute-start.87 = (bf16[128,2048]{1,0:T(8,128)(2,1)}, bf16[128,2048]{1,0:T(8,128)(2,1)}, u32[]{:S(2)}, u32[]{:S(2)}) collective-permute-start(bf16[128,2048]{1,0:T(8,128)(2,1)} %slice.811), channel_id=1, source_target_pairs={{0,4},{2,6},{4,0},{6,2},{1,5},{3,7},{5,1},{7,3},{8,12},{10,14},{12... | collective-permute-start | bytes 1572872 | tf_op jit(solution)/shard_map/ppermute | solution.py:633
  640.0 296.7 %reduce-scatter.7.cloned.1.call-start = ((), (), s32[]{:S(2)}) async-start(), calls=%async_computation.9 | async-start | bytes 5242880 | tf_op jit(solution)/shard_map/reduce_scatter | solution.py:896
  661.7 34.8 %collective-permute-start.88 = (bf16[256,2048]{1,0:T(8,128)(2,1)S(1)}, bf16[256,2048]{1,0:T(8,128)(2,1)S(1)}, u32[]{:S(2)}, u32[]{:S(2)}) collective-permute-start(bf16[256,2048]{1,0:T(8,128)(2,1)S(1)} %get-tuple-element.563.refs_24_), channel_id=1, source_target_pairs={{0,1},{1,0},{2,3},{3,2},{4,5},{5,4},{6,7},{7,6},{8,9},{9,8},{10,11... | collective-permute-start | bytes 3145736 | tf_op jit(solution)/shard_map/ppermute | solution.py:636
  700.6 49.0 %collective-permute-start.100 = (bf16[256,2048]{1,0:T(8,128)(2,1)}, bf16[256,2048]{1,0:T(8,128)(2,1)S(1)}, u32[]{:S(2)}, u32[]{:S(2)}) collective-permute-start(bf16[256,2048]{1,0:T(8,128)(2,1)} %convolution_add_fusion.18), channel_id=1, source_target_pairs={{0,2},{2,0},{4,6},{6,4},{1,3},{3,1},{5,7},{7,5},{8,10},{10,8},{12,... | collective-permute-start | bytes 3145736 | tf_op jit(solution)/shard_map/ppermute | solution.py:633
  701.9 47.8 %collective-permute-start.101 = (bf16[256,2048]{1,0:T(8,128)(2,1)}, bf16[256,2048]{1,0:T(8,128)(2,1)S(1)}, u32[]{:S(2)}, u32[]{:S(2)}) collective-permute-start(bf16[256,2048]{1,0:T(8,128)(2,1)} %convolution_add_fusion.17), channel_id=1, source_target_pairs={{0,4},{2,6},{4,0},{6,2},{1,5},{3,7},{5,1},{7,3},{8,12},{10,14},{12... | collective-permute-start | bytes 3145736 | tf_op jit(solution)/shard_map/ppermute | solution.py:633
  702.9 46.8 %collective-permute-start.102 = (bf16[256,2048]{1,0:T(8,128)(2,1)}, bf16[256,2048]{1,0:T(8,128)(2,1)S(1)}, u32[]{:S(2)}, u32[]{:S(2)}) collective-permute-start(bf16[256,2048]{1,0:T(8,128)(2,1)} %convolution_add_fusion.16), channel_id=1, source_target_pairs={{0,6},{2,4},{4,2},{6,0},{1,7},{3,5},{5,3},{7,1},{8,14},{10,12},{12... | collective-permute-start | bytes 3145736 | tf_op jit(solution)/shard_map/ppermute | solution.py:633
  757.0 41.8 %collective-permute-start.104 = (bf16[256,2048]{1,0:T(8,128)(2,1)}, bf16[256,2048]{1,0:T(8,128)(2,1)S(1)}, u32[]{:S(2)}, u32[]{:S(2)}) collective-permute-start(bf16[256,2048]{1,0:T(8,128)(2,1)} %convolution_convert_fusion.19), channel_id=1, source_target_pairs={{0,1},{1,0},{2,3},{3,2},{4,5},{5,4},{6,7},{7,6},{8,9},{9,8},{10,11... | collective-permute-start | bytes 3145736 | tf_op jit(solution)/shard_map/ppermute | solution.py:636
  762.9 33.3 %collective-permute-start.106 = (bf16[128,2048]{1,0:T(8,128)(2,1)}, bf16[128,2048]{1,0:T(8,128)(2,1)}, u32[]{:S(2)}, u32[]{:S(2)}) collective-permute-start(bf16[128,2048]{1,0:T(8,128)(2,1)} %slice.810), channel_id=1, source_target_pairs={{0,2},{2,0},{4,6},{6,4},{1,3},{3,1},{5,7},{7,5},{8,10},{10,8},{12,... | collective-permute-start | bytes 1572872 | tf_op jit(solution)/shard_map/ppermute | solution.py:633
  765.7 31.8 %collective-permute-start.113 = (bf16[128,2048]{1,0:T(8,128)(2,1)}, bf16[128,2048]{1,0:T(8,128)(2,1)}, u32[]{:S(2)}, u32[]{:S(2)}) collective-permute-start(bf16[128,2048]{1,0:T(8,128)(2,1)} %slice.809), channel_id=1, source_target_pairs={{0,4},{2,6},{4,0},{6,2},{1,5},{3,7},{5,1},{7,3},{8,12},{10,14},{12... | collective-permute-start | bytes 1572872 | tf_op jit(solution)/shard_map/ppermute | solution.py:633
  811.2 282.2 %reduce-scatter.9.cloned.1.call-start = ((), (), s32[]{:S(2)}) async-start(), calls=%async_computation.10 | async-start | bytes 10813440 | tf_op jit(solution)/shard_map/reduce_scatter | solution.py:896
  811.7 25.8 %collective-permute-start.116 = (bf16[256,2048]{1,0:T(8,128)(2,1)}, bf16[256,2048]{1,0:T(8,128)(2,1)S(1)}, u32[]{:S(2)}, u32[]{:S(2)}) collective-permute-start(bf16[256,2048]{1,0:T(8,128)(2,1)} %get-tuple-element.610.refs_8_), channel_id=1, source_target_pairs={{0,2},{2,0},{4,6},{6,4},{1,3},{3,1},{5,7},{7,5},{8,10},{10,8},{12,... | collective-permute-start | bytes 3145736 | tf_op jit(solution)/shard_map/ppermute | solution.py:633
  812.6 26.1 %collective-permute-start.120 = (bf16[256,2048]{1,0:T(8,128)(2,1)}, bf16[256,2048]{1,0:T(8,128)(2,1)S(1)}, u32[]{:S(2)}, u32[]{:S(2)}) collective-permute-start(bf16[256,2048]{1,0:T(8,128)(2,1)} %get-tuple-element.610.refs_8_), channel_id=1, source_target_pairs={{0,4},{2,6},{4,0},{6,2},{1,5},{3,7},{5,1},{7,3},{8,12},{10,14},{12... | collective-permute-start | bytes 3145736 | tf_op jit(solution)/shard_map/ppermute | solution.py:633
  916.0 241.0 %reduce-scatter.11.cloned.1.call-start = ((), (), s32[]{:S(2)}) async-start(), calls=%async_computation.11 | async-start | bytes 5242880 | tf_op jit(solution)/shard_map/reduce_scatter | solution.py:896
  938.3 32.4 %collective-permute-start.132 = (bf16[256,2048]{1,0:T(8,128)(2,1)S(1)}, bf16[256,2048]{1,0:T(8,128)(2,1)S(1)}, u32[]{:S(2)}, u32[]{:S(2)}) collective-permute-start(bf16[256,2048]{1,0:T(8,128)(2,1)S(1)} %get-tuple-element.699.refs_24_), channel_id=1, source_target_pairs={{0,1},{1,0},{2,3},{3,2},{4,5},{5,4},{6,7},{7,6},{8,9},{9,8},{10,11... | collective-permute-start | bytes 3145736 | tf_op jit(solution)/shard_map/ppermute | solution.py:636
  975.3 49.1 %collective-permute-start.140 = (bf16[3136,128]{1,0:T(8,128)(2,1)S(1)}, bf16[3136,128]{1,0:T(8,128)(2,1)S(1)}, u32[]{:S(2)}, u32[]{:S(2)}) collective-permute-start(bf16[3136,128]{1,0:T(8,128)(2,1)S(1)} %get-tuple-element.782), channel_id=1, source_target_pairs={{0,2},{2,0},{4,6},{6,4},{1,3},{3,1},{5,7},{7,5},{8,10},{10,8},{12,... | collective-permute-start | bytes 2408456 | tf_op jit(solution)/shard_map/ppermute | solution.py:633
  976.6 47.8 %collective-permute-start.141 = (bf16[3136,128]{1,0:T(8,128)(2,1)S(1)}, bf16[3136,128]{1,0:T(8,128)(2,1)S(1)}, u32[]{:S(2)}, u32[]{:S(2)}) collective-permute-start(bf16[3136,128]{1,0:T(8,128)(2,1)S(1)} %get-tuple-element.781), channel_id=1, source_target_pairs={{0,4},{2,6},{4,0},{6,2},{1,5},{3,7},{5,1},{7,3},{8,12},{10,14},{12... | collective-permute-start | bytes 2408456 | tf_op jit(solution)/shard_map/ppermute | solution.py:633
  977.6 46.8 %collective-permute-start.142 = (bf16[3136,128]{1,0:T(8,128)(2,1)S(1)}, bf16[3136,128]{1,0:T(8,128)(2,1)S(1)}, u32[]{:S(2)}, u32[]{:S(2)}) collective-permute-start(bf16[3136,128]{1,0:T(8,128)(2,1)S(1)} %get-tuple-element.780), channel_id=1, source_target_pairs={{0,6},{2,4},{4,2},{6,0},{1,7},{3,5},{5,3},{7,1},{8,14},{10,12},{12... | collective-permute-start | bytes 2408456 | tf_op jit(solution)/shard_map/ppermute | solution.py:633
  1070.2 50.2 %collective-permute-start.103 = (bf16[256,2048]{1,0:T(8,128)(2,1)}, bf16[256,2048]{1,0:T(8,128)(2,1)}, u32[]{:S(2)}, u32[]{:S(2)}) collective-permute-start(bf16[256,2048]{1,0:T(8,128)(2,1)} %add_convert_fusion), channel_id=1, source_target_pairs={{0,1},{1,0},{2,3},{3,2},{4,5},{5,4},{6,7},{7,6},{8,9},{9,8},{10,11... | collective-permute-start | bytes 3145736 | tf_op jit(solution)/shard_map/ppermute | solution.py:636
  1100.9 49.4 %collective-permute-start.153 = (f32[256,2048]{1,0:T(8,128)}, f32[256,2048]{1,0:T(8,128)}, u32[]{:S(2)}, u32[]{:S(2)}) collective-permute-start(f32[256,2048]{1,0:T(8,128)} %fusion.36), channel_id=1, source_target_pairs={{0,1},{1,0},{2,3},{3,2},{4,5},{5,4},{6,7},{7,6},{8,9},{9,8},{10,11... | collective-permute-start | bytes 6291464 | tf_op jit(solution)/shard_map/ppermute | solution.py:636
  (360 other events, 3733.3 us)
Sparse Core Ops, SparseCore 0:
  27.4 79.1 all-gather.4
  108.8 152.0 all-gather.6
  262.5 79.2 all-gather.8
  343.8 152.1 all-gather.10
  640.1 148.1 reduce-scatter.4
  811.3 76.7 reduce-scatter.6
  916.1 148.3 reduce-scatter.8
  1066.9 85.4 reduce-scatter.10

commit v3 on v2

--- a/solution.py
+++ b/solution.py
@@ -212,9 +212,8 @@
 
     lax.fori_loop(0, ctx_count, prepare, 0)
 
-    small = min(256, block)
-    key_index = lax.broadcasted_iota(jnp.int32, (small, small), 0)
-    query_index = lax.broadcasted_iota(jnp.int32, (small, small), 1)
+    key_index = lax.broadcasted_iota(jnp.int32, (block, block), 0)
+    query_index = lax.broadcasted_iota(jnp.int32, (block, block), 1)
 
     def pair(head, key_rows, query_rows, diagonal):
         query = query_wide[head, query_rows, :]
@@ -233,13 +232,7 @@
 
         def over_keys(key_place, unused, head=head):
             key_rows = pl.ds(pl.multiple_of(key_place * block, block), block)
-            for key_part in range(block // small):
-                for query_part in range(key_part, block // small):
-                    small_rows = [
-                        pl.ds(pl.multiple_of(key_place * block + part * small, small), small)
-                        for part in (key_part, query_part)
-                    ]
-                    pair(head, *small_rows, key_part == query_part)
+            pair(head, key_rows, key_rows, True)
 
             def over_queries(query_place, inner):
                 pair(head, key_rows, pl.ds(pl.multiple_of(query_place * block, block), block), False)
@@ -534,11 +527,11 @@
         if place == 0:
             copies[0].wait()
         gate = dot_nt(rows_in[...], gate_w[...])
-        gate_out[...] = gate
+        gate_out[...] = gate.astype(low)
         if place == 0:
             copies[1].wait()
         up = dot_nt(rows_in[...], up_w[...])
-        up_out[...] = up
+        up_out[...] = up.astype(low)
         units = (gate / (1.0 + jnp.exp(-gate)) * up).astype(low)
         units_out[...] = units
         if place == 0:
@@ -552,7 +545,7 @@
     inside = pl.BlockSpec(memory_space=pltpu.VMEM)
     out_shape = (
         [jax.ShapeDtypeStruct((rows, features), kind) for kind in (full, low)]
-        + [jax.ShapeDtypeStruct((rows, units), full)] * 4
+        + [jax.ShapeDtypeStruct((rows, units), low)] * 4
         + [jax.ShapeDtypeStruct((rows, units), low)] * 2
     )
     done = pl.pallas_call(
@@ -561,11 +554,17 @@
         out_specs=[inside] * len(out_shape),
         out_shape=out_shape,
         scratch_shapes=[pltpu.VMEM((units, features), low)] * 3 + [pltpu.SemaphoreType.DMA((3,))],
-        compiler_params=pltpu.CompilerParams(vmem_limit_bytes=48 * 2**20),
+        compiler_params=pltpu.CompilerParams(vmem_limit_bytes=58 * 2**20),
         cost_estimate=pl.CostEstimate(flops=0, bytes_accessed=0, transcendentals=0),
         name="units",
     )(*pieces, weights)
     return (done[:2], done[2:4], done[4:6], done[6:8])
+
+
+def halves_kernel(tp_ref, own_ref, other_ref, out_ref):
+    rows = own_ref.shape[0]
+    for place, ref in ((tp_ref[0], own_ref), (1 - tp_ref[0], other_ref)):
+        out_ref[pl.ds(pl.multiple_of(place * rows, rows), rows), :] = ref[...]
 
 
 def local_kernel(kernel, ctx, arrays, out_shape):
@@ -681,7 +680,7 @@
             for mine, other in zip(pieces[::2], pieces[1::2])
         ]
 
-    def reduce_rows(self, sums, first_fill=None, second_fill=None):
+    def reduce_rows(self, sums, first_fill=None, second_fill=None, at_once=False):
         if not self.paired:
             return lax.psum_scatter(
                 sums[0].astype(low), ("ctx", "tp"), scatter_dimension=0, tiled=True
@@ -689,20 +688,21 @@
         own, first, second, far = sums
         half = own.shape[0] // 2
         far = far.astype(low)
-        early = [
-            self.across(far[:half], 1),
-            self.across(far[half:], 2),
-            self.across(first[:half].astype(low), 1),
-            self.across(second[half:].astype(low), 2),
-        ]
-        if second_fill is not None:
+        early = [far[:half], far[half:], first[:half].astype(low), second[half:].astype(low)]
+        if at_once:
+            early, first_fill = tied(early, first_fill)
+            fill = second_fill(first_fill)
+        early = [self.across(part, 1 + place % 2) for place, part in enumerate(early)]
+        if second_fill is not None and not at_once:
             early[:2], first_fill = tied(early[:2], first_fill)
         far_top, far_end, first_top, second_end = [part.astype(full) for part in early]
         late = [(second[:half] + far_top).astype(low), (first[half:] + far_end).astype(low)]
-        if second_fill is not None:
+        if at_once:
+            late, fill = tied(late, fill)
+        elif second_fill is not None:
             late, first_fill = tied(late, first_fill)
         late = [self.across(late[0], 2), self.across(late[1], 1)]
-        if second_fill is not None:
+        if second_fill is not None and not at_once:
             fill = second_fill(first_fill)
             late, fill = tied(late, fill)
         second_top, first_end = [part.astype(full) for part in late]
@@ -722,11 +722,12 @@
     def both_halves(self, value):
         if not self.paired:
             return lax.all_gather(value, "tp", axis=0, tiled=True)
-        other = self.swap(value)
-        return jnp.where(
-            self.tp == 0,
-            jnp.concatenate([value, other], axis=0),
-            jnp.concatenate([other, value], axis=0),
+        rows, columns = value.shape
+        return local_kernel(
+            halves_kernel,
+            self.tp,
+            [value, self.swap(value)],
+            jax.ShapeDtypeStruct((self.tp_count * rows, columns), value.dtype),
         )
 
     def exchange(self, value, axis, count):
@@ -1096,7 +1097,7 @@
         def backward_units(pieces, slot):
             grad_gates, grad_ups, partials = [], [], []
             for place, rows_in in enumerate(pieces, slot * len(pieces)):
-                gate, up = gates[place], ups[place]
+                gate, up = gates[place].astype(full), ups[place].astype(full)
                 grad_hidden = dot_nt(rows_in, down)
                 sigmoid_gate = jax.nn.sigmoid(gate)
                 grad_gates.append(
@@ -1160,7 +1161,7 @@
         )
         grad_qkv, travel, branch = lax.optimization_barrier((grad_qkv, travel, branch))
         if last:
-            result = (middle + group.add_sums(travel)).astype(low)
+            result = group.both_halves((middle + group.add_sums(travel)).astype(low))
         else:
             unit_stacks = group.join_units(
                 travel, hidden_width * ctx_count, index + 1, layer_total, unit_stacks
@@ -1174,11 +1175,12 @@
                 sums,
                 (grad_qkv, branch),
                 lambda held: weight_grads([(held[0], normed_one), (heads, held[1])]),
+                index == 0,
             )
         else:
             heads_grad = sum_dots([(grad_qkv, normed_one), (heads, branch)])
             grad_normed_one = group.reduce_rows(sums)
-        grad_normed_one = tied(grad_normed_one, units_part)[0]
+        grad_normed_one, (units_part, result) = tied(grad_normed_one, (units_part, result))
         heads_part = sum_shard(heads_grad, 1)
         if index:
             waiting = jnp.concatenate([units_part, heads_part], axis=0)
@@ -1195,7 +1197,6 @@
         group.split_send(units_part), hidden_width * ctx_count, 0, layer_total, unit_stacks
     )
     norm_total, bias_total = group.total(jnp.stack(norm_list), jnp.stack(input_bias_list))
-    result = group.both_halves(result)
     tokens_grad = group.both_halves(grad_stream)
     heads_part = tied(heads_part, (unit_stacks, norm_total, bias_total, result, tokens_grad))[0]
     head_stacks = group.join_heads(

time: 1190 us -> 1170 us (0.983)
  other arithmetic: 89.7 us -> 67.9 us
  local copies, waits for them, and re-layouts: 77.1 us -> 61.9 us
  waiting for transfers between devices: 370 us -> 383 us
    ppermute x7, waiting for transfers between devices: 11.1 us -> 26.9 us  [exchange(): lax.ppermute(value, axis, [(i, i ^ step) for i in range(count)])]
    unnamed x479 -> x465, local copies, waits for them, and re-layouts: 38.4 us -> 23.8 us
    ppermute x94, waiting for transfers between devices: 345 us -> 333 us  [across(): lax.ppermute(value, 'ctx', [(i, i ^ step) for i in range(self.ctx_count)])]
  transfers between devices with their start and end apart: 175 -> 175, of which waited for: 65 -> 64; matrix products, arithmetic and copies ran while one was open for 24% -> 22% of each run, Pallas kernels for 28% -> 29%
where the time goes in v3:
time: 1170 us; the launch traced here: 1160 us
  waiting for transfers between devices  383 us (33%)
  Pallas kernels  336 us (29%)
  matrix products  155 us (13%)
  starting transfers between devices  134 us (11%)
  other arithmetic  67.9 us (6%)
  local copies, waits for them, and re-layouts  61.9 us (5%)
  between operations  19.1 us (2%)
    ppermute x94, waiting for transfers between devices, across(): lax.ppermute(value, 'ctx', [(i, i ^ step) for i in range(self.ctx_count)])  333 us
    ppermute x94, starting transfers between devices, across(): lax.ppermute(value, 'ctx', [(i, i ^ step) for i in range(self.ctx_count)])  110 us
    pallas_call x6, Pallas kernels, weight_grads(): pl.pallas_call(kernel, grid=(features // block,), in_specs=[pl.BlockSpec(...  94.4 us
    dot_general x64, matrix products, dot_nt(): lax.dot_general(left, right, (((1,), (1,)), ((), ())), preferred_element_...  93.8 us
    pallas_call x2, Pallas kernels, attend_back(): pl.pallas_call(functools.partial(attend_back_kernel, ctx_count, tp_count,...  89.1 us
    pallas_call x2, Pallas kernels, attend(): pl.pallas_call(functools.partial(attend_kernel, ctx_count, tp_count, slot...  85.8 us
    dot_general x56, matrix products, dot_nn(): lax.dot_general(left, right, (((1,), (0,)), ((), ())), preferred_element_...  61.4 us
    pallas_call x4, Pallas kernels, units_call(): pl.pallas_call(units_kernel, in_specs=[inside] * 2 + [pl.BlockSpec(memory...  43.7 us
  transfers between devices with their start and end apart: 175, of which 64 were waited for; matrix products, arithmetic and copies ran while one was open for 22% of the time, Pallas kernels for 29%

profile of v3, /device:TPU:8, one launch (start us, length us, event | category | flops | bytes accessed | tf_op | source)
XLA Modules:
  0.0 1157.1 jit_solution(17238447828030864180)
XLA Ops:
  21.5 4.5 collective-permute-done.8.refs_1_
  39.1 15.3 %collective-permute-done.1.refs_2_.refs_18_ = bf16[256,2048]{1,0:T(8,128)(2,1)} collective-permute-done((bf16[256,2048]{1,0:T(8,128)(2,1)}, bf16[256,2048]{1,0:T(8,128)(2,1)}, u32[]{:S(2)}, u32[]{:S(2)}) %collective-permute-start.1) | collective-permute-done | bytes 1048608 | tf_op jit(solution)/shard_map/ppermute | solution.py:632
  70.1 5.2 collective-permute-done.32.refs_1_
  75.2 17.8 %collective-permute-done.33.refs_2_ = bf16[2112,128]{1,0:T(8,128)(2,1)} collective-permute-done((bf16[2112,128]{1,0:T(8,128)(2,1)}, bf16[2112,128]{1,0:T(8,128)(2,1)}, u32[]{:S(2)}, u32[]{:S(2)}) %collective-permute-start.33) | collective-permute-done | bytes 540704 | tf_op jit(solution)/shard_map/ppermute | solution.py:632
  101.0 5.6 fusion.40
  113.6 43.0 %attend.2 = (bf16[256,256]{1,0:T(8,128)(2,1)S(1)}, bf16[256,256]{1,0:T(8,128)(2,1)S(1)}, bf16[256,256]{1,0:T(8,128)(2,1)S(1)}, bf16[256,256]{1,0:T(8,128)(2,1)S(...) custom-call(s32[8]{0:T(128)S(1)} %fusion.194.order_ref, ...), custom_call_target="tpu_custom_call" | custom-call | flops 34359738368 | tf_op jit(solution)/shard_map/attend/pallas_call | solution.py:286
  171.9 8.5 collective-permute-done.19
  184.7 6.9 collective-permute-done.16
  191.6 14.1 %collective-permute-done.20 = bf16[128,2048]{1,0:T(8,128)(2,1)S(1)} collective-permute-done((bf16[128,2048]{1,0:T(8,128)(2,1)S(1)}, bf16[128,2048]{1,0:T(8,128)(2,1)S(1)}, u32[]{:S(2)}, u32[]{:S(2)}) %collective-permute-start.20) | collective-permute-done | bytes 524320 | tf_op jit(solution)/shard_map/ppermute | solution.py:632
  210.5 22.3 %collective-permute-done.25.mine_in.refs_18_.refs_26_ = bf16[256,2048]{1,0:T(8,128)(2,1)S(1)} collective-permute-done((bf16[256,2048]{1,0:T(8,128)(2,1)S(1)}, bf16[256,2048]{1,0:T(8,128)(2,1)S(1)}, u32[]{:S(2)}, u32[]{:S(2)}) %collective-permute-start.25) | collective-permute-done | bytes 1048608 | tf_op jit(solution)/shard_map/ppermute | solution.py:632
  236.6 9.9 collective-permute-done.29
  250.7 10.3 all-gather.7.cloned.1.call-done.weights_hbm
  260.9 10.7 units.7
  271.7 11.1 units.5
  283.2 11.1 units.4
  294.5 10.9 units.6
  312.5 8.7 collective-permute-done.40
  326.4 6.0 collective-permute-done.37
  332.4 13.7 %collective-permute-done.41 = bf16[128,2048]{1,0:T(8,128)(2,1)} collective-permute-done((bf16[128,2048]{1,0:T(8,128)(2,1)}, bf16[128,2048]{1,0:T(8,128)(2,1)}, u32[]{:S(2)}, u32[]{:S(2)}) %collective-permute-start.41) | collective-permute-done | bytes 524320 | tf_op jit(solution)/shard_map/ppermute | solution.py:632
  354.7 21.9 %collective-permute-done.46.refs_2_.refs_18_ = bf16[256,2048]{1,0:T(8,128)(2,1)S(1)} collective-permute-done((bf16[256,2048]{1,0:T(8,128)(2,1)S(1)}, bf16[256,2048]{1,0:T(8,128)(2,1)S(1)}, u32[]{:S(2)}, u32[]{:S(2)}) %collective-permute-start.46) | collective-permute-done | bytes 1048608 | tf_op jit(solution)/shard_map/ppermute | solution.py:632
  379.8 8.9 collective-permute-done.50
  396.4 42.8 %attend.3 = (bf16[256,256]{1,0:T(8,128)(2,1)S(1)}, bf16[256,256]{1,0:T(8,128)(2,1)S(1)}, bf16[256,256]{1,0:T(8,128)(2,1)S(1)}, bf16[256,256]{1,0:T(8,128)(2,1)S(...) custom-call(s32[8]{0:T(128)S(1)} %fusion.194.order_ref, ...), custom_call_target="tpu_custom_call" | custom-call | flops 34359738368 | tf_op jit(solution)/shard_map/attend/pallas_call | solution.py:286
  450.5 9.0 collective-permute-done.65
  464.7 6.1 collective-permute-done.62
  473.9 10.1 collective-permute-done.66
  486.8 9.2 all-gather.11.cloned.1.call-done
  585.6 11.4 weight_grads.6.refs_32_
  606.4 20.4 %weight_grads.7 = bf16[2112,2048]{1,0:T(8,128)(2,1)} custom-call(bf16[256,704]{1,0:T(8,128)(2,1)} %copy-done.95, bf16[256,704]{1,0:T(8,128)(2,1)} %copy-done.113, bf16[256,704]{1,0:T(8,128)(2,1)} %copy-done.96, bf16[256,704]{1,0:T(8,128)(2,1)} %copy-done.115, bf16[256,704]{1,0:T(8,128)(2,1)} %copy-done.98, ...), custom_call_target="tpu_custom_call", output_to_operand_aliasing={{}: (32, {})} | custom-call | flops 11811160064 | bytes 11534336 | tf_op jit(solution)/shard_map/weight_grads/pallas_call | solution.py:473
  649.4 14.5 %collective-permute-done.89.refs_26_ = bf16[256,2048]{1,0:T(8,128)(2,1)S(1)} collective-permute-done((bf16[256,2048]{1,0:T(8,128)(2,1)S(1)}, bf16[256,2048]{1,0:T(8,128)(2,1)S(1)}, u32[]{:S(2)}, u32[]{:S(2)}) %collective-permute-start.89) | collective-permute-done | bytes 1048608 | tf_op jit(solution)/shard_map/ppermute | solution.py:632
  668.2 9.0 collective-permute-done.93
  685.0 44.3 %attend_back.2 = (bf16[256,768]{1,0:T(8,128)(2,1)S(1)}, bf16[256,768]{1,0:T(8,128)(2,1)}, bf16[256,768]{1,0:T(8,128)(2,1)}, bf16[256,768]{1,0:T(8,128)(2,1)}, bf...) custom-call(s32[8]{0:T(128)S(1)} %fusion.194.order_ref, ...), custom_call_target="tpu_custom_call" | custom-call | flops 34359738368 | tf_op jit(solution)/shard_map/attend_back/pallas_call | solution.py:325
  749.0 6.8 collective-permute-done.108
  760.2 15.3 %weight_grads.8 = bf16[1024,2048]{1,0:T(8,128)(2,1)} custom-call(bf16[256,768]{1,0:T(8,128)(2,1)} %copy-done.15, bf16[256,768]{1,0:T(8,128)(2,1)} %get-tuple-element.541.refs_1_, bf16[256,768]{1,0:T(8,128)(2,1)} %get-tuple-element.542.refs_2_, bf16[256,768]{1,0:T(8,128)(2,1)} %get-tuple-element.543.refs_3_, bf16[256,768]{1,0:T(8,128)(2,1)} %get-tuple-element.544.refs_4_, ...), custom_call_target="tpu_custom_call" | custom-call | flops 8589934592 | bytes 8388608 | tf_op jit(solution)/shard_map/weight_grads/pallas_call | solution.py:473
  805.5 12.0 %collective-permute-done.116.refs_10_ = bf16[256,2048]{1,0:T(8,128)(2,1)S(1)} collective-permute-done((bf16[256,2048]{1,0:T(8,128)(2,1)}, bf16[256,2048]{1,0:T(8,128)(2,1)S(1)}, u32[]{:S(2)}, u32[]{:S(2)}) %collective-permute-start.116) | collective-permute-done | bytes 1048608 | tf_op jit(solution)/shard_map/ppermute | solution.py:632
  824.2 7.7 collective-permute-done.123
  857.9 11.6 %weight_grads.9.refs_32_ = bf16[2112,2048]{1,0:T(8,128)(2,1)} custom-call(bf16[256,704]{1,0:T(8,128)(2,1)} %get-tuple-element.591.refs_0_, bf16[256,704]{1,0:T(8,128)(2,1)} %get-tuple-element.592.refs_1_, bf16[256,704]{1,0:T(8,128)(2,1)} %get-tuple-element.593.refs_2_, bf16[256,704]{1,0:T(8,128)(2,1)} %get-tuple-element.594.refs_3_, ...), custom_call_target="tpu_custom_call" | custom-call | flops 5905580032 | bytes 5767168 | tf_op jit(solution)/shard_map/weight_grads/pallas_call | solution.py:473
  875.4 20.1 %weight_grads.10 = bf16[2112,2048]{1,0:T(8,128)(2,1)} custom-call(bf16[256,704]{1,0:T(8,128)(2,1)} %copy-done.73, bf16[256,704]{1,0:T(8,128)(2,1)} %copy-done.76, bf16[256,704]{1,0:T(8,128)(2,1)} %copy-done.97, bf16[256,704]{1,0:T(8,128)(2,1)} %copy-done.116, bf16[256,704]{1,0:T(8,128)(2,1)} %copy-done.74, ...), custom_call_target="tpu_custom_call", output_to_operand_aliasing={{}: (32, {})} | custom-call | flops 11811160064 | bytes 11534336 | tf_op jit(solution)/shard_map/weight_grads/pallas_call | solution.py:473
  900.4 9.2 collective-permute-done.119
  920.7 18.2 %collective-permute-done.133.refs_26_ = bf16[256,2048]{1,0:T(8,128)(2,1)} collective-permute-done((bf16[256,2048]{1,0:T(8,128)(2,1)S(1)}, bf16[256,2048]{1,0:T(8,128)(2,1)}, u32[]{:S(2)}, u32[]{:S(2)}) %collective-permute-start.133) | collective-permute-done | bytes 1048608 | tf_op jit(solution)/shard_map/ppermute | solution.py:632
  961.2 44.8 %attend_back.3 = (bf16[256,768]{1,0:T(8,128)(2,1)S(1)}, bf16[256,768]{1,0:T(8,128)(2,1)}, bf16[256,768]{1,0:T(8,128)(2,1)}, bf16[256,768]{1,0:T(8,128)(2,1)}, bf...) custom-call(s32[8]{0:T(128)S(1)} %fusion.194.order_ref, ...), custom_call_target="tpu_custom_call" | custom-call | flops 34359738368 | tf_op jit(solution)/shard_map/attend_back/pallas_call | solution.py:325
  1019.0 15.6 %weight_grads.11 = bf16[1024,2048]{1,0:T(8,128)(2,1)} custom-call(bf16[256,768]{1,0:T(8,128)(2,1)} %copy-done.13, bf16[256,768]{1,0:T(8,128)(2,1)} %get-tuple-element.664.refs_1_, bf16[256,768]{1,0:T(8,128)(2,1)} %get-tuple-element.665.refs_2_, bf16[256,768]{1,0:T(8,128)(2,1)} %get-tuple-element.666.refs_3_, bf16[256,768]{1,0:T(8,128)(2,1)} %get-tuple-element.667.refs_4_, ...), custom_call_target="tpu_custom_call" | custom-call | flops 8589934592 | bytes 8388608 | tf_op jit(solution)/shard_map/weight_grads/pallas_call | solution.py:473
  1047.2 7.6 collective-permute-done.147
  1056.6 9.5 collective-permute-done.152
  1091.1 5.4 collective-permute-done.158
  1100.3 9.1 collective-permute-done.159
  1114.1 8.9 collective-permute-done.160
  1137.6 5.0 collective-permute-done.164.refs_1_
  1142.6 5.7 collective-permute-done.165.refs_2_
  (1106 shorter events, 482.3 us)
Async XLA Ops:
  7.2 104.6 %all-gather.5.cloned.1.call-start = ((), (), s32[]{:S(2)}) async-start(), calls=%async_computation.4 | async-start | bytes 5242880 | tf_op jit(solution)/shard_map/all_gather | solution.py:893
  27.3 233.7 %all-gather.7.cloned.1.call-start = ((), (), s32[]{:S(2)}) async-start(), calls=%async_computation.5 | async-start | bytes 10813440 | tf_op jit(solution)/shard_map/all_gather | solution.py:893
  31.1 27.2 %collective-permute-start.3 = (bf16[256,2048]{1,0:T(8,128)(2,1)}, bf16[256,2048]{1,0:T(8,128)(2,1)}, u32[]{:S(2)}, u32[]{:S(2)}) collective-permute-start(bf16[256,2048]{1,0:T(8,128)(2,1)} %fusion.32.refs_0_.refs_16_), channel_id=1, source_target_pairs={{0,4},{2,6},{4,0},{6,2},{1,5},{3,7},{5,1},{7,3},{8,12},{10,14},{12... | collective-permute-start | bytes 3145736 | tf_op jit(solution)/shard_map/ppermute | solution.py:632
  56.3 40.7 %collective-permute-start.5 = (bf16[128,2048]{1,0:T(8,128)(2,1)}, bf16[128,2048]{1,0:T(8,128)(2,1)}, u32[]{:S(2)}, u32[]{:S(2)}) collective-permute-start(bf16[128,2048]{1,0:T(8,128)(2,1)} %slice.426), channel_id=1, source_target_pairs={{0,4},{2,6},{4,0},{6,2},{1,5},{3,7},{5,1},{7,3},{8,12},{10,14},{12... | collective-permute-start | bytes 1572872 | tf_op jit(solution)/shard_map/ppermute | solution.py:632
  61.2 31.9 %collective-permute-start.33 = (bf16[2112,128]{1,0:T(8,128)(2,1)}, bf16[2112,128]{1,0:T(8,128)(2,1)}, u32[]{:S(2)}, u32[]{:S(2)}) collective-permute-start(bf16[2112,128]{1,0:T(8,128)(2,1)} %get-tuple-element.771), channel_id=1, source_target_pairs={{0,4},{2,6},{4,0},{6,2},{1,5},{3,7},{5,1},{7,3},{8,12},{10,14},{12... | collective-permute-start | bytes 1622024 | tf_op jit(solution)/shard_map/ppermute | solution.py:632
  61.2 31.9 %collective-permute-start.34 = (bf16[2112,128]{1,0:T(8,128)(2,1)}, bf16[2112,128]{1,0:T(8,128)(2,1)}, u32[]{:S(2)}, u32[]{:S(2)}) collective-permute-start(bf16[2112,128]{1,0:T(8,128)(2,1)} %get-tuple-element.770), channel_id=1, source_target_pairs={{0,6},{2,4},{4,2},{6,0},{1,7},{3,5},{5,3},{7,1},{8,14},{10,12},{12... | collective-permute-start | bytes 1622024 | tf_op jit(solution)/shard_map/ppermute | solution.py:632
  68.6 29.5 %collective-permute-start.6 = (bf16[128,2048]{1,0:T(8,128)(2,1)}, bf16[128,2048]{1,0:T(8,128)(2,1)}, u32[]{:S(2)}, u32[]{:S(2)}) collective-permute-start(bf16[128,2048]{1,0:T(8,128)(2,1)} %slice.427), channel_id=1, source_target_pairs={{0,2},{2,0},{4,6},{6,4},{1,3},{3,1},{5,7},{7,5},{8,10},{10,8},{12,... | collective-permute-start | bytes 1572872 | tf_op jit(solution)/shard_map/ppermute | solution.py:632
  75.2 31.3 %collective-permute-start = (bf16[256,2048]{1,0:T(8,128)(2,1)}, bf16[256,2048]{1,0:T(8,128)(2,1)}, u32[]{:S(2)}, u32[]{:S(2)}) collective-permute-start(bf16[256,2048]{1,0:T(8,128)(2,1)} %fusion.32.refs_0_.refs_16_), channel_id=1, source_target_pairs={{0,1},{1,0},{2,3},{3,2},{4,5},{5,4},{6,7},{7,6},{8,9},{9,8},{10,11... | collective-permute-start | bytes 3145736 | tf_op jit(solution)/shard_map/ppermute | solution.py:635
  96.7 254.8 %all-gather.9.cloned.1.call-start = ((), (), s32[]{:S(2)}) async-start(), calls=%async_computation.6 | async-start | bytes 5242880 | tf_op jit(solution)/shard_map/all_gather | solution.py:893
  108.3 48.4 %collective-permute-start.11 = (bf16[3136,128]{1,0:T(8,128)(2,1)}, bf16[3136,128]{1,0:T(8,128)(2,1)S(1)}, u32[]{:S(2)}, u32[]{:S(2)}) collective-permute-start(bf16[3136,128]{1,0:T(8,128)(2,1)} %get-tuple-element.762), channel_id=1, source_target_pairs={{0,2},{2,0},{4,6},{6,4},{1,3},{3,1},{5,7},{7,5},{8,10},{10,8},{12,... | collective-permute-start | bytes 2408456 | tf_op jit(solution)/shard_map/ppermute | solution.py:632
  109.8 46.9 %collective-permute-start.12 = (bf16[3136,128]{1,0:T(8,128)(2,1)}, bf16[3136,128]{1,0:T(8,128)(2,1)S(1)}, u32[]{:S(2)}, u32[]{:S(2)}) collective-permute-start(bf16[3136,128]{1,0:T(8,128)(2,1)} %get-tuple-element.761), channel_id=1, source_target_pairs={{0,4},{2,6},{4,0},{6,2},{1,5},{3,7},{5,1},{7,3},{8,12},{10,14},{12... | collective-permute-start | bytes 2408456 | tf_op jit(solution)/shard_map/ppermute | solution.py:632
  111.5 45.2 %collective-permute-start.13 = (bf16[3136,128]{1,0:T(8,128)(2,1)}, bf16[3136,128]{1,0:T(8,128)(2,1)S(1)}, u32[]{:S(2)}, u32[]{:S(2)}) collective-permute-start(bf16[3136,128]{1,0:T(8,128)(2,1)} %get-tuple-element.760), channel_id=1, source_target_pairs={{0,6},{2,4},{4,2},{6,0},{1,7},{3,5},{5,3},{7,1},{8,14},{10,12},{12... | collective-permute-start | bytes 2408456 | tf_op jit(solution)/shard_map/ppermute | solution.py:632
  162.7 43.3 %collective-permute-start.14 = (bf16[256,2048]{1,0:T(8,128)(2,1)S(1)}, bf16[256,2048]{1,0:T(8,128)(2,1)S(1)}, u32[]{:S(2)}, u32[]{:S(2)}) collective-permute-start(bf16[256,2048]{1,0:T(8,128)(2,1)S(1)} %convolution_convert_fusion.11), channel_id=1, source_target_pairs={{0,1},{1,0},{2,3},{3,2},{4,5},{5,4},{6,7},{7,6},{8,9},{9,8},{10,11... | collective-permute-start | bytes 3145736 | tf_op jit(solution)/shard_map/ppermute | solution.py:635
  171.7 34.2 %collective-permute-start.23 = (bf16[128,2048]{1,0:T(8,128)(2,1)S(1)}, bf16[128,2048]{1,0:T(8,128)(2,1)S(1)}, u32[]{:S(2)}, u32[]{:S(2)}) collective-permute-start(bf16[128,2048]{1,0:T(8,128)(2,1)S(1)} %slice.817), channel_id=1, source_target_pairs={{0,4},{2,6},{4,0},{6,2},{1,5},{3,7},{5,1},{7,3},{8,12},{10,14},{12... | collective-permute-start | bytes 1572872 | tf_op jit(solution)/shard_map/ppermute | solution.py:632
  208.8 26.8 %collective-permute-start.27 = (bf16[256,2048]{1,0:T(8,128)(2,1)S(1)}, bf16[256,2048]{1,0:T(8,128)(2,1)S(1)}, u32[]{:S(2)}, u32[]{:S(2)}) collective-permute-start(bf16[256,2048]{1,0:T(8,128)(2,1)S(1)} %add_convert_fusion.4.mine_in.refs_16_.refs_24_), channel_id=1, source_target_pairs={{0,4},{2,6},{4,0},{6,2},{1,5},{3,7},{5,1},{7,3},{8,12},{10,14},{12... | collective-permute-start | bytes 3145736 | tf_op jit(solution)/shard_map/ppermute | solution.py:632
  235.3 260.6 %all-gather.11.cloned.1.call-start = ((), (), s32[]{:S(2)}) async-start(), calls=%async_computation.7 | async-start | bytes 10813440 | tf_op jit(solution)/shard_map/all_gather | solution.py:893
  271.7 34.3 %collective-permute-start.39 = (bf16[256,2048]{1,0:T(8,128)(2,1)}, bf16[256,2048]{1,0:T(8,128)(2,1)S(1)}, u32[]{:S(2)}, u32[]{:S(2)}) collective-permute-start(bf16[256,2048]{1,0:T(8,128)(2,1)} %get-tuple-element.404), channel_id=1, source_target_pairs={{0,1},{1,0},{2,3},{3,2},{4,5},{5,4},{6,7},{7,6},{8,9},{9,8},{10,11... | collective-permute-start | bytes 3145736 | tf_op jit(solution)/shard_map/ppermute | solution.py:635
  294.3 54.3 %collective-permute-start.35 = (bf16[256,2048]{1,0:T(8,128)(2,1)}, bf16[256,2048]{1,0:T(8,128)(2,1)S(1)}, u32[]{:S(2)}, u32[]{:S(2)}) collective-permute-start(bf16[256,2048]{1,0:T(8,128)(2,1)} %get-tuple-element.392), channel_id=1, source_target_pairs={{0,1},{1,0},{2,3},{3,2},{4,5},{5,4},{6,7},{7,6},{8,9},{9,8},{10,11... | collective-permute-start | bytes 3145736 | tf_op jit(solution)/shard_map/ppermute | solution.py:635
  311.9 35.5 %collective-permute-start.44 = (bf16[128,2048]{1,0:T(8,128)(2,1)S(1)}, bf16[128,2048]{1,0:T(8,128)(2,1)S(1)}, u32[]{:S(2)}, u32[]{:S(2)}) collective-permute-start(bf16[128,2048]{1,0:T(8,128)(2,1)S(1)} %slice.815), channel_id=1, source_target_pairs={{0,4},{2,6},{4,0},{6,2},{1,5},{3,7},{5,1},{7,3},{8,12},{10,14},{12... | collective-permute-start | bytes 1572872 | tf_op jit(solution)/shard_map/ppermute | solution.py:632
  326.3 458.8 %reduce-scatter.5.cloned.1.call-start = ((), (), s32[]{:S(2)}) async-start(), calls=%async_computation.8 | async-start | bytes 10813440 | tf_op jit(solution)/shard_map/reduce_scatter | solution.py:897
  392.8 46.4 %collective-permute-start.53 = (bf16[256,2048]{1,0:T(8,128)(2,1)}, bf16[256,2048]{1,0:T(8,128)(2,1)}, u32[]{:S(2)}, u32[]{:S(2)}) collective-permute-start(bf16[256,2048]{1,0:T(8,128)(2,1)} %constant_dynamic-slice_fusion.12.refs_8_), channel_id=1, source_target_pairs={{0,2},{2,0},{4,6},{6,4},{1,3},{3,1},{5,7},{7,5},{8,10},{10,8},{12,... | collective-permute-start | bytes 3145736 | tf_op jit(solution)/shard_map/ppermute | solution.py:632
  393.2 47.7 %collective-permute-start.54 = (bf16[256,2048]{1,0:T(8,128)(2,1)}, bf16[256,2048]{1,0:T(8,128)(2,1)}, u32[]{:S(2)}, u32[]{:S(2)}) collective-permute-start(bf16[256,2048]{1,0:T(8,128)(2,1)} %constant_dynamic-slice_fusion.12.refs_8_), channel_id=1, source_target_pairs={{0,4},{2,6},{4,0},{6,2},{1,5},{3,7},{5,1},{7,3},{8,12},{10,14},{12... | collective-permute-start | bytes 3145736 | tf_op jit(solution)/shard_map/ppermute | solution.py:632
  394.4 46.5 %collective-permute-start.55 = (bf16[256,2048]{1,0:T(8,128)(2,1)}, bf16[256,2048]{1,0:T(8,128)(2,1)}, u32[]{:S(2)}, u32[]{:S(2)}) collective-permute-start(bf16[256,2048]{1,0:T(8,128)(2,1)} %constant_dynamic-slice_fusion.12.refs_8_), channel_id=1, source_target_pairs={{0,6},{2,4},{4,2},{6,0},{1,7},{3,5},{5,3},{7,1},{8,14},{10,12},{12... | collective-permute-start | bytes 3145736 | tf_op jit(solution)/shard_map/ppermute | solution.py:632
  498.7 26.0 %collective-permute-start.72 = (bf16[256,2048]{1,0:T(8,128)(2,1)S(1)}, bf16[256,2048]{1,0:T(8,128)(2,1)S(1)}, u32[]{:S(2)}, u32[]{:S(2)}) collective-permute-start(bf16[256,2048]{1,0:T(8,128)(2,1)S(1)} %add_convert_fusion.1.refs_16_.refs_24_), channel_id=1, source_target_pairs={{0,2},{2,0},{4,6},{6,4},{1,3},{3,1},{5,7},{7,5},{8,10},{10,8},{12,... | collective-permute-start | bytes 3145736 | tf_op jit(solution)/shard_map/ppermute | solution.py:632
  500.5 27.7 %collective-permute-start.76 = (bf16[256,2048]{1,0:T(8,128)(2,1)S(1)}, bf16[256,2048]{1,0:T(8,128)(2,1)S(1)}, u32[]{:S(2)}, u32[]{:S(2)}) collective-permute-start(bf16[256,2048]{1,0:T(8,128)(2,1)S(1)} %add_convert_fusion.1.refs_16_.refs_24_), channel_id=1, source_target_pairs={{0,4},{2,6},{4,0},{6,2},{1,5},{3,7},{5,1},{7,3},{8,12},{10,14},{12... | collective-permute-start | bytes 3145736 | tf_op jit(solution)/shard_map/ppermute | solution.py:632
  562.9 68.5 %collective-permute-start.75 = (bf16[128,2048]{1,0:T(8,128)(2,1)S(1)}, bf16[128,2048]{1,0:T(8,128)(2,1)}, u32[]{:S(2)}, u32[]{:S(2)}) collective-permute-start(bf16[128,2048]{1,0:T(8,128)(2,1)S(1)} %slice.812), channel_id=1, source_target_pairs={{0,2},{2,0},{4,6},{6,4},{1,3},{3,1},{5,7},{7,5},{8,10},{10,8},{12,... | collective-permute-start | bytes 1572872 | tf_op jit(solution)/shard_map/ppermute | solution.py:632
  575.2 58.0 %collective-permute-start.87 = (bf16[128,2048]{1,0:T(8,128)(2,1)}, bf16[128,2048]{1,0:T(8,128)(2,1)}, u32[]{:S(2)}, u32[]{:S(2)}) collective-permute-start(bf16[128,2048]{1,0:T(8,128)(2,1)} %slice.811), channel_id=1, source_target_pairs={{0,4},{2,6},{4,0},{6,2},{1,5},{3,7},{5,1},{7,3},{8,12},{10,14},{12... | collective-permute-start | bytes 1572872 | tf_op jit(solution)/shard_map/ppermute | solution.py:632
  626.8 291.0 %reduce-scatter.7.cloned.1.call-start = ((), (), s32[]{:S(2)}) async-start(), calls=%async_computation.9 | async-start | bytes 5242880 | tf_op jit(solution)/shard_map/reduce_scatter | solution.py:897
  639.8 25.3 %collective-permute-start.91 = (bf16[256,2048]{1,0:T(8,128)(2,1)S(1)}, bf16[256,2048]{1,0:T(8,128)(2,1)S(1)}, u32[]{:S(2)}, u32[]{:S(2)}) collective-permute-start(bf16[256,2048]{1,0:T(8,128)(2,1)S(1)} %get-tuple-element.548.refs_24_), channel_id=1, source_target_pairs={{0,4},{2,6},{4,0},{6,2},{1,5},{3,7},{5,1},{7,3},{8,12},{10,14},{12... | collective-permute-start | bytes 3145736 | tf_op jit(solution)/shard_map/ppermute | solution.py:632
  643.3 34.9 %collective-permute-start.88 = (bf16[256,2048]{1,0:T(8,128)(2,1)S(1)}, bf16[256,2048]{1,0:T(8,128)(2,1)S(1)}, u32[]{:S(2)}, u32[]{:S(2)}) collective-permute-start(bf16[256,2048]{1,0:T(8,128)(2,1)S(1)} %get-tuple-element.548.refs_24_), channel_id=1, source_target_pairs={{0,1},{1,0},{2,3},{3,2},{4,5},{5,4},{6,7},{7,6},{8,9},{9,8},{10,11... | collective-permute-start | bytes 3145736 | tf_op jit(solution)/shard_map/ppermute | solution.py:635
  681.4 47.9 %collective-permute-start.100 = (bf16[256,2048]{1,0:T(8,128)(2,1)}, bf16[256,2048]{1,0:T(8,128)(2,1)}, u32[]{:S(2)}, u32[]{:S(2)}) collective-permute-start(bf16[256,2048]{1,0:T(8,128)(2,1)} %convolution_add_fusion.18), channel_id=1, source_target_pairs={{0,2},{2,0},{4,6},{6,4},{1,3},{3,1},{5,7},{7,5},{8,10},{10,8},{12,... | collective-permute-start | bytes 3145736 | tf_op jit(solution)/shard_map/ppermute | solution.py:632
  682.9 47.7 %collective-permute-start.101 = (bf16[256,2048]{1,0:T(8,128)(2,1)}, bf16[256,2048]{1,0:T(8,128)(2,1)}, u32[]{:S(2)}, u32[]{:S(2)}) collective-permute-start(bf16[256,2048]{1,0:T(8,128)(2,1)} %convolution_add_fusion.17), channel_id=1, source_target_pairs={{0,4},{2,6},{4,0},{6,2},{1,5},{3,7},{5,1},{7,3},{8,12},{10,14},{12... | collective-permute-start | bytes 3145736 | tf_op jit(solution)/shard_map/ppermute | solution.py:632
  683.5 47.2 %collective-permute-start.102 = (bf16[256,2048]{1,0:T(8,128)(2,1)}, bf16[256,2048]{1,0:T(8,128)(2,1)}, u32[]{:S(2)}, u32[]{:S(2)}) collective-permute-start(bf16[256,2048]{1,0:T(8,128)(2,1)} %convolution_add_fusion.16), channel_id=1, source_target_pairs={{0,6},{2,4},{4,2},{6,0},{1,7},{3,5},{5,3},{7,1},{8,14},{10,12},{12... | collective-permute-start | bytes 3145736 | tf_op jit(solution)/shard_map/ppermute | solution.py:632
  737.1 43.6 %collective-permute-start.103 = (bf16[256,2048]{1,0:T(8,128)(2,1)}, bf16[256,2048]{1,0:T(8,128)(2,1)S(1)}, u32[]{:S(2)}, u32[]{:S(2)}) collective-permute-start(bf16[256,2048]{1,0:T(8,128)(2,1)} %convolution_convert_fusion.19), channel_id=1, source_target_pairs={{0,1},{1,0},{2,3},{3,2},{4,5},{5,4},{6,7},{7,6},{8,9},{9,8},{10,11... | collective-permute-start | bytes 3145736 | tf_op jit(solution)/shard_map/ppermute | solution.py:635
  743.9 34.3 %collective-permute-start.105 = (bf16[128,2048]{1,0:T(8,128)(2,1)S(1)}, bf16[128,2048]{1,0:T(8,128)(2,1)S(1)}, u32[]{:S(2)}, u32[]{:S(2)}) collective-permute-start(bf16[128,2048]{1,0:T(8,128)(2,1)S(1)} %slice.810), channel_id=1, source_target_pairs={{0,2},{2,0},{4,6},{6,4},{1,3},{3,1},{5,7},{7,5},{8,10},{10,8},{12,... | collective-permute-start | bytes 1572872 | tf_op jit(solution)/shard_map/ppermute | solution.py:632
  746.0 33.5 %collective-permute-start.112 = (bf16[128,2048]{1,0:T(8,128)(2,1)S(1)}, bf16[128,2048]{1,0:T(8,128)(2,1)S(1)}, u32[]{:S(2)}, u32[]{:S(2)}) collective-permute-start(bf16[128,2048]{1,0:T(8,128)(2,1)S(1)} %slice.809), channel_id=1, source_target_pairs={{0,4},{2,6},{4,0},{6,2},{1,5},{3,7},{5,1},{7,3},{8,12},{10,14},{12... | collective-permute-start | bytes 1572872 | tf_op jit(solution)/shard_map/ppermute | solution.py:632
  791.1 277.5 %reduce-scatter.9.cloned.1.call-start = ((), (), s32[]{:S(2)}) async-start(), calls=%async_computation.10 | async-start | bytes 10813440 | tf_op jit(solution)/shard_map/reduce_scatter | solution.py:897
  791.6 25.8 %collective-permute-start.116 = (bf16[256,2048]{1,0:T(8,128)(2,1)}, bf16[256,2048]{1,0:T(8,128)(2,1)S(1)}, u32[]{:S(2)}, u32[]{:S(2)}) collective-permute-start(bf16[256,2048]{1,0:T(8,128)(2,1)} %get-tuple-element.599.refs_8_), channel_id=1, source_target_pairs={{0,2},{2,0},{4,6},{6,4},{1,3},{3,1},{5,7},{7,5},{8,10},{10,8},{12,... | collective-permute-start | bytes 3145736 | tf_op jit(solution)/shard_map/ppermute | solution.py:632
  793.1 25.6 %collective-permute-start.120 = (bf16[256,2048]{1,0:T(8,128)(2,1)}, bf16[256,2048]{1,0:T(8,128)(2,1)S(1)}, u32[]{:S(2)}, u32[]{:S(2)}) collective-permute-start(bf16[256,2048]{1,0:T(8,128)(2,1)} %get-tuple-element.599.refs_8_), channel_id=1, source_target_pairs={{0,4},{2,6},{4,0},{6,2},{1,5},{3,7},{5,1},{7,3},{8,12},{10,14},{12... | collective-permute-start | bytes 3145736 | tf_op jit(solution)/shard_map/ppermute | solution.py:632
  895.5 236.6 %reduce-scatter.11.cloned.1.call-start = ((), (), s32[]{:S(2)}) async-start(), calls=%async_computation.11 | async-start | bytes 5242880 | tf_op jit(solution)/shard_map/reduce_scatter | solution.py:897
  919.4 32.8 %collective-permute-start.132 = (bf16[256,2048]{1,0:T(8,128)(2,1)S(1)}, bf16[256,2048]{1,0:T(8,128)(2,1)S(1)}, u32[]{:S(2)}, u32[]{:S(2)}) collective-permute-start(bf16[256,2048]{1,0:T(8,128)(2,1)S(1)} %get-tuple-element.671.refs_24_), channel_id=1, source_target_pairs={{0,1},{1,0},{2,3},{3,2},{4,5},{5,4},{6,7},{7,6},{8,9},{9,8},{10,11... | collective-permute-start | bytes 3145736 | tf_op jit(solution)/shard_map/ppermute | solution.py:635
  957.7 48.3 %collective-permute-start.140 = (bf16[3136,128]{1,0:T(8,128)(2,1)}, bf16[3136,128]{1,0:T(8,128)(2,1)S(1)}, u32[]{:S(2)}, u32[]{:S(2)}) collective-permute-start(bf16[3136,128]{1,0:T(8,128)(2,1)} %get-tuple-element.758), channel_id=1, source_target_pairs={{0,2},{2,0},{4,6},{6,4},{1,3},{3,1},{5,7},{7,5},{8,10},{10,8},{12,... | collective-permute-start | bytes 2408456 | tf_op jit(solution)/shard_map/ppermute | solution.py:632
  958.9 47.2 %collective-permute-start.141 = (bf16[3136,128]{1,0:T(8,128)(2,1)S(1)}, bf16[3136,128]{1,0:T(8,128)(2,1)S(1)}, u32[]{:S(2)}, u32[]{:S(2)}) collective-permute-start(bf16[3136,128]{1,0:T(8,128)(2,1)S(1)} %get-tuple-element.757), channel_id=1, source_target_pairs={{0,4},{2,6},{4,0},{6,2},{1,5},{3,7},{5,1},{7,3},{8,12},{10,14},{12... | collective-permute-start | bytes 2408456 | tf_op jit(solution)/shard_map/ppermute | solution.py:632
  959.9 46.2 %collective-permute-start.142 = (bf16[3136,128]{1,0:T(8,128)(2,1)S(1)}, bf16[3136,128]{1,0:T(8,128)(2,1)S(1)}, u32[]{:S(2)}, u32[]{:S(2)}) collective-permute-start(bf16[3136,128]{1,0:T(8,128)(2,1)S(1)} %get-tuple-element.756), channel_id=1, source_target_pairs={{0,6},{2,4},{4,2},{6,0},{1,7},{3,5},{5,3},{7,1},{8,14},{10,12},{12... | collective-permute-start | bytes 2408456 | tf_op jit(solution)/shard_map/ppermute | solution.py:632
  1074.5 53.5 %collective-permute-start.153 = (f32[256,2048]{1,0:T(8,128)S(1)}, f32[256,2048]{1,0:T(8,128)}, u32[]{:S(2)}, u32[]{:S(2)}) collective-permute-start(f32[256,2048]{1,0:T(8,128)S(1)} %fusion.36.own_ref), channel_id=1, source_target_pairs={{0,1},{1,0},{2,3},{3,2},{4,5},{5,4},{6,7},{7,6},{8,9},{9,8},{10,11... | collective-permute-start | bytes 6291464 | tf_op jit(solution)/shard_map/ppermute | solution.py:635
  1085.2 38.5 %collective-permute-start.161 = (bf16[2112,128]{1,0:T(8,128)(2,1)}, bf16[2112,128]{1,0:T(8,128)(2,1)}, u32[]{:S(2)}, u32[]{:S(2)}) collective-permute-start(bf16[2112,128]{1,0:T(8,128)(2,1)} %get-tuple-element.768), channel_id=1, source_target_pairs={{0,2},{2,0},{4,6},{6,4},{1,3},{3,1},{5,7},{7,5},{8,10},{10,8},{12,... | collective-permute-start | bytes 1622024 | tf_op jit(solution)/shard_map/ppermute | solution.py:632
  1085.7 38.0 %collective-permute-start.162 = (bf16[2112,128]{1,0:T(8,128)(2,1)}, bf16[2112,128]{1,0:T(8,128)(2,1)}, u32[]{:S(2)}, u32[]{:S(2)}) collective-permute-start(bf16[2112,128]{1,0:T(8,128)(2,1)} %get-tuple-element.767), channel_id=1, source_target_pairs={{0,4},{2,6},{4,0},{6,2},{1,5},{3,7},{5,1},{7,3},{8,12},{10,14},{12... | collective-permute-start | bytes 1622024 | tf_op jit(solution)/shard_map/ppermute | solution.py:632
  1086.8 36.9 %collective-permute-start.163 = (bf16[2112,128]{1,0:T(8,128)(2,1)}, bf16[2112,128]{1,0:T(8,128)(2,1)}, u32[]{:S(2)}, u32[]{:S(2)}) collective-permute-start(bf16[2112,128]{1,0:T(8,128)(2,1)} %get-tuple-element.766), channel_id=1, source_target_pairs={{0,6},{2,4},{4,2},{6,0},{1,7},{3,5},{5,3},{7,1},{8,14},{10,12},{12... | collective-permute-start | bytes 1622024 | tf_op jit(solution)/shard_map/ppermute | solution.py:632
  (353 other events, 4218.9 us)
Sparse Core Ops, SparseCore 0:
  27.4 79.1 all-gather.4
  108.8 152.0 all-gather.6
  262.5 79.2 all-gather.8
  343.8 152.0 all-gather.10
  626.9 149.0 reduce-scatter.4
  791.2 76.9 reduce-scatter.6
  895.7 148.4 reduce-scatter.8
  1046.6 85.5 reduce-scatter.10
